TPU v7x, 128 devices: a whole 4x4x4 slice. The times are simulated.
128 devices in a mesh: dp: 16 (over y, z_hi, core), mp: 8 (over z_lo, x).
Axes of the slice: x: 4, y: 4, z: 4 (z_hi: 2, z_lo: 2; z = z_hi * 2 + z_lo), core: 2. Of those that a mesh axis runs over, the one named last changes fastest.
Arguments:
- patches: bfloat16 [2048, 6144], P('dp'), may hold values from -6 to 6
- patch_pos: int32 [2048], P('dp'), may hold values from 0 to 1023
- tile_counts: int32 [8], P('mp'), may hold values from 1 to 4, as said below
- pos_table: bfloat16 [1024, 6144], replicated, may hold values from -3 to 3
- w_qkv: bfloat16 [6144, 3, 4096], P('mp', None, 'dp'), may hold values from -0.078125 to 0.078125
- qk_gain: float32 [2, 128], replicated, may hold values from 0.5 to 9
- w_attn_out: bfloat16 [4096, 6144], P('dp', 'mp'), may hold values from -0.09375 to 0.09375
- w_mlp_in: bfloat16 [6144, 12288], P('mp', 'dp'), may hold values from -0.078125 to 0.078125
- mlp_bias: float32 [12288], P('dp'), may hold values from -3 to 3
- w_mlp_out: bfloat16 [12288, 6144], P('dp', 'mp'), may hold values from -0.0546875 to 0.0546875
- norm_gain: float32 [6144], replicated, may hold values from 0.25 to 1.75
Outputs:
- encoded: bfloat16 [2048, 6144], P(('dp', 'mp'))
Inputs may be any that keep to these rules, and one draw needn't show every extreme that they name: `tile_counts`: every draw has an image with 4 tiles.
All inputs are finite; a program needn't handle non-finite values.
Results may differ from a plain program's by a relative error of at most 0.03.
Values may be sent and summed in bfloat16 or wider, within the bound.
No kernel may reach another device: no remote copies, remote signals or barrier semaphores. Data moves between devices by JAX's collectives and lax.ppermute only.
A program may use at most 128 MiB of HBM per device.

v0:
```python
import functools
import itertools

import jax
import jax.numpy as jnp
from jax import lax
from jax.experimental import pallas as pl
from jax.experimental.pallas import tpu as pltpu
from jax.sharding import Mesh, PartitionSpec as P

TILE = 64
HS = 128
AXES = ("y", "zh", "c", "zl", "x")
SIZES = {"y": 4, "zh": 2, "c": 2, "zl": 2, "x": 4}
bf16 = jnp.bfloat16
f32 = jnp.float32
norm_eps = 1e-06


def limit(mib):
    return pltpu.CompilerParams(vmem_limit_bytes=mib * 2**20)


CHEAP = pl.CostEstimate(flops=1000, bytes_accessed=1000, transcendentals=0)


def pairs(place):
    out = []
    for spot in itertools.product(*[range(SIZES[a]) for a in AXES]):
        here = dict(zip(AXES, spot))
        there = place(dict(here))
        ends = []
        for point in (here, there):
            index = 0
            for a in AXES:
                index = index * SIZES[a] + point[a] % SIZES[a]
            ends.append(index)
        out.append(tuple(ends))
    return out


def route(value, place):
    return lax.ppermute(value, AXES, pairs(place))


def send(value, **shift):
    def place(d):
        for a, by in shift.items():
            d[a] += by
        return d

    return route(value, place)


def cross(value, by=0):
    def place(d):
        d["zh"], d["zl"] = d["zl"], d["zh"]
        d["x"] += by
        return d

    return route(value, place)


def after(value, *others):
    return lax.optimization_barrier((value, *others))[0]


def dot(a, b):
    return jnp.dot(a, b, preferred_element_type=f32)


def whole(shape):
    return pl.BlockSpec(shape, lambda *_: (0,) * len(shape))


def shape_of(*shape, dtype=bf16):
    return jax.ShapeDtypeStruct(shape, dtype)


def lookup(chosen, refs):
    few = refs[0].shape[0]
    parts = [dot(chosen[:, i * few : (i + 1) * few], ref[...]) for i, ref in enumerate(refs)]
    return parts[0] + parts[1] + parts[2] + parts[3]


def choose(pos_ref, chosen):
    rows, slots = chosen.shape
    at = jnp.broadcast_to(pos_ref[...].astype(f32), (rows, rows)).T[:, 0:1]
    spots = lax.broadcasted_iota(jnp.int32, (rows, slots), 1)
    chosen[...] = (spots == at.astype(jnp.int32)).astype(f32).astype(bf16)


def measure_kernel(patches_ref, pos_ref, t0, t1, t2, t3, out_ref, chosen, means, devs):
    j, blocks = pl.program_id(0), pl.num_programs(0)
    rows, cols = patches_ref.shape

    @pl.when(j == 0)
    def _():
        choose(pos_ref, chosen)
        means[...] = jnp.zeros_like(means)
        devs[...] = jnp.zeros_like(devs)

    e = (patches_ref[...].astype(f32) + lookup(chosen, (t0, t1, t2, t3))).astype(bf16).astype(f32)
    mean = jnp.mean(e, axis=1, keepdims=True)
    dev = jnp.sum((e - mean) ** 2, axis=1, keepdims=True)
    lane = lax.broadcasted_iota(jnp.int32, (rows, 128), 1)
    means[...] = jnp.where(lane == j, mean, means[...])
    devs[...] = jnp.where(lane == j, dev, devs[...])

    @pl.when(j == blocks - 1)
    def _():
        count = blocks
        mu = jnp.sum(means[...], axis=1, keepdims=True) / count
        apart = jnp.where(lane < blocks, (means[...] - mu) ** 2, 0.0)
        total = jnp.sum(devs[...], axis=1, keepdims=True) + cols * jnp.sum(apart, axis=1, keepdims=True)
        scale = lax.rsqrt(total / (cols * count) + norm_eps)
        out_ref[...] = jnp.where(lane == 0, mu, scale).T[:8]


def measure(patches, pos, table, blocks):
    rows, cols, few = patches.shape[0], patches.shape[1] // blocks, table.shape[0] // 4
    return pl.pallas_call(
        measure_kernel,
        grid=(blocks,),
        in_specs=[pl.BlockSpec((rows, cols), lambda j: (0, j)), whole((1, rows))]
        + [pl.BlockSpec((few, cols), functools.partial(lambda i, j: (i, j), i)) for i in range(4)],
        out_specs=whole((8, rows)),
        out_shape=shape_of(8, rows, dtype=f32),
        scratch_shapes=[
            pltpu.VMEM((rows, table.shape[0]), bf16),
            pltpu.VMEM((rows, 128), f32),
            pltpu.VMEM((rows, 128), f32),
        ],
        compiler_params=limit(52),
        cost_estimate=CHEAP,
        name="measure",
    )(patches, pos, table, table, table, table)


def embed_kernel(info_ref, patches_ref, pos_ref, stat_ref, gain_ref, t0, t1, t2, t3, e_ref, normed_ref, chosen):
    @pl.when(pl.program_id(0) == 0)
    def _():
        choose(pos_ref, chosen)

    e = (patches_ref[0].astype(f32) + lookup(chosen, (t0, t1, t2, t3))).astype(bf16)
    e_ref[0] = e
    rows = e.shape[0]
    turned = jnp.concatenate([stat_ref[...]] * (rows // 8), axis=0).T
    normed_ref[0] = ((e.astype(f32) - turned[:, 0:1]) * turned[:, 1:2] * gain_ref[...]).astype(bf16)


def embed(info, patches, pos, stat, table, gain):
    _, rows, cols = patches.shape
    few = table.shape[0] // 4
    return pl.pallas_call(
        embed_kernel,
        grid_spec=pltpu.PrefetchScalarGridSpec(
            num_scalar_prefetch=1,
            grid=(2,),
            in_specs=[
                pl.BlockSpec((1, rows, cols), lambda s, info: (s, 0, 0)),
                pl.BlockSpec((1, rows), lambda s, info: (0, 0)),
                pl.BlockSpec((8, rows), lambda s, info: (0, 0)),
                pl.BlockSpec((1, cols), lambda s, info: (0, info[2 + s])),
            ]
            + [pl.BlockSpec((few, cols), functools.partial(lambda i, s, info: (i, info[2 + s]), i)) for i in range(4)],
            out_specs=[pl.BlockSpec((1, rows, cols), lambda s, info: (s, 0, 0))] * 2,
            scratch_shapes=[pltpu.VMEM((rows, table.shape[0]), bf16)],
        ),
        out_shape=[shape_of(2, rows, cols)] * 2,
        compiler_params=limit(52),
        cost_estimate=CHEAP,
        name="embed",
    )(info, patches, pos, stat, gain, table, table, table, table)


def project_kernel(info_ref, x0, x1, x2, x3, w00, w01, w10, w11, o0, o1, o2, o3, held):
    rows = x0.shape[1]
    zl, x = info_ref[1], info_ref[2]

    @pl.when(pl.program_id(0) == 0)
    def _():
        for far, ref in enumerate((x0, x1, x2, x3)):
            k = lax.rem(8 - x - far, 4)
            for s in range(2):
                held[s, pl.ds(pl.multiple_of(k * rows, rows), rows)] = ref[lax.rem(zl + s, 2)]

    def weight(ref):
        w = ref[...]
        return w.reshape(w.shape[-2:])

    for core, (near, far) in enumerate(((w00, w01), (w10, w11))):
        got = dot(held[0], weight(near)) + dot(held[1], weight(far))
        n = got.shape[1]
        for k, ref in enumerate((o0, o1, o2, o3)):
            ref[:, core * n : (core + 1) * n] = got[k * rows : (k + 1) * rows].astype(ref.dtype)


def project(info, xs, ws):
    _, rows, depth = xs[0].shape
    if ws[0].ndim == 3:
        spec = pl.BlockSpec((1, depth, ws[0].shape[2]), lambda i: (i, 0, 0))
        steps, n = ws[0].shape[0], 2 * ws[0].shape[2]
    else:
        n = 512
        spec = pl.BlockSpec((depth, n // 2), lambda i: (0, i))
        steps = 2 * ws[0].shape[1] // n
    return pl.pallas_call(
        project_kernel,
        grid=(steps,),
        in_specs=[pl.BlockSpec(memory_space=pltpu.SMEM)] + [whole((2, rows, depth))] * 4 + [spec] * 4,
        out_specs=[pl.BlockSpec((rows, n), lambda i: (0, i))] * 4,
        out_shape=[shape_of(rows, steps * n, dtype=f32 if k == 0 else bf16) for k in range(4)],
        scratch_shapes=[pltpu.VMEM((2, 4 * rows, depth), bf16)],
        compiler_params=limit(20),
        cost_estimate=CHEAP,
        name="project",
    )(info, *xs, *ws)


def heads_kernel(p0, p1, p2, p3, gain_ref, q_ref, kv_ref):
    part = pl.program_id(0)
    gain = gain_ref[pl.ds(jnp.minimum(part, 1), 1)]
    for h in range(q_ref.shape[1] // HS):
        at = slice(h * HS, (h + 1) * HS)
        v = p0[:, at] + p1[:, at].astype(f32) + p2[:, at].astype(f32) + p3[:, at].astype(f32)
        centered = v - jnp.mean(v, axis=1, keepdims=True)
        spread = lax.rsqrt(jnp.mean(centered * centered, axis=1, keepdims=True) + norm_eps)
        normed = (centered * spread * gain).astype(bf16)

        @pl.when(part == 0)
        def _():
            q_ref[:, at] = normed

        @pl.when(part > 0)
        def _():
            kv_ref[0, :, at] = jnp.where(part == 1, normed.astype(f32), v).astype(bf16)


def head_values(parts, gain):
    rows, n = parts[0].shape[0], parts[0].shape[1] // 3
    return pl.pallas_call(
        heads_kernel,
        grid=(3,),
        in_specs=[pl.BlockSpec((rows, n), lambda i: (0, i))] * 4 + [whole(gain.shape)],
        out_specs=[whole((rows, n)), pl.BlockSpec((1, rows, n), lambda i: (jnp.maximum(i - 1, 0), 0, 0))],
        out_shape=[shape_of(rows, n), shape_of(2, rows, n)],
        compiler_params=limit(8),
        cost_estimate=CHEAP,
        name="heads",
    )(*parts, gain)


def hidden_kernel(att_ref, p0, p1, p2, p3, b0, b1, out_ref):
    step = pl.program_id(0)

    @pl.when(step == 0)
    def _():
        out_ref[...] = att_ref[...]

    @pl.when(step > 0)
    def _():
        bias = jnp.concatenate([b0[...], b1[...]], axis=1)
        v = p0[...] + p1[...].astype(f32) + p2[...].astype(f32) + p3[...].astype(f32) + bias
        out_ref[...] = (v * 0.5 * (1.0 + lax.erf(v * 0.5**0.5))).astype(bf16)


def hidden_units(attended, parts, bias, bias_far):
    rows, n = attended.shape
    steps = parts[0].shape[1] // n

    def block(i):
        return 0, jnp.maximum(i - 1, 0)

    return pl.pallas_call(
        hidden_kernel,
        grid=(1 + steps,),
        in_specs=[whole((rows, n))] + [pl.BlockSpec((rows, n), block)] * 4 + [pl.BlockSpec((1, n // 2), block)] * 2,
        out_specs=pl.BlockSpec((rows, n), lambda i: (0, i)),
        out_shape=shape_of(rows, (1 + steps) * n),
        compiler_params=limit(8),
        cost_estimate=CHEAP,
        name="hidden",
    )(attended, *parts, bias, bias_far)


def attend_kernel(info_ref, count_ref, q_ref, near_ref, far_ref, out_ref):
    core, live = info_ref[4], count_ref[0] * TILE
    rows, n = q_ref.shape
    slot = lax.broadcasted_iota(jnp.int32, (rows, rows), 1)
    heads = n // HS
    for h in range(heads):
        at = slice(h * HS, (h + 1) * HS)
        o = (h + heads // 2) % heads
        other = slice(o * HS, (o + 1) * HS)
        q = q_ref[:, at]
        score = []
        for k, first in ((near_ref[0, :, at], core * rows), (far_ref[0, :, other], (1 - core) * rows)):
            s = lax.dot_general(q, k, (((1,), (1,)), ((), ())), preferred_element_type=f32) * HS ** (-0.5)
            score.append(jnp.where(slot + first < live, s, -1e30))
        top = jnp.maximum(jnp.max(score[0], axis=1, keepdims=True), jnp.max(score[1], axis=1, keepdims=True))
        lifted = [jnp.exp(s - top) for s in score]
        total = jnp.sum(lifted[0], axis=1, keepdims=True) + jnp.sum(lifted[1], axis=1, keepdims=True)
        probs = [(v / total).astype(bf16) for v in lifted]
        out_ref[:, at] = (dot(probs[0], near_ref[1, :, at]) + dot(probs[1], far_ref[1, :, other])).astype(bf16)


def attend(info, count, q, near, far):
    return pl.pallas_call(
        attend_kernel,
        in_specs=[pl.BlockSpec(memory_space=pltpu.SMEM)] * 2 + [pl.BlockSpec(memory_space=pltpu.VMEM)] * 3,
        out_shape=shape_of(*q.shape),
        compiler_params=limit(6),
        cost_estimate=CHEAP,
        name="attend",
    )(info, count, q, near, far)


def output_kernel(info_ref, e_ref, *refs):
    u_refs, weights, outs = refs[0:4], refs[4:8], refs[8:16]
    held, total = refs[16], refs[17]
    step = pl.program_id(0)
    rows, a_cols = u_refs[0].shape[0], u_refs[0].shape[1] // 4
    half, n = rows // 2, total.shape[1]
    zh, zl, x = info_ref[0], info_ref[1], info_ref[2]

    @pl.when(step == 0)
    def _():
        for k in range(4):
            held[k * rows : (k + 1) * rows] = u_refs[k][...]

    def multiply(ws, side):
        depth = a_cols // 2
        few = (ws[0].shape[0] - depth) // 3
        acc = None
        for core in range(2):
            t = dot(held[:, core * depth : (core + 1) * depth], ws[core][:depth])
            acc = t if acc is None else acc + t
        for i in range(3):
            for core in range(2):
                at = a_cols + (2 * i + core) * few
                acc = acc + dot(held[:, at : at + few], ws[core][depth + i * few : depth + (i + 1) * few])
        total[...] = acc

        @pl.when(zh == zl)
        def _():
            own = pl.ds(pl.multiple_of(x * rows, rows), rows)
            cut = pl.ds(pl.multiple_of((step - 3 * side) * n, n), n)
            total[own] += e_ref[lax.rem(zl + side, 2), :, cut].astype(f32)

    @pl.when(step < 3)
    def _():
        multiply(weights[:2], 0)

    @pl.when(step >= 3)
    def _():
        multiply(weights[2:], 1)

    for j in range(4):
        for h in range(2):
            k = lax.rem(x + 4 - j, 4)
            at = pl.multiple_of(k * rows + lax.rem(zh + h, 2) * half, half)
            outs[2 * j + h][...] = total[pl.ds(at, half)].astype(bf16)


def output(info, e, units, ws):
    rows, half = units[0].shape[0], units[0].shape[0] // 2
    depth, width = ws[0][0].shape
    n = width // 3
    near = pl.BlockSpec((depth, n), lambda j: (0, jnp.minimum(j, 2)))
    far = pl.BlockSpec((depth, n), lambda j: (0, jnp.maximum(j - 3, 0)))
    return pl.pallas_call(
        output_kernel,
        grid=(6,),
        in_specs=[pl.BlockSpec(memory_space=pltpu.SMEM)]
        + [whole(v.shape) for v in [e] + units]
        + [near, near, far, far],
        out_specs=[pl.BlockSpec((half, n), lambda j: (0, j))] * 8,
        out_shape=[shape_of(half, 2 * width)] * 8,
        scratch_shapes=[
            pltpu.VMEM((4 * rows, units[0].shape[1]), bf16),
            pltpu.VMEM((4 * rows, n), f32),
        ],
        compiler_params=limit(24),
        cost_estimate=CHEAP,
        name="output",
    )(info, e, *units, *ws[0], *ws[1])


def finish_kernel(info_ref, *refs):
    parts, outs, held = refs[:8], refs[8:12], refs[12]
    total = parts[0][...].astype(f32)
    for ref in parts[1:]:
        total = total + ref[...].astype(f32)
    held[...] = total.astype(bf16)
    few = held.shape[0] // 4
    for k in range(4):
        outs[k][...] = held[pl.ds(pl.multiple_of(lax.rem(info_ref[2] + k, 4) * few, few), few)]


def finish(info, parts):
    half, cols = parts[0].shape
    return pl.pallas_call(
        finish_kernel,
        in_specs=[pl.BlockSpec(memory_space=pltpu.SMEM)] + [pl.BlockSpec(memory_space=pltpu.VMEM)] * 8,
        out_shape=[shape_of(half // 4, cols)] * 4,
        scratch_shapes=[pltpu.VMEM((half, cols), bf16)],
        compiler_params=limit(8),
        cost_estimate=CHEAP,
        name="finish",
    )(info, *parts)


def assemble_kernel(info_ref, *refs):
    out_ref = refs[4]
    zh, x = info_ref[0], info_ref[2]
    cols = refs[0].shape[1] // 2
    for i, k in enumerate((2, 1, 3, 0)):
        from_x = lax.rem(x + 4 - k, 4)
        for side in range(2):
            block = jnp.where(zh == side, 0, 4) + from_x
            out_ref[:, pl.ds(pl.multiple_of(block * cols, cols), cols)] = refs[i][:, side * cols : (side + 1) * cols]


def assemble(info, pieces):
    few, cols = pieces[0].shape
    return pl.pallas_call(
        assemble_kernel,
        in_specs=[pl.BlockSpec(memory_space=pltpu.SMEM)] + [pl.BlockSpec(memory_space=pltpu.VMEM)] * 4,
        out_shape=shape_of(few, 4 * cols),
        compiler_params=limit(4),
        cost_estimate=CHEAP,
        name="assemble",
    )(info, *pieces)


def shards(
    patches,
    patch_pos,
    tile_counts,
    pos_table,
    w_qkv,
    qk_gain,
    w_attn_out,
    w_mlp_in,
    mlp_bias,
    w_mlp_out,
    norm_gain,
):
    y, zh, c, zl, x = [lax.axis_index(a) for a in AXES]
    info = jnp.stack([zh, zl, x, x + 4, c])

    def count_to(d):
        image = d["zl"] * 4 + d["x"]
        if image % 2 != d["zl"]:
            d["zh"] += 1
        d["zl"], d["x"] = image % 2, image // 2 - d["y"] + 4
        return d

    wq = jnp.transpose(w_qkv, (1, 0, 2))
    wq_z = send(wq, zl=1)
    wq_c = send(wq, c=1)
    wm_c = send(w_mlp_in, c=1)

    cols = w_mlp_in.shape[0]
    pos = patch_pos[None]
    mine = jnp.stack([lax.dynamic_slice_in_dim(patches, (x + 4 * i) * cols, cols, 1) for i in range(2)])
    mine = cross(mine)
    pos_far = cross(pos)
    stat = measure(patches, pos, pos_table, 8)
    stat = after(stat, wq_c, wm_c)
    counts = route(after(tile_counts, stat), count_to)
    bias = mlp_bias[None]
    bias_far = send(after(bias, stat), c=1)
    e, normed = embed(info, mine, pos_far, cross(stat), pos_table, norm_gain[None])
    xs = {0: normed}
    for k in (2, 1, 3):
        xs[k] = send(normed, y=k)
    xs = [xs[k] for k in range(4)]

    wm_z = send(after(w_mlp_in, wq_z, normed, counts, bias_far), zl=1)
    wq_cz = send(after(wq_z, normed, counts, bias_far), c=1)
    wo = jnp.concatenate([after(w_attn_out, normed), w_mlp_out])

    def exchange(p):
        got = {k: send(p[k] if isinstance(p, (list, tuple)) else p, x=k) for k in (2, 1, 3)}
        return [p[0] if isinstance(p, (list, tuple)) else p] + [got[k] for k in (1, 2, 3)]

    first = project(info, xs, [wq, wq_z, wq_c, wq_cz])
    qkv = exchange(first)
    second = project(info, xs, [w_mlp_in, wm_z, wm_c, send(after(wm_z, first[0]), c=1)])
    pre = exchange(second)
    wo_z = send(after(wo, wm_z, first[0]), zl=1)
    q, kv = head_values([after(qkv[0], second[0])] + qkv[1:], qk_gain)
    kv_far = send(kv, c=1)
    attended = attend(info, counts, q, kv, kv_far)
    units = hidden_units(attended, pre, bias, bias_far)
    wo_c = send(after(wo, units), c=1)
    wo_cz = send(after(wo_z, units), c=1)
    units = exchange(units)

    parts = output(info, e, units, [[wo, wo_c], [wo_z, wo_cz]])
    moves = [(2, 1), (2, 0), (1, 1), (3, 1), (0, 1), (1, 0), (3, 0)]
    moved = {(j, h): send(parts[2 * j + h], y=j, zh=h) for j, h in moves}
    pieces = finish(info, [parts[0]] + [moved[m] for m in moves])
    return assemble(info, [cross(pieces[k], k) for k in (2, 1, 3, 0)])


def solution(mesh):
    fine = Mesh(mesh.devices.reshape([SIZES[a] for a in AXES]), AXES)
    dp, mp = ("y", "zh", "c"), ("zl", "x")
    placed = (
        P(dp, None),
        P(dp),
        P(mp),
        P(),
        P(mp, None, dp),
        P(),
        P(dp, mp),
        P(mp, dp),
        P(dp),
        P(dp, mp),
        P(),
    )
    return jax.shard_map(shards, mesh=fine, in_specs=placed, out_specs=P(dp + mp, None), check_vma=False)
```

profile of v0, /device:TPU:32, one launch (start us, length us, event | category | flops | bytes accessed | tf_op | source)
XLA Modules:
  0.0 177.4 jit_solution(11581254336573516323)
XLA Ops:
  2.4 5.4 %collective-permute-start = (bf16[2,128,768]{2,1,0:T(8,128)(2,1)}, bf16[2,128,768]{2,1,0:T(8,128)(2,1)S(1)}, u32[]{:S(2)}, u32[]{:S(2)}) collective-permute-start(bf16[2,128,768]{2,1,0:T(8,128)(2,1)} %pad_maximum_fusion), channel_id=1, source_target_pairs={{0,0},{1,1},{2,2},{3,3},{4,16},{5,17},{6,18},{7,19},{8,8},{9,9},{1... | collective-permute-start | bytes 1179656 | tf_op jit(solution)/shard_map/ppermute | solution.py:43
  7.8 9.1 %measure.1 = f32[8,128]{1,0:T(8,128)S(1)} custom-call(bf16[128,6144]{1,0:T(8,128)(2,1)S(1)} %copy-done, s32[1,128]{1,0:T(1,128)S(1)} %bitcast.16, bf16[1024,6144]{1,0:T(8,128)(2,1)} %t3.3, bf16[1024,6144]{1,0:T(8,128)(2,1)} %t3.3, bf16[1024,6144]{1,0:T(8,128)(2,1)} %t3.3, bf16[1024,6144]{1,0:T(8,128)(2,1)} %t3.3), custom_call_target="tpu_custom_call" | custom-call | flops 1000 | bytes 1000 | tf_op jit(solution)/shard_map/measure/pallas_call | solution.py:122
  19.0 3.9 %collective-permute-start.1 = (s32[1,128]{1,0:T(1,128)S(1)}, s32[1,128]{1,0:T(1,128)S(1)}, u32[]{:S(2)}, u32[]{:S(2)}) collective-permute-start(s32[1,128]{1,0:T(1,128)S(1)} %bitcast.17), channel_id=1, source_target_pairs={{0,0},{1,1},{2,2},{3,3},{4,16},{5,17},{6,18},{7,19},{8,8},{9,9},{1... | collective-permute-start | bytes 1544 | tf_op jit(solution)/shard_map/ppermute | solution.py:43
  24.4 6.4 %collective-permute-start.5 = (s32[1]{0:T(128)}, s32[1]{0:T(128)}, u32[]{:S(2)}, u32[]{:S(2)}) collective-permute-start(s32[1]{0:T(128)} %param.13), channel_id=1, source_target_pairs={{0,0},{1,20},{2,1},{3,21},{4,18},{5,6},{6,19},{7,7},{8,8},{9,28},{... | collective-permute-start | bytes 20 | tf_op jit(solution)/shard_map/ppermute | solution.py:43
  30.9 3.3 %embed.1 = (bf16[2,128,768]{2,1,0:T(8,128)(2,1)S(1)}, bf16[2,128,768]{2,1,0:T(8,128)(2,1)S(1)}) custom-call(s32[5]{0:T(128)S(1)} %stack.32.info_ref, bf16[2,128,768]{2,1,0:T(8,128)(2,1)S(1)} %collective-permute-done.patches_ref, s32[1,128]{1,0:T(1,128)S(1)} %collective-permute-done.1.pos_ref, f32[8,128]{1,0:T(8,128)S(1)} %collective-permute-done.4.stat_ref, ...), custom_call_target="tpu_custom_call" | custom-call | flops 1000 | bytes 1000 | tf_op jit(solution)/shard_map/embed/pallas_call | solution.py:155
  34.4 2.8 %collective-permute-start.8 = (bf16[2,128,768]{2,1,0:T(8,128)(2,1)S(1)}, bf16[2,128,768]{2,1,0:T(8,128)(2,1)S(1)}, u32[]{:S(2)}, u32[]{:S(2)}) collective-permute-start(bf16[2,128,768]{2,1,0:T(8,128)(2,1)S(1)} %get-tuple-element.43.x0), channel_id=1, source_target_pairs={{0,96},{1,97},{2,98},{3,99},{4,100},{5,101},{6,102},{7,103},{8,104... | collective-permute-start | bytes 1179656 | tf_op jit(solution)/shard_map/ppermute | solution.py:43
  38.2 16.3 %collective-permute-done.8.x3 = bf16[2,128,768]{2,1,0:T(8,128)(2,1)S(1)} collective-permute-done((bf16[2,128,768]{2,1,0:T(8,128)(2,1)S(1)}, bf16[2,128,768]{2,1,0:T(8,128)(2,1)S(1)}, u32[]{:S(2)}, u32[]{:S(2)}) %collective-permute-start.8) | collective-permute-done | bytes 393248 | tf_op jit(solution)/shard_map/ppermute | solution.py:43
  54.6 3.4 %collective-permute-done.6.x1 = bf16[2,128,768]{2,1,0:T(8,128)(2,1)S(1)} collective-permute-done((bf16[2,128,768]{2,1,0:T(8,128)(2,1)S(1)}, bf16[2,128,768]{2,1,0:T(8,128)(2,1)S(1)}, u32[]{:S(2)}, u32[]{:S(2)}) %collective-permute-start.6) | collective-permute-done | bytes 393248 | tf_op jit(solution)/shard_map/ppermute | solution.py:43
  58.0 4.5 %project.2 = (f32[128,1536]{1,0:T(8,128)S(1)}, bf16[128,1536]{1,0:T(8,128)(2,1)S(1)}, bf16[128,1536]{1,0:T(8,128)(2,1)S(1)}, bf16[128,1536]{1,0:T(8,128)(2,1)S(1)}) custom-call(s32[5]{0:T(128)S(1)} %stack.32.info_ref, bf16[2,128,768]{2,1,0:T(8,128)(2,1)S(1)} %get-tuple-element.43.x0, bf16[2,128,768]{2,1,0:T(8,128)(2,1)S(1)} %collective-permute-done.6.x1, ...), custom_call_target="tpu_custom_call" | custom-call | flops 1000 | bytes 1000 | tf_op jit(solution)/shard_map/project/pallas_call | solution.py:208
  68.2 4.1 %project.3 = (f32[128,1536]{1,0:T(8,128)S(1)}, bf16[128,1536]{1,0:T(8,128)(2,1)S(1)}, bf16[128,1536]{1,0:T(8,128)(2,1)S(1)}, bf16[128,1536]{1,0:T(8,128)(2,1)S(1)}) custom-call(s32[5]{0:T(128)S(1)} %stack.32.info_ref, bf16[2,128,768]{2,1,0:T(8,128)(2,1)S(1)} %get-tuple-element.43.x0, bf16[2,128,768]{2,1,0:T(8,128)(2,1)S(1)} %collective-permute-done.6.x1, ...), custom_call_target="tpu_custom_call" | custom-call | flops 1000 | bytes 1000 | tf_op jit(solution)/shard_map/project/pallas_call | solution.py:208
  72.7 13.3 %collective-permute-done.14.p1 = bf16[128,1536]{1,0:T(8,128)(2,1)S(1)} collective-permute-done((bf16[128,1536]{1,0:T(8,128)(2,1)S(1)}, bf16[128,1536]{1,0:T(8,128)(2,1)S(1)}, u32[]{:S(2)}, u32[]{:S(2)}) %collective-permute-start.14) | collective-permute-done | bytes 393248 | tf_op jit(solution)/shard_map/ppermute | solution.py:43
  87.0 2.5 %heads.1 = (bf16[128,512]{1,0:T(8,128)(2,1)S(1)}, bf16[2,128,512]{2,1,0:T(8,128)(2,1)S(1)}) custom-call(f32[128,1536]{1,0:T(8,128)S(1)} %get-tuple-element.50.p0, bf16[128,1536]{1,0:T(8,128)(2,1)S(1)} %collective-permute-done.14.p1, bf16[128,1536]{1,0:T(8,128)(2,1)S(1)} %collective-permute-done.15.p2, bf16[128,1536]{1,0:T(8,128)(2,1)S(1)} %collective-permute-done.16.p3, ...), custom_call_target="tpu_custom_call" | custom-call | flops 1000 | bytes 1000 | tf_op jit(solution)/shard_map/heads/pallas_call | solution.py:242
  91.1 2.7 %attend.1.att_ref = bf16[128,512]{1,0:T(8,128)(2,1)S(1)} custom-call(s32[5]{0:T(128)S(1)} %stack.32.info_ref, s32[1]{0:T(128)} %collective-permute-done.5.count_ref, bf16[128,512]{1,0:T(8,128)(2,1)S(1)} %get-tuple-element.54.q_ref, bf16[2,128,512]{2,1,0:T(8,128)(2,1)S(1)} %get-tuple-element.55.near_ref, bf16[2,128,512]{2,1,0:T(8,128)(2,1)S(1)} %collective-permute-done.17.far_ref), custom_call_target="tpu_custom_call" | custom-call | flops 1000 | bytes 1000 | tf_op jit(solution)/shard_map/attend/pallas_call | solution.py:309
  93.7 8.4 %collective-permute-done.18.p1 = bf16[128,1536]{1,0:T(8,128)(2,1)S(1)} collective-permute-done((bf16[128,1536]{1,0:T(8,128)(2,1)S(1)}, bf16[128,1536]{1,0:T(8,128)(2,1)S(1)}, u32[]{:S(2)}, u32[]{:S(2)}) %collective-permute-start.18) | collective-permute-done | bytes 393248 | tf_op jit(solution)/shard_map/ppermute | solution.py:43
  107.5 21.9 %collective-permute-done.23.refs_3_ = bf16[128,2048]{1,0:T(8,128)(2,1)S(1)} collective-permute-done((bf16[128,2048]{1,0:T(8,128)(2,1)S(1)}, bf16[128,2048]{1,0:T(8,128)(2,1)S(1)}, u32[]{:S(2)}, u32[]{:S(2)}) %collective-permute-start.23) | collective-permute-done | bytes 524320 | tf_op jit(solution)/shard_map/ppermute | solution.py:43
  129.3 3.4 %collective-permute-done.21.refs_1_ = bf16[128,2048]{1,0:T(8,128)(2,1)S(1)} collective-permute-done((bf16[128,2048]{1,0:T(8,128)(2,1)S(1)}, bf16[128,2048]{1,0:T(8,128)(2,1)S(1)}, u32[]{:S(2)}, u32[]{:S(2)}) %collective-permute-start.21) | collective-permute-done | bytes 524320 | tf_op jit(solution)/shard_map/ppermute | solution.py:43
  132.7 6.1 %output.1 = (bf16[64,1536]{1,0:T(8,128)(2,1)S(1)}, bf16[64,1536]{1,0:T(8,128)(2,1)S(1)}, bf16[64,1536]{1,0:T(8,128)(2,1)S(1)}, bf16[64,1536]{1,0:T(8,128)(2,1)S(...) custom-call(s32[5]{0:T(128)S(1)} %stack.32.info_ref, ...), custom_call_target="tpu_custom_call" | custom-call | flops 1000 | bytes 1000 | tf_op jit(solution)/shard_map/output/pallas_call | solution.py:372
  138.8 3.7 %collective-permute-start.27 = (bf16[64,1536]{1,0:T(8,128)(2,1)S(1)}, bf16[64,1536]{1,0:T(8,128)(2,1)S(1)}, u32[]{:S(2)}, u32[]{:S(2)}) collective-permute-start(bf16[64,1536]{1,0:T(8,128)(2,1)S(1)} %get-tuple-element.64), channel_id=1, source_target_pairs={{0,80},{1,81},{2,82},{3,83},{4,84},{5,85},{6,86},{7,87},{8,88},{9,... | collective-permute-start | bytes 589832 | tf_op jit(solution)/shard_map/ppermute | solution.py:43
  144.4 4.2 %collective-permute-start.30 = (bf16[64,1536]{1,0:T(8,128)(2,1)S(1)}, bf16[64,1536]{1,0:T(8,128)(2,1)S(1)}, u32[]{:S(2)}, u32[]{:S(2)}) collective-permute-start(bf16[64,1536]{1,0:T(8,128)(2,1)S(1)} %get-tuple-element.67), channel_id=1, source_target_pairs={{0,112},{1,113},{2,114},{3,115},{4,116},{5,117},{6,118},{7,119},{8... | collective-permute-start | bytes 589832 | tf_op jit(solution)/shard_map/ppermute | solution.py:43
  155.2 5.0 %collective-permute-done.29.refs_3_ = bf16[64,1536]{1,0:T(8,128)(2,1)S(1)} collective-permute-done((bf16[64,1536]{1,0:T(8,128)(2,1)S(1)}, bf16[64,1536]{1,0:T(8,128)(2,1)S(1)}, u32[]{:S(2)}, u32[]{:S(2)}) %collective-permute-start.29) | collective-permute-done | bytes 196640 | tf_op jit(solution)/shard_map/ppermute | solution.py:43
  160.3 3.7 %collective-permute-done.31.refs_5_ = bf16[64,1536]{1,0:T(8,128)(2,1)S(1)} collective-permute-done((bf16[64,1536]{1,0:T(8,128)(2,1)S(1)}, bf16[64,1536]{1,0:T(8,128)(2,1)S(1)}, u32[]{:S(2)}, u32[]{:S(2)}) %collective-permute-start.31) | collective-permute-done | bytes 196640 | tf_op jit(solution)/shard_map/ppermute | solution.py:43
  166.4 3.8 %collective-permute-start.36 = (bf16[16,1536]{1,0:T(8,128)(2,1)S(1)}, bf16[16,1536]{1,0:T(8,128)(2,1)S(1)}, u32[]{:S(2)}, u32[]{:S(2)}) collective-permute-start(bf16[16,1536]{1,0:T(8,128)(2,1)S(1)} %get-tuple-element.73), channel_id=1, source_target_pairs={{0,3},{1,0},{2,1},{3,2},{4,19},{5,16},{6,17},{7,18},{8,11},{9,8},{... | collective-permute-start | bytes 147464 | tf_op jit(solution)/shard_map/ppermute | solution.py:43
  170.2 3.4 %collective-permute-start.37 = (bf16[16,1536]{1,0:T(8,128)(2,1)S(1)}, bf16[16,1536]{1,0:T(8,128)(2,1)S(1)}, u32[]{:S(2)}, u32[]{:S(2)}) collective-permute-start(bf16[16,1536]{1,0:T(8,128)(2,1)S(1)} %get-tuple-element.74), channel_id=1, source_target_pairs={{0,0},{1,1},{2,2},{3,3},{4,16},{5,17},{6,18},{7,19},{8,8},{9,9},{1... | collective-permute-start | bytes 147464 | tf_op jit(solution)/shard_map/ppermute | solution.py:43
  173.7 2.5 %collective-permute-done.37.refs_3_ = bf16[16,1536]{1,0:T(8,128)(2,1)S(1)} collective-permute-done((bf16[16,1536]{1,0:T(8,128)(2,1)S(1)}, bf16[16,1536]{1,0:T(8,128)(2,1)S(1)}, u32[]{:S(2)}, u32[]{:S(2)}) %collective-permute-start.37) | collective-permute-done | bytes 49184 | tf_op jit(solution)/shard_map/ppermute | solution.py:43
  (86 shorter events, 33.3 us)
Async XLA Ops:
  0.0 16.9 %collective-permute-start.2 = (bf16[3,768,256]{2,1,0:T(8,128)(2,1)}, bf16[3,768,256]{2,1,0:T(8,128)(2,1)}, u32[]{:S(2)}, u32[]{:S(2)}) collective-permute-start(bf16[3,768,256]{2,1,0:T(8,128)(2,1)} %bitcast.12), channel_id=1, source_target_pairs={{0,8},{1,9},{2,10},{3,11},{4,12},{5,13},{6,14},{7,15},{8,0},{9,1},... | collective-permute-start | bytes 3538952 | tf_op jit(solution)/shard_map/ppermute | solution.py:43
  0.0 16.9 %collective-permute-start.3 = (bf16[768,768]{1,0:T(8,128)(2,1)}, bf16[768,768]{1,0:T(8,128)(2,1)S(1)}, u32[]{:S(2)}, u32[]{:S(2)}) collective-permute-start(bf16[768,768]{1,0:T(8,128)(2,1)} %w00.1), channel_id=1, source_target_pairs={{0,8},{1,9},{2,10},{3,11},{4,12},{5,13},{6,14},{7,15},{8,0},{9,1},... | collective-permute-start | bytes 3538952 | tf_op jit(solution)/shard_map/ppermute | solution.py:43
  0.5 33.7 %collective-permute-start.9 = (bf16[3,768,256]{2,1,0:T(8,128)(2,1)}, bf16[3,768,256]{2,1,0:T(8,128)(2,1)}, u32[]{:S(2)}, u32[]{:S(2)}) collective-permute-start(bf16[3,768,256]{2,1,0:T(8,128)(2,1)} %bitcast.13), channel_id=1, source_target_pairs={{0,4},{1,5},{2,6},{3,7},{4,0},{5,1},{6,2},{7,3},{8,12},{9,13},{10,... | collective-permute-start | bytes 3538952 | tf_op jit(solution)/shard_map/ppermute | solution.py:43
  2.4 28.5 %collective-permute-start = (bf16[2,128,768]{2,1,0:T(8,128)(2,1)}, bf16[2,128,768]{2,1,0:T(8,128)(2,1)S(1)}, u32[]{:S(2)}, u32[]{:S(2)}) collective-permute-start(bf16[2,128,768]{2,1,0:T(8,128)(2,1)} %pad_maximum_fusion), channel_id=1, source_target_pairs={{0,0},{1,1},{2,2},{3,3},{4,16},{5,17},{6,18},{7,19},{8,8},{9,9},{1... | collective-permute-start | bytes 1179656 | tf_op jit(solution)/shard_map/ppermute | solution.py:43
  34.2 23.7 %collective-permute-start.11 = (bf16[3,768,256]{2,1,0:T(8,128)(2,1)}, bf16[3,768,256]{2,1,0:T(8,128)(2,1)S(1)}, u32[]{:S(2)}, u32[]{:S(2)}) collective-permute-start(bf16[3,768,256]{2,1,0:T(8,128)(2,1)} %collective-permute-done.9.w01), channel_id=1, source_target_pairs={{0,8},{1,9},{2,10},{3,11},{4,12},{5,13},{6,14},{7,15},{8,0},{9,1},... | collective-permute-start | bytes 3538952 | tf_op jit(solution)/shard_map/ppermute | solution.py:43
  34.3 28.4 %collective-permute-start.12 = (bf16[768,768]{1,0:T(8,128)(2,1)S(1)}, bf16[768,768]{1,0:T(8,128)(2,1)S(1)}, u32[]{:S(2)}, u32[]{:S(2)}) collective-permute-start(bf16[768,768]{1,0:T(8,128)(2,1)S(1)} %copy-done.2), channel_id=1, source_target_pairs={{0,4},{1,5},{2,6},{3,7},{4,0},{5,1},{6,2},{7,3},{8,12},{9,13},{10,... | collective-permute-start | bytes 3538952 | tf_op jit(solution)/shard_map/ppermute | solution.py:43
  34.4 20.1 %collective-permute-start.8 = (bf16[2,128,768]{2,1,0:T(8,128)(2,1)S(1)}, bf16[2,128,768]{2,1,0:T(8,128)(2,1)S(1)}, u32[]{:S(2)}, u32[]{:S(2)}) collective-permute-start(bf16[2,128,768]{2,1,0:T(8,128)(2,1)S(1)} %get-tuple-element.43.x0), channel_id=1, source_target_pairs={{0,96},{1,97},{2,98},{3,99},{4,100},{5,101},{6,102},{7,103},{8,104... | collective-permute-start | bytes 1179656 | tf_op jit(solution)/shard_map/ppermute | solution.py:43
  37.2 17.3 %collective-permute-start.7 = (bf16[2,128,768]{2,1,0:T(8,128)(2,1)S(1)}, bf16[2,128,768]{2,1,0:T(8,128)(2,1)S(1)}, u32[]{:S(2)}, u32[]{:S(2)}) collective-permute-start(bf16[2,128,768]{2,1,0:T(8,128)(2,1)S(1)} %get-tuple-element.43.x0), channel_id=1, source_target_pairs={{0,64},{1,65},{2,66},{3,67},{4,68},{5,69},{6,70},{7,71},{8,72},{9,... | collective-permute-start | bytes 1179656 | tf_op jit(solution)/shard_map/ppermute | solution.py:43
  37.2 20.7 %collective-permute-start.6 = (bf16[2,128,768]{2,1,0:T(8,128)(2,1)S(1)}, bf16[2,128,768]{2,1,0:T(8,128)(2,1)S(1)}, u32[]{:S(2)}, u32[]{:S(2)}) collective-permute-start(bf16[2,128,768]{2,1,0:T(8,128)(2,1)S(1)} %get-tuple-element.43.x0), channel_id=1, source_target_pairs={{0,32},{1,33},{2,34},{3,35},{4,36},{5,37},{6,38},{7,39},{8,40},{9,... | collective-permute-start | bytes 1179656 | tf_op jit(solution)/shard_map/ppermute | solution.py:43
  62.8 40.8 %collective-permute-start.25 = (bf16[1024,768]{1,0:T(8,128)(2,1)S(1)}, bf16[1024,768]{1,0:T(8,128)(2,1)S(1)}, u32[]{:S(2)}, u32[]{:S(2)}) collective-permute-start(bf16[1024,768]{1,0:T(8,128)(2,1)S(1)} %constant_dynamic-update-slice_fusion.refs_4_), channel_id=1, source_target_pairs={{0,4},{1,5},{2,6},{3,7},{4,0},{5,1},{6,2},{7,3},{8,12},{9,13},{10,... | collective-permute-start | bytes 4718600 | tf_op jit(solution)/shard_map/ppermute | solution.py:43
  64.5 21.6 %collective-permute-start.14 = (bf16[128,1536]{1,0:T(8,128)(2,1)S(1)}, bf16[128,1536]{1,0:T(8,128)(2,1)S(1)}, u32[]{:S(2)}, u32[]{:S(2)}) collective-permute-start(bf16[128,1536]{1,0:T(8,128)(2,1)S(1)} %get-tuple-element.51), channel_id=1, source_target_pairs={{0,1},{1,2},{2,3},{3,0},{4,5},{5,6},{6,7},{7,4},{8,9},{9,10},{10,1... | collective-permute-start | bytes 1179656 | tf_op jit(solution)/shard_map/ppermute | solution.py:43
  64.5 21.6 %collective-permute-start.15 = (bf16[128,1536]{1,0:T(8,128)(2,1)S(1)}, bf16[128,1536]{1,0:T(8,128)(2,1)S(1)}, u32[]{:S(2)}, u32[]{:S(2)}) collective-permute-start(bf16[128,1536]{1,0:T(8,128)(2,1)S(1)} %get-tuple-element.52), channel_id=1, source_target_pairs={{0,2},{1,3},{2,0},{3,1},{4,6},{5,7},{6,4},{7,5},{8,10},{9,11},{10,... | collective-permute-start | bytes 1179656 | tf_op jit(solution)/shard_map/ppermute | solution.py:43
  66.5 20.4 %collective-permute-start.16 = (bf16[128,1536]{1,0:T(8,128)(2,1)S(1)}, bf16[128,1536]{1,0:T(8,128)(2,1)S(1)}, u32[]{:S(2)}, u32[]{:S(2)}) collective-permute-start(bf16[128,1536]{1,0:T(8,128)(2,1)S(1)} %get-tuple-element.53), channel_id=1, source_target_pairs={{0,3},{1,0},{2,1},{3,2},{4,7},{5,4},{6,5},{7,6},{8,11},{9,8},{10,9... | collective-permute-start | bytes 1179656 | tf_op jit(solution)/shard_map/ppermute | solution.py:43
  72.2 30.0 %collective-permute-start.18 = (bf16[128,1536]{1,0:T(8,128)(2,1)S(1)}, bf16[128,1536]{1,0:T(8,128)(2,1)S(1)}, u32[]{:S(2)}, u32[]{:S(2)}) collective-permute-start(bf16[128,1536]{1,0:T(8,128)(2,1)S(1)} %get-tuple-element.56), channel_id=1, source_target_pairs={{0,1},{1,2},{2,3},{3,0},{4,5},{5,6},{6,7},{7,4},{8,9},{9,10},{10,1... | collective-permute-start | bytes 1179656 | tf_op jit(solution)/shard_map/ppermute | solution.py:43
  86.1 16.1 %collective-permute-start.19 = (bf16[128,1536]{1,0:T(8,128)(2,1)S(1)}, bf16[128,1536]{1,0:T(8,128)(2,1)S(1)}, u32[]{:S(2)}, u32[]{:S(2)}) collective-permute-start(bf16[128,1536]{1,0:T(8,128)(2,1)S(1)} %get-tuple-element.57), channel_id=1, source_target_pairs={{0,2},{1,3},{2,0},{3,1},{4,6},{5,7},{6,4},{7,5},{8,10},{9,11},{10,... | collective-permute-start | bytes 1179656 | tf_op jit(solution)/shard_map/ppermute | solution.py:43
  86.1 16.8 %collective-permute-start.20 = (bf16[128,1536]{1,0:T(8,128)(2,1)S(1)}, bf16[128,1536]{1,0:T(8,128)(2,1)S(1)}, u32[]{:S(2)}, u32[]{:S(2)}) collective-permute-start(bf16[128,1536]{1,0:T(8,128)(2,1)S(1)} %get-tuple-element.58), channel_id=1, source_target_pairs={{0,3},{1,0},{2,1},{3,2},{4,7},{5,4},{6,5},{7,6},{8,11},{9,8},{10,9... | collective-permute-start | bytes 1179656 | tf_op jit(solution)/shard_map/ppermute | solution.py:43
  103.5 29.2 %collective-permute-start.24 = (bf16[1024,768]{1,0:T(8,128)(2,1)S(1)}, bf16[1024,768]{1,0:T(8,128)(2,1)S(1)}, u32[]{:S(2)}, u32[]{:S(2)}) collective-permute-start(bf16[1024,768]{1,0:T(8,128)(2,1)S(1)} %constant_dynamic-update-slice_fusion.refs_4_), channel_id=1, source_target_pairs={{0,8},{1,9},{2,10},{3,11},{4,12},{5,13},{6,14},{7,15},{8,0},{9,1},... | collective-permute-start | bytes 4718600 | tf_op jit(solution)/shard_map/ppermute | solution.py:43
  103.6 29.1 %collective-permute-start.26 = (bf16[1024,768]{1,0:T(8,128)(2,1)S(1)}, bf16[1024,768]{1,0:T(8,128)(2,1)S(1)}, u32[]{:S(2)}, u32[]{:S(2)}) collective-permute-start(bf16[1024,768]{1,0:T(8,128)(2,1)S(1)} %collective-permute-done.25.refs_6_), channel_id=1, source_target_pairs={{0,8},{1,9},{2,10},{3,11},{4,12},{5,13},{6,14},{7,15},{8,0},{9,1},... | collective-permute-start | bytes 4718600 | tf_op jit(solution)/shard_map/ppermute | solution.py:43
  104.1 25.2 %collective-permute-start.23 = (bf16[128,2048]{1,0:T(8,128)(2,1)S(1)}, bf16[128,2048]{1,0:T(8,128)(2,1)S(1)}, u32[]{:S(2)}, u32[]{:S(2)}) collective-permute-start(bf16[128,2048]{1,0:T(8,128)(2,1)S(1)} %hidden.1.refs_0_), channel_id=1, source_target_pairs={{0,3},{1,0},{2,1},{3,2},{4,7},{5,4},{6,5},{7,6},{8,11},{9,8},{10,9... | collective-permute-start | bytes 1572872 | tf_op jit(solution)/shard_map/ppermute | solution.py:43
  106.6 22.7 %collective-permute-start.22 = (bf16[128,2048]{1,0:T(8,128)(2,1)S(1)}, bf16[128,2048]{1,0:T(8,128)(2,1)S(1)}, u32[]{:S(2)}, u32[]{:S(2)}) collective-permute-start(bf16[128,2048]{1,0:T(8,128)(2,1)S(1)} %hidden.1.refs_0_), channel_id=1, source_target_pairs={{0,2},{1,3},{2,0},{3,1},{4,6},{5,7},{6,4},{7,5},{8,10},{9,11},{10,... | collective-permute-start | bytes 1572872 | tf_op jit(solution)/shard_map/ppermute | solution.py:43
  106.6 26.1 %collective-permute-start.21 = (bf16[128,2048]{1,0:T(8,128)(2,1)S(1)}, bf16[128,2048]{1,0:T(8,128)(2,1)S(1)}, u32[]{:S(2)}, u32[]{:S(2)}) collective-permute-start(bf16[128,2048]{1,0:T(8,128)(2,1)S(1)} %hidden.1.refs_0_), channel_id=1, source_target_pairs={{0,1},{1,2},{2,3},{3,0},{4,5},{5,6},{6,7},{7,4},{8,9},{9,10},{10,1... | collective-permute-start | bytes 1572872 | tf_op jit(solution)/shard_map/ppermute | solution.py:43
  142.9 17.2 %collective-permute-start.29 = (bf16[64,1536]{1,0:T(8,128)(2,1)S(1)}, bf16[64,1536]{1,0:T(8,128)(2,1)S(1)}, u32[]{:S(2)}, u32[]{:S(2)}) collective-permute-start(bf16[64,1536]{1,0:T(8,128)(2,1)S(1)} %get-tuple-element.66), channel_id=1, source_target_pairs={{0,48},{1,49},{2,50},{3,51},{4,52},{5,53},{6,54},{7,55},{8,56},{9,... | collective-permute-start | bytes 589832 | tf_op jit(solution)/shard_map/ppermute | solution.py:43
  144.4 15.9 %collective-permute-start.30 = (bf16[64,1536]{1,0:T(8,128)(2,1)S(1)}, bf16[64,1536]{1,0:T(8,128)(2,1)S(1)}, u32[]{:S(2)}, u32[]{:S(2)}) collective-permute-start(bf16[64,1536]{1,0:T(8,128)(2,1)S(1)} %get-tuple-element.67), channel_id=1, source_target_pairs={{0,112},{1,113},{2,114},{3,115},{4,116},{5,117},{6,118},{7,119},{8... | collective-permute-start | bytes 589832 | tf_op jit(solution)/shard_map/ppermute | solution.py:43
  148.6 15.4 %collective-permute-start.31 = (bf16[64,1536]{1,0:T(8,128)(2,1)S(1)}, bf16[64,1536]{1,0:T(8,128)(2,1)S(1)}, u32[]{:S(2)}, u32[]{:S(2)}) collective-permute-start(bf16[64,1536]{1,0:T(8,128)(2,1)S(1)} %get-tuple-element.68), channel_id=1, source_target_pairs={{0,16},{1,17},{2,18},{3,19},{4,20},{5,21},{6,22},{7,23},{8,24},{9,... | collective-permute-start | bytes 589832 | tf_op jit(solution)/shard_map/ppermute | solution.py:43
  (23 other events, 260.0 us)
where the time goes:
time: 178 us; the launch traced here: 177 us
  waiting for transfers between devices  84.7 us (48%)
  starting transfers between devices  55.3 us (31%)
  Pallas kernels  35 us (20%)
    ppermute x38, waiting for transfers between devices, route(): return lax.ppermute(value, AXES, pairs(place))  84.7 us
    ppermute x38, starting transfers between devices, route(): return lax.ppermute(value, AXES, pairs(place))  55.3 us
    pallas_call x1, Pallas kernels, measure(): pl.pallas_call(measure_kernel, grid=(blocks,), in_specs=[pl.BlockSpec((ro...  9.11 us
    pallas_call x2, Pallas kernels, project(): pl.pallas_call(project_kernel, grid=(steps,), in_specs=[pl.BlockSpec(memo...  8.51 us
    pallas_call x1, Pallas kernels, output(): pl.pallas_call(output_kernel, grid=(6,), in_specs=[pl.BlockSpec(memory_sp...  6.12 us
  transfers between devices with their start and end apart: 38, of which 16 were waited for; matrix products, arithmetic and copies ran while one was open for 1% of the time, Pallas kernels for 15%

commit v1 on v0

--- a/solution.py
+++ b/solution.py
@@ -15,6 +15,7 @@
 bf16 = jnp.bfloat16
 f32 = jnp.float32
 norm_eps = 1e-06
+GROUPS = ((0, 1, 3), (2,))
 
 
 def limit(mib):
@@ -83,9 +84,9 @@
     return parts[0] + parts[1] + parts[2] + parts[3]
 
 
-def choose(pos_ref, chosen):
+def choose(pos, chosen):
     rows, slots = chosen.shape
-    at = jnp.broadcast_to(pos_ref[...].astype(f32), (rows, rows)).T[:, 0:1]
+    at = jnp.broadcast_to(pos.astype(f32), (rows, rows)).T[:, 0:1]
     spots = lax.broadcasted_iota(jnp.int32, (rows, slots), 1)
     chosen[...] = (spots == at.astype(jnp.int32)).astype(f32).astype(bf16)
 
@@ -96,7 +97,7 @@
 
     @pl.when(j == 0)
     def _():
-        choose(pos_ref, chosen)
+        choose(pos_ref[...], chosen)
         means[...] = jnp.zeros_like(means)
         devs[...] = jnp.zeros_like(devs)
 
@@ -114,7 +115,9 @@
         apart = jnp.where(lane < blocks, (means[...] - mu) ** 2, 0.0)
         total = jnp.sum(devs[...], axis=1, keepdims=True) + cols * jnp.sum(apart, axis=1, keepdims=True)
         scale = lax.rsqrt(total / (cols * count) + norm_eps)
-        out_ref[...] = jnp.where(lane == 0, mu, scale).T[:8]
+        where = jnp.broadcast_to(pos_ref[...], out_ref.shape).astype(f32)
+        row = lax.broadcasted_iota(jnp.int32, out_ref.shape, 0)
+        out_ref[...] = jnp.where(row == 2, where, jnp.where(lane == 0, mu, scale).T[:8])
 
 
 def measure(patches, pos, table, blocks):
@@ -137,10 +140,10 @@
     )(patches, pos, table, table, table, table)
 
 
-def embed_kernel(info_ref, patches_ref, pos_ref, stat_ref, gain_ref, t0, t1, t2, t3, e_ref, normed_ref, chosen):
+def embed_kernel(info_ref, patches_ref, stat_ref, gain_ref, t0, t1, t2, t3, e_ref, normed_ref, chosen):
     @pl.when(pl.program_id(0) == 0)
     def _():
-        choose(pos_ref, chosen)
+        choose(stat_ref[2:3], chosen)
 
     e = (patches_ref[0].astype(f32) + lookup(chosen, (t0, t1, t2, t3))).astype(bf16)
     e_ref[0] = e
@@ -149,7 +152,7 @@
     normed_ref[0] = ((e.astype(f32) - turned[:, 0:1]) * turned[:, 1:2] * gain_ref[...]).astype(bf16)
 
 
-def embed(info, patches, pos, stat, table, gain):
+def embed(info, patches, stat, table, gain):
     _, rows, cols = patches.shape
     few = table.shape[0] // 4
     return pl.pallas_call(
@@ -159,7 +162,6 @@
             grid=(2,),
             in_specs=[
                 pl.BlockSpec((1, rows, cols), lambda s, info: (s, 0, 0)),
-                pl.BlockSpec((1, rows), lambda s, info: (0, 0)),
                 pl.BlockSpec((8, rows), lambda s, info: (0, 0)),
                 pl.BlockSpec((1, cols), lambda s, info: (0, info[2 + s])),
             ]
@@ -171,7 +173,7 @@
         compiler_params=limit(52),
         cost_estimate=CHEAP,
         name="embed",
-    )(info, patches, pos, stat, gain, table, table, table, table)
+    )(info, patches, stat, gain, table, table, table, table)
 
 
 def project_kernel(info_ref, x0, x1, x2, x3, w00, w01, w10, w11, o0, o1, o2, o3, held):
@@ -316,9 +318,9 @@
     )(info, count, q, near, far)
 
 
-def output_kernel(info_ref, e_ref, *refs):
-    u_refs, weights, outs = refs[0:4], refs[4:8], refs[8:16]
-    held, total = refs[16], refs[17]
+def output_kernel(ks, info_ref, e_ref, *refs):
+    u_refs, weights, outs = refs[: len(ks)], refs[len(ks) : len(ks) + 4], refs[len(ks) + 4 : -2]
+    held, total = refs[-2:]
     step = pl.program_id(0)
     rows, a_cols = u_refs[0].shape[0], u_refs[0].shape[1] // 4
     half, n = rows // 2, total.shape[1]
@@ -326,8 +328,8 @@
 
     @pl.when(step == 0)
     def _():
-        for k in range(4):
-            held[k * rows : (k + 1) * rows] = u_refs[k][...]
+        for i, ref in enumerate(u_refs):
+            held[i * rows : (i + 1) * rows] = ref[...]
 
     def multiply(ws, side):
         depth = a_cols // 2
@@ -342,11 +344,12 @@
                 acc = acc + dot(held[:, at : at + few], ws[core][depth + i * few : depth + (i + 1) * few])
         total[...] = acc
 
-        @pl.when(zh == zl)
-        def _():
-            own = pl.ds(pl.multiple_of(x * rows, rows), rows)
-            cut = pl.ds(pl.multiple_of((step - 3 * side) * n, n), n)
-            total[own] += e_ref[lax.rem(zl + side, 2), :, cut].astype(f32)
+        for i, k in enumerate(ks):
+
+            @pl.when(jnp.logical_and(zh == zl, x == k))
+            def _():
+                cut = pl.ds(pl.multiple_of((step - 3 * side) * n, n), n)
+                total[i * rows : (i + 1) * rows] += e_ref[lax.rem(zl + side, 2), :, cut].astype(f32)
 
     @pl.when(step < 3)
     def _():
@@ -356,30 +359,29 @@
     def _():
         multiply(weights[2:], 1)
 
-    for j in range(4):
+    for i in range(len(ks)):
         for h in range(2):
-            k = lax.rem(x + 4 - j, 4)
-            at = pl.multiple_of(k * rows + lax.rem(zh + h, 2) * half, half)
-            outs[2 * j + h][...] = total[pl.ds(at, half)].astype(bf16)
-
-
-def output(info, e, units, ws):
+            at = pl.multiple_of(i * rows + lax.rem(zh + h, 2) * half, half)
+            outs[2 * i + h][...] = total[pl.ds(at, half)].astype(bf16)
+
+
+def output(info, e, ks, units, ws):
     rows, half = units[0].shape[0], units[0].shape[0] // 2
     depth, width = ws[0][0].shape
     n = width // 3
     near = pl.BlockSpec((depth, n), lambda j: (0, jnp.minimum(j, 2)))
     far = pl.BlockSpec((depth, n), lambda j: (0, jnp.maximum(j - 3, 0)))
     return pl.pallas_call(
-        output_kernel,
+        functools.partial(output_kernel, ks),
         grid=(6,),
         in_specs=[pl.BlockSpec(memory_space=pltpu.SMEM)]
         + [whole(v.shape) for v in [e] + units]
         + [near, near, far, far],
-        out_specs=[pl.BlockSpec((half, n), lambda j: (0, j))] * 8,
-        out_shape=[shape_of(half, 2 * width)] * 8,
+        out_specs=[pl.BlockSpec((half, n), lambda j: (0, j))] * (2 * len(ks)),
+        out_shape=[shape_of(half, 2 * width)] * (2 * len(ks)),
         scratch_shapes=[
-            pltpu.VMEM((4 * rows, units[0].shape[1]), bf16),
-            pltpu.VMEM((4 * rows, n), f32),
+            pltpu.VMEM((len(ks) * rows, units[0].shape[1]), bf16),
+            pltpu.VMEM((len(ks) * rows, n), f32),
         ],
         compiler_params=limit(24),
         cost_estimate=CHEAP,
@@ -465,21 +467,20 @@
     cols = w_mlp_in.shape[0]
     pos = patch_pos[None]
     mine = jnp.stack([lax.dynamic_slice_in_dim(patches, (x + 4 * i) * cols, cols, 1) for i in range(2)])
-    mine = cross(mine)
-    pos_far = cross(pos)
+    counts = route(tile_counts, count_to)
+    mine = cross(after(mine, counts))
     stat = measure(patches, pos, pos_table, 8)
     stat = after(stat, wq_c, wm_c)
-    counts = route(after(tile_counts, stat), count_to)
     bias = mlp_bias[None]
     bias_far = send(after(bias, stat), c=1)
-    e, normed = embed(info, mine, pos_far, cross(stat), pos_table, norm_gain[None])
+    e, normed = embed(info, mine, cross(stat), pos_table, norm_gain[None])
     xs = {0: normed}
     for k in (2, 1, 3):
         xs[k] = send(normed, y=k)
     xs = [xs[k] for k in range(4)]
 
-    wm_z = send(after(w_mlp_in, wq_z, normed, counts, bias_far), zl=1)
-    wq_cz = send(after(wq_z, normed, counts, bias_far), c=1)
+    wm_z = send(after(w_mlp_in, wq_z, normed, bias_far), zl=1)
+    wq_cz = send(after(wq_z, normed, bias_far), c=1)
     wo = jnp.concatenate([after(w_attn_out, normed), w_mlp_out])
 
     def exchange(p):
@@ -497,12 +498,22 @@
     units = hidden_units(attended, pre, bias, bias_far)
     wo_c = send(after(wo, units), c=1)
     wo_cz = send(after(wo_z, units), c=1)
-    units = exchange(units)
-
-    parts = output(info, e, units, [[wo, wo_c], [wo_z, wo_cz]])
-    moves = [(2, 1), (2, 0), (1, 1), (3, 1), (0, 1), (1, 0), (3, 0)]
-    moved = {(j, h): send(parts[2 * j + h], y=j, zh=h) for j, h in moves}
-    pieces = finish(info, [parts[0]] + [moved[m] for m in moves])
+
+    def to_owner(k, h):
+        def place(d):
+            d["y"] += d["x"] + 4 - k
+            d["zh"] += h
+            return d
+
+        return place
+
+    far = {0: units, 1: send(units, x=1), 3: send(units, x=3)}
+    far[2] = send(after(units, far[1], far[3]), x=2)
+    parts = []
+    for ks in GROUPS:
+        got = output(info, e, ks, [far[k] for k in ks], [[wo, wo_c], [wo_z, wo_cz]])
+        parts += [route(got[2 * i + h], to_owner(k, h)) for i, k in enumerate(ks) for h in (1, 0)]
+    pieces = finish(info, parts)
     return assemble(info, [cross(pieces[k], k) for k in (2, 1, 3, 0)])
 
 

time: 178 us -> 169 us (0.949)
  waiting for transfers between devices: 84.7 us -> 52 us
  starting transfers between devices: 55.3 us -> 75.8 us
  Pallas kernels: 35 us -> 37.5 us
    ppermute x38, waiting for transfers between devices: 84.7 us -> 52 us  [route(): return lax.ppermute(value, AXES, pairs(place))]
    ppermute x38, starting transfers between devices: 55.3 us -> 75.8 us  [route(): return lax.ppermute(value, AXES, pairs(place))]
    pallas_call x1 -> x2, Pallas kernels: 6.12 us -> 8.42 us  [output(): pl.pallas_call(functools.partial(output_kernel, ks), grid=(6,), in_specs=...]
  transfers between devices with their start and end apart: 38 -> 38, of which waited for: 16 -> 10; matrix products, arithmetic and copies ran while one was open for 1% -> 1% of each run, Pallas kernels for 15% -> 21%
where the time goes in v1:
time: 169 us; the launch traced here: 168 us
  starting transfers between devices  75.8 us (45%)
  waiting for transfers between devices  52 us (31%)
  Pallas kernels  37.5 us (22%)
    ppermute x38, starting transfers between devices, route(): return lax.ppermute(value, AXES, pairs(place))  75.8 us
    ppermute x38, waiting for transfers between devices, route(): return lax.ppermute(value, AXES, pairs(place))  52 us
    pallas_call x1, Pallas kernels, measure(): pl.pallas_call(measure_kernel, grid=(blocks,), in_specs=[pl.BlockSpec((ro...  9.11 us
    pallas_call x2, Pallas kernels, project(): pl.pallas_call(project_kernel, grid=(steps,), in_specs=[pl.BlockSpec(memo...  8.52 us
    pallas_call x2, Pallas kernels, output(): pl.pallas_call(functools.partial(output_kernel, ks), grid=(6,), in_specs=...  8.42 us
  transfers between devices with their start and end apart: 38, of which 10 were waited for; matrix products, arithmetic and copies ran while one was open for 1% of the time, Pallas kernels for 21%

profile of v1, /device:TPU:32, one launch (start us, length us, event | category | flops | bytes accessed | tf_op | source)
XLA Modules:
  0.0 167.8 jit_solution(7094148645181624321)
XLA Ops:
  0.5 7.9 %collective-permute-start = (s32[1]{0:T(128)}, s32[1]{0:T(128)}, u32[]{:S(2)}, u32[]{:S(2)}) collective-permute-start(s32[1]{0:T(128)} %param.13), channel_id=1, source_target_pairs={{0,0},{1,20},{2,1},{3,21},{4,18},{5,6},{6,19},{7,7},{8,8},{9,28},{... | collective-permute-start | bytes 20 | tf_op jit(solution)/shard_map/ppermute | solution.py:44
  12.2 9.1 %measure.1 = f32[8,128]{1,0:T(8,128)S(1)} custom-call(bf16[128,6144]{1,0:T(8,128)(2,1)S(1)} %copy-done, s32[1,128]{1,0:T(1,128)S(1)} %bitcast.16, bf16[1024,6144]{1,0:T(8,128)(2,1)} %t3.3, bf16[1024,6144]{1,0:T(8,128)(2,1)} %t3.3, bf16[1024,6144]{1,0:T(8,128)(2,1)} %t3.3, bf16[1024,6144]{1,0:T(8,128)(2,1)} %t3.3), custom_call_target="tpu_custom_call" | custom-call | flops 1000 | bytes 1000 | tf_op jit(solution)/shard_map/measure/pallas_call | solution.py:125
  21.4 3.9 %collective-permute-start.4 = (f32[8,128]{1,0:T(8,128)S(1)}, f32[8,128]{1,0:T(8,128)S(1)}, u32[]{:S(2)}, u32[]{:S(2)}) collective-permute-start(f32[8,128]{1,0:T(8,128)S(1)} %measure.1), channel_id=1, source_target_pairs={{0,0},{1,1},{2,2},{3,3},{4,16},{5,17},{6,18},{7,19},{8,8},{9,9},{1... | collective-permute-start | bytes 12296 | tf_op jit(solution)/shard_map/ppermute | solution.py:44
  26.9 3.3 %embed.1 = (bf16[2,128,768]{2,1,0:T(8,128)(2,1)S(1)}, bf16[2,128,768]{2,1,0:T(8,128)(2,1)S(1)}) custom-call(s32[5]{0:T(128)S(1)} %stack.32.info_ref, bf16[2,128,768]{2,1,0:T(8,128)(2,1)S(1)} %collective-permute-done.1.patches_ref, f32[8,128]{1,0:T(8,128)S(1)} %collective-permute-done.4.stat_ref, f32[1,6144]{1,0:T(1,128)S(1)} %bitcast.15, ...), custom_call_target="tpu_custom_call" | custom-call | flops 1000 | bytes 1000 | tf_op jit(solution)/shard_map/embed/pallas_call | solution.py:158
  32.9 3.8 %collective-permute-start.6 = (bf16[2,128,768]{2,1,0:T(8,128)(2,1)S(1)}, bf16[2,128,768]{2,1,0:T(8,128)(2,1)S(1)}, u32[]{:S(2)}, u32[]{:S(2)}) collective-permute-start(bf16[2,128,768]{2,1,0:T(8,128)(2,1)S(1)} %get-tuple-element.44.x0), channel_id=1, source_target_pairs={{0,64},{1,65},{2,66},{3,67},{4,68},{5,69},{6,70},{7,71},{8,72},{9,... | collective-permute-start | bytes 1179656 | tf_op jit(solution)/shard_map/ppermute | solution.py:44
  36.9 7.9 %collective-permute-done.5.x1 = bf16[2,128,768]{2,1,0:T(8,128)(2,1)S(1)} collective-permute-done((bf16[2,128,768]{2,1,0:T(8,128)(2,1)S(1)}, bf16[2,128,768]{2,1,0:T(8,128)(2,1)S(1)}, u32[]{:S(2)}, u32[]{:S(2)}) %collective-permute-start.5) | collective-permute-done | bytes 393248 | tf_op jit(solution)/shard_map/ppermute | solution.py:44
  44.8 9.6 %collective-permute-done.6.x2 = bf16[2,128,768]{2,1,0:T(8,128)(2,1)S(1)} collective-permute-done((bf16[2,128,768]{2,1,0:T(8,128)(2,1)S(1)}, bf16[2,128,768]{2,1,0:T(8,128)(2,1)S(1)}, u32[]{:S(2)}, u32[]{:S(2)}) %collective-permute-start.6) | collective-permute-done | bytes 393248 | tf_op jit(solution)/shard_map/ppermute | solution.py:44
  54.4 4.5 %project.2 = (f32[128,1536]{1,0:T(8,128)S(1)}, bf16[128,1536]{1,0:T(8,128)(2,1)S(1)}, bf16[128,1536]{1,0:T(8,128)(2,1)S(1)}, bf16[128,1536]{1,0:T(8,128)(2,1)S(1)}) custom-call(s32[5]{0:T(128)S(1)} %stack.32.info_ref, bf16[2,128,768]{2,1,0:T(8,128)(2,1)S(1)} %get-tuple-element.44.x0, bf16[2,128,768]{2,1,0:T(8,128)(2,1)S(1)} %collective-permute-done.5.x1, ...), custom_call_target="tpu_custom_call" | custom-call | flops 1000 | bytes 1000 | tf_op jit(solution)/shard_map/project/pallas_call | solution.py:210
  60.9 3.9 %collective-permute-start.14 = (bf16[128,1536]{1,0:T(8,128)(2,1)S(1)}, bf16[128,1536]{1,0:T(8,128)(2,1)S(1)}, u32[]{:S(2)}, u32[]{:S(2)}) collective-permute-start(bf16[128,1536]{1,0:T(8,128)(2,1)S(1)} %get-tuple-element.53), channel_id=1, source_target_pairs={{0,2},{1,3},{2,0},{3,1},{4,6},{5,7},{6,4},{7,5},{8,10},{9,11},{10,... | collective-permute-start | bytes 1179656 | tf_op jit(solution)/shard_map/ppermute | solution.py:44
  66.5 4.1 %project.3 = (f32[128,1536]{1,0:T(8,128)S(1)}, bf16[128,1536]{1,0:T(8,128)(2,1)S(1)}, bf16[128,1536]{1,0:T(8,128)(2,1)S(1)}, bf16[128,1536]{1,0:T(8,128)(2,1)S(1)}) custom-call(s32[5]{0:T(128)S(1)} %stack.32.info_ref, bf16[2,128,768]{2,1,0:T(8,128)(2,1)S(1)} %get-tuple-element.44.x0, bf16[2,128,768]{2,1,0:T(8,128)(2,1)S(1)} %collective-permute-done.5.x1, ...), custom_call_target="tpu_custom_call" | custom-call | flops 1000 | bytes 1000 | tf_op jit(solution)/shard_map/project/pallas_call | solution.py:210
  73.4 10.8 %collective-permute-start.18 = (bf16[128,1536]{1,0:T(8,128)(2,1)S(1)}, bf16[128,1536]{1,0:T(8,128)(2,1)S(1)}, u32[]{:S(2)}, u32[]{:S(2)}) collective-permute-start(bf16[128,1536]{1,0:T(8,128)(2,1)S(1)} %get-tuple-element.58), channel_id=1, source_target_pairs={{0,2},{1,3},{2,0},{3,1},{4,6},{5,7},{6,4},{7,5},{8,10},{9,11},{10,... | collective-permute-start | bytes 1179656 | tf_op jit(solution)/shard_map/ppermute | solution.py:44
  84.4 2.5 %heads.1 = (bf16[128,512]{1,0:T(8,128)(2,1)S(1)}, bf16[2,128,512]{2,1,0:T(8,128)(2,1)S(1)}) custom-call(f32[128,1536]{1,0:T(8,128)S(1)} %get-tuple-element.51.p0, bf16[128,1536]{1,0:T(8,128)(2,1)S(1)} %collective-permute-done.13.p1, bf16[128,1536]{1,0:T(8,128)(2,1)S(1)} %collective-permute-done.14.p2, bf16[128,1536]{1,0:T(8,128)(2,1)S(1)} %collective-permute-done.15.p3, ...), custom_call_target="tpu_custom_call" | custom-call | flops 1000 | bytes 1000 | tf_op jit(solution)/shard_map/heads/pallas_call | solution.py:244
  88.5 2.8 %attend.1.att_ref = bf16[128,512]{1,0:T(8,128)(2,1)S(1)} custom-call(s32[5]{0:T(128)S(1)} %stack.32.info_ref, s32[1]{0:T(128)} %collective-permute-done.count_ref, bf16[128,512]{1,0:T(8,128)(2,1)S(1)} %get-tuple-element.55.q_ref, bf16[2,128,512]{2,1,0:T(8,128)(2,1)S(1)} %get-tuple-element.56.near_ref, bf16[2,128,512]{2,1,0:T(8,128)(2,1)S(1)} %collective-permute-done.16.far_ref), custom_call_target="tpu_custom_call" | custom-call | flops 1000 | bytes 1000 | tf_op jit(solution)/shard_map/attend/pallas_call | solution.py:311
  91.3 8.1 %collective-permute-done.18.p2 = bf16[128,1536]{1,0:T(8,128)(2,1)S(1)} collective-permute-done((bf16[128,1536]{1,0:T(8,128)(2,1)S(1)}, bf16[128,1536]{1,0:T(8,128)(2,1)S(1)}, u32[]{:S(2)}, u32[]{:S(2)}) %collective-permute-start.18) | collective-permute-done | bytes 393248 | tf_op jit(solution)/shard_map/ppermute | solution.py:44
  103.9 11.9 %collective-permute-done.20.refs_1_ = bf16[128,2048]{1,0:T(8,128)(2,1)S(1)} collective-permute-done((bf16[128,2048]{1,0:T(8,128)(2,1)S(1)}, bf16[128,2048]{1,0:T(8,128)(2,1)S(1)}, u32[]{:S(2)}, u32[]{:S(2)}) %collective-permute-start.20) | collective-permute-done | bytes 524320 | tf_op jit(solution)/shard_map/ppermute | solution.py:44
  118.3 5.2 %output.2 = (bf16[64,1536]{1,0:T(8,128)(2,1)S(1)}, bf16[64,1536]{1,0:T(8,128)(2,1)S(1)}, bf16[64,1536]{1,0:T(8,128)(2,1)S(1)}, bf16[64,1536]{1,0:T(8,128)(2,1)S(...) custom-call(s32[5]{0:T(128)S(1)} %stack.32.info_ref, bf16[2,128,768]{2,1,0:T(8,128)(2,1)S(1)} %get-tuple-element.43.e_ref, ...), custom_call_target="tpu_custom_call" | custom-call | flops 1000 | bytes 1000 | tf_op jit(solution)/shard_map/output/pallas_call | solution.py:374
  125.8 4.6 %collective-permute-start.27 = (bf16[64,1536]{1,0:T(8,128)(2,1)S(1)}, bf16[64,1536]{1,0:T(8,128)(2,1)S(1)}, u32[]{:S(2)}, u32[]{:S(2)}) collective-permute-start(bf16[64,1536]{1,0:T(8,128)(2,1)S(1)} %get-tuple-element.66), channel_id=1, source_target_pairs={{0,112},{1,17},{2,50},{3,83},{4,116},{5,21},{6,54},{7,87},{8,120},... | collective-permute-start | bytes 589832 | tf_op jit(solution)/shard_map/ppermute | solution.py:44
  132.3 2.7 %collective-permute-start.29 = (bf16[64,1536]{1,0:T(8,128)(2,1)S(1)}, bf16[64,1536]{1,0:T(8,128)(2,1)S(1)}, u32[]{:S(2)}, u32[]{:S(2)}) collective-permute-start(bf16[64,1536]{1,0:T(8,128)(2,1)S(1)} %get-tuple-element.68), channel_id=1, source_target_pairs={{0,48},{1,81},{2,114},{3,19},{4,52},{5,85},{6,118},{7,23},{8,56},{... | collective-permute-start | bytes 589832 | tf_op jit(solution)/shard_map/ppermute | solution.py:44
  135.0 3.2 %output.3 = (bf16[64,1536]{1,0:T(8,128)(2,1)S(1)}, bf16[64,1536]{1,0:T(8,128)(2,1)S(1)}) custom-call(s32[5]{0:T(128)S(1)} %stack.32.info_ref, bf16[2,128,768]{2,1,0:T(8,128)(2,1)S(1)} %get-tuple-element.43.e_ref, bf16[128,2048]{1,0:T(8,128)(2,1)S(1)} %collective-permute-done.31.refs_0_, ...), custom_call_target="tpu_custom_call" | custom-call | flops 1000 | bytes 1000 | tf_op jit(solution)/shard_map/output/pallas_call | solution.py:374
  140.2 4.5 %collective-permute-start.32 = (bf16[64,1536]{1,0:T(8,128)(2,1)S(1)}, bf16[64,1536]{1,0:T(8,128)(2,1)S(1)}, u32[]{:S(2)}, u32[]{:S(2)}) collective-permute-start(bf16[64,1536]{1,0:T(8,128)(2,1)S(1)} %get-tuple-element.71), channel_id=1, source_target_pairs={{0,80},{1,113},{2,18},{3,51},{4,84},{5,117},{6,22},{7,55},{8,88},{... | collective-permute-start | bytes 589832 | tf_op jit(solution)/shard_map/ppermute | solution.py:44
  144.7 2.8 %collective-permute-start.33 = (bf16[64,1536]{1,0:T(8,128)(2,1)S(1)}, bf16[64,1536]{1,0:T(8,128)(2,1)S(1)}, u32[]{:S(2)}, u32[]{:S(2)}) collective-permute-start(bf16[64,1536]{1,0:T(8,128)(2,1)S(1)} %get-tuple-element.72), channel_id=1, source_target_pairs={{0,64},{1,97},{2,2},{3,35},{4,68},{5,101},{6,6},{7,39},{8,72},{9,1... | collective-permute-start | bytes 589832 | tf_op jit(solution)/shard_map/ppermute | solution.py:44
  147.5 7.0 %collective-permute-done.30.refs_5_ = bf16[64,1536]{1,0:T(8,128)(2,1)S(1)} collective-permute-done((bf16[64,1536]{1,0:T(8,128)(2,1)S(1)}, bf16[64,1536]{1,0:T(8,128)(2,1)S(1)}, u32[]{:S(2)}, u32[]{:S(2)}) %collective-permute-start.30) | collective-permute-done | bytes 196640 | tf_op jit(solution)/shard_map/ppermute | solution.py:44
  155.5 3.0 %collective-permute-start.35 = (bf16[16,1536]{1,0:T(8,128)(2,1)S(1)}, bf16[16,1536]{1,0:T(8,128)(2,1)S(1)}, u32[]{:S(2)}, u32[]{:S(2)}) collective-permute-start(bf16[16,1536]{1,0:T(8,128)(2,1)S(1)} %get-tuple-element.74), channel_id=1, source_target_pairs={{0,1},{1,2},{2,3},{3,0},{4,17},{5,18},{6,19},{7,16},{8,9},{9,10},{... | collective-permute-start | bytes 147464 | tf_op jit(solution)/shard_map/ppermute | solution.py:44
  159.7 4.8 %collective-permute-start.37 = (bf16[16,1536]{1,0:T(8,128)(2,1)S(1)}, bf16[16,1536]{1,0:T(8,128)(2,1)S(1)}, u32[]{:S(2)}, u32[]{:S(2)}) collective-permute-start(bf16[16,1536]{1,0:T(8,128)(2,1)S(1)} %get-tuple-element.76), channel_id=1, source_target_pairs={{0,0},{1,1},{2,2},{3,3},{4,16},{5,17},{6,18},{7,19},{8,8},{9,9},{1... | collective-permute-start | bytes 147464 | tf_op jit(solution)/shard_map/ppermute | solution.py:44
  (87 shorter events, 35.5 us)
Async XLA Ops:
  0.0 21.3 %collective-permute-start.2 = (bf16[3,768,256]{2,1,0:T(8,128)(2,1)}, bf16[3,768,256]{2,1,0:T(8,128)(2,1)}, u32[]{:S(2)}, u32[]{:S(2)}) collective-permute-start(bf16[3,768,256]{2,1,0:T(8,128)(2,1)} %bitcast.12), channel_id=1, source_target_pairs={{0,8},{1,9},{2,10},{3,11},{4,12},{5,13},{6,14},{7,15},{8,0},{9,1},... | collective-permute-start | bytes 3538952 | tf_op jit(solution)/shard_map/ppermute | solution.py:44
  0.0 21.3 %collective-permute-start.3 = (bf16[768,768]{1,0:T(8,128)(2,1)}, bf16[768,768]{1,0:T(8,128)(2,1)S(1)}, u32[]{:S(2)}, u32[]{:S(2)}) collective-permute-start(bf16[768,768]{1,0:T(8,128)(2,1)} %w00.1), channel_id=1, source_target_pairs={{0,8},{1,9},{2,10},{3,11},{4,12},{5,13},{6,14},{7,15},{8,0},{9,1},... | collective-permute-start | bytes 3538952 | tf_op jit(solution)/shard_map/ppermute | solution.py:44
  0.5 29.7 %collective-permute-start.8 = (bf16[3,768,256]{2,1,0:T(8,128)(2,1)}, bf16[3,768,256]{2,1,0:T(8,128)(2,1)}, u32[]{:S(2)}, u32[]{:S(2)}) collective-permute-start(bf16[3,768,256]{2,1,0:T(8,128)(2,1)} %bitcast.13), channel_id=1, source_target_pairs={{0,4},{1,5},{2,6},{3,7},{4,0},{5,1},{6,2},{7,3},{8,12},{9,13},{10,... | collective-permute-start | bytes 3538952 | tf_op jit(solution)/shard_map/ppermute | solution.py:44
  10.3 15.2 %collective-permute-start.1 = (bf16[2,128,768]{2,1,0:T(8,128)(2,1)}, bf16[2,128,768]{2,1,0:T(8,128)(2,1)S(1)}, u32[]{:S(2)}, u32[]{:S(2)}) collective-permute-start(bf16[2,128,768]{2,1,0:T(8,128)(2,1)} %pad_maximum_fusion), channel_id=1, source_target_pairs={{0,0},{1,1},{2,2},{3,3},{4,16},{5,17},{6,18},{7,19},{8,8},{9,9},{1... | collective-permute-start | bytes 1179656 | tf_op jit(solution)/shard_map/ppermute | solution.py:44
  30.2 24.2 %collective-permute-start.10 = (bf16[3,768,256]{2,1,0:T(8,128)(2,1)}, bf16[3,768,256]{2,1,0:T(8,128)(2,1)S(1)}, u32[]{:S(2)}, u32[]{:S(2)}) collective-permute-start(bf16[3,768,256]{2,1,0:T(8,128)(2,1)} %collective-permute-done.8.w01), channel_id=1, source_target_pairs={{0,8},{1,9},{2,10},{3,11},{4,12},{5,13},{6,14},{7,15},{8,0},{9,1},... | collective-permute-start | bytes 3538952 | tf_op jit(solution)/shard_map/ppermute | solution.py:44
  30.3 28.6 %collective-permute-start.11 = (bf16[768,768]{1,0:T(8,128)(2,1)S(1)}, bf16[768,768]{1,0:T(8,128)(2,1)S(1)}, u32[]{:S(2)}, u32[]{:S(2)}) collective-permute-start(bf16[768,768]{1,0:T(8,128)(2,1)S(1)} %copy-done.2), channel_id=1, source_target_pairs={{0,4},{1,5},{2,6},{3,7},{4,0},{5,1},{6,2},{7,3},{8,12},{9,13},{10,... | collective-permute-start | bytes 3538952 | tf_op jit(solution)/shard_map/ppermute | solution.py:44
  32.9 21.6 %collective-permute-start.6 = (bf16[2,128,768]{2,1,0:T(8,128)(2,1)S(1)}, bf16[2,128,768]{2,1,0:T(8,128)(2,1)S(1)}, u32[]{:S(2)}, u32[]{:S(2)}) collective-permute-start(bf16[2,128,768]{2,1,0:T(8,128)(2,1)S(1)} %get-tuple-element.44.x0), channel_id=1, source_target_pairs={{0,64},{1,65},{2,66},{3,67},{4,68},{5,69},{6,70},{7,71},{8,72},{9,... | collective-permute-start | bytes 1179656 | tf_op jit(solution)/shard_map/ppermute | solution.py:44
  36.7 17.8 %collective-permute-start.7 = (bf16[2,128,768]{2,1,0:T(8,128)(2,1)S(1)}, bf16[2,128,768]{2,1,0:T(8,128)(2,1)S(1)}, u32[]{:S(2)}, u32[]{:S(2)}) collective-permute-start(bf16[2,128,768]{2,1,0:T(8,128)(2,1)S(1)} %get-tuple-element.44.x0), channel_id=1, source_target_pairs={{0,96},{1,97},{2,98},{3,99},{4,100},{5,101},{6,102},{7,103},{8,104... | collective-permute-start | bytes 1179656 | tf_op jit(solution)/shard_map/ppermute | solution.py:44
  59.1 41.1 %collective-permute-start.23 = (bf16[1024,768]{1,0:T(8,128)(2,1)S(1)}, bf16[1024,768]{1,0:T(8,128)(2,1)S(1)}, u32[]{:S(2)}, u32[]{:S(2)}) collective-permute-start(bf16[1024,768]{1,0:T(8,128)(2,1)S(1)} %constant_dynamic-update-slice_fusion.refs_3_.refs_1_), channel_id=1, source_target_pairs={{0,4},{1,5},{2,6},{3,7},{4,0},{5,1},{6,2},{7,3},{8,12},{9,13},{10,... | collective-permute-start | bytes 4718600 | tf_op jit(solution)/shard_map/ppermute | solution.py:44
  60.9 23.3 %collective-permute-start.14 = (bf16[128,1536]{1,0:T(8,128)(2,1)S(1)}, bf16[128,1536]{1,0:T(8,128)(2,1)S(1)}, u32[]{:S(2)}, u32[]{:S(2)}) collective-permute-start(bf16[128,1536]{1,0:T(8,128)(2,1)S(1)} %get-tuple-element.53), channel_id=1, source_target_pairs={{0,2},{1,3},{2,0},{3,1},{4,6},{5,7},{6,4},{7,5},{8,10},{9,11},{10,... | collective-permute-start | bytes 1179656 | tf_op jit(solution)/shard_map/ppermute | solution.py:44
  64.9 19.5 %collective-permute-start.15 = (bf16[128,1536]{1,0:T(8,128)(2,1)S(1)}, bf16[128,1536]{1,0:T(8,128)(2,1)S(1)}, u32[]{:S(2)}, u32[]{:S(2)}) collective-permute-start(bf16[128,1536]{1,0:T(8,128)(2,1)S(1)} %get-tuple-element.54), channel_id=1, source_target_pairs={{0,3},{1,0},{2,1},{3,2},{4,7},{5,4},{6,5},{7,6},{8,11},{9,8},{10,9... | collective-permute-start | bytes 1179656 | tf_op jit(solution)/shard_map/ppermute | solution.py:44
  70.6 20.7 %collective-permute-start.17 = (bf16[128,1536]{1,0:T(8,128)(2,1)S(1)}, bf16[128,1536]{1,0:T(8,128)(2,1)S(1)}, u32[]{:S(2)}, u32[]{:S(2)}) collective-permute-start(bf16[128,1536]{1,0:T(8,128)(2,1)S(1)} %get-tuple-element.57), channel_id=1, source_target_pairs={{0,1},{1,2},{2,3},{3,0},{4,5},{5,6},{6,7},{7,4},{8,9},{9,10},{10,1... | collective-permute-start | bytes 1179656 | tf_op jit(solution)/shard_map/ppermute | solution.py:44
  73.4 26.0 %collective-permute-start.18 = (bf16[128,1536]{1,0:T(8,128)(2,1)S(1)}, bf16[128,1536]{1,0:T(8,128)(2,1)S(1)}, u32[]{:S(2)}, u32[]{:S(2)}) collective-permute-start(bf16[128,1536]{1,0:T(8,128)(2,1)S(1)} %get-tuple-element.58), channel_id=1, source_target_pairs={{0,2},{1,3},{2,0},{3,1},{4,6},{5,7},{6,4},{7,5},{8,10},{9,11},{10,... | collective-permute-start | bytes 1179656 | tf_op jit(solution)/shard_map/ppermute | solution.py:44
  84.2 15.2 %collective-permute-start.19 = (bf16[128,1536]{1,0:T(8,128)(2,1)S(1)}, bf16[128,1536]{1,0:T(8,128)(2,1)S(1)}, u32[]{:S(2)}, u32[]{:S(2)}) collective-permute-start(bf16[128,1536]{1,0:T(8,128)(2,1)S(1)} %get-tuple-element.59), channel_id=1, source_target_pairs={{0,3},{1,0},{2,1},{3,2},{4,7},{5,4},{6,5},{7,6},{8,11},{9,8},{10,9... | collective-permute-start | bytes 1179656 | tf_op jit(solution)/shard_map/ppermute | solution.py:44
  100.1 18.3 %collective-permute-start.22 = (bf16[1024,768]{1,0:T(8,128)(2,1)S(1)}, bf16[1024,768]{1,0:T(8,128)(2,1)S(1)}, u32[]{:S(2)}, u32[]{:S(2)}) collective-permute-start(bf16[1024,768]{1,0:T(8,128)(2,1)S(1)} %constant_dynamic-update-slice_fusion.refs_3_.refs_1_), channel_id=1, source_target_pairs={{0,8},{1,9},{2,10},{3,11},{4,12},{5,13},{6,14},{7,15},{8,0},{9,1},... | collective-permute-start | bytes 4718600 | tf_op jit(solution)/shard_map/ppermute | solution.py:44
  100.2 18.2 %collective-permute-start.24 = (bf16[1024,768]{1,0:T(8,128)(2,1)S(1)}, bf16[1024,768]{1,0:T(8,128)(2,1)S(1)}, u32[]{:S(2)}, u32[]{:S(2)}) collective-permute-start(bf16[1024,768]{1,0:T(8,128)(2,1)S(1)} %collective-permute-done.23.refs_5_.refs_3_), channel_id=1, source_target_pairs={{0,8},{1,9},{2,10},{3,11},{4,12},{5,13},{6,14},{7,15},{8,0},{9,1},... | collective-permute-start | bytes 4718600 | tf_op jit(solution)/shard_map/ppermute | solution.py:44
  100.7 15.1 %collective-permute-start.20 = (bf16[128,2048]{1,0:T(8,128)(2,1)S(1)}, bf16[128,2048]{1,0:T(8,128)(2,1)S(1)}, u32[]{:S(2)}, u32[]{:S(2)}) collective-permute-start(bf16[128,2048]{1,0:T(8,128)(2,1)S(1)} %hidden.1.refs_0_), channel_id=1, source_target_pairs={{0,1},{1,2},{2,3},{3,0},{4,5},{5,6},{6,7},{7,4},{8,9},{9,10},{10,1... | collective-permute-start | bytes 1572872 | tf_op jit(solution)/shard_map/ppermute | solution.py:44
  115.9 16.4 %collective-permute-start.31 = (bf16[128,2048]{1,0:T(8,128)(2,1)S(1)}, bf16[128,2048]{1,0:T(8,128)(2,1)S(1)}, u32[]{:S(2)}, u32[]{:S(2)}) collective-permute-start(bf16[128,2048]{1,0:T(8,128)(2,1)S(1)} %hidden.1.refs_0_), channel_id=1, source_target_pairs={{0,2},{1,3},{2,0},{3,1},{4,6},{5,7},{6,4},{7,5},{8,10},{9,11},{10,... | collective-permute-start | bytes 1572872 | tf_op jit(solution)/shard_map/ppermute | solution.py:44
  123.6 14.7 %collective-permute-start.25 = (bf16[64,1536]{1,0:T(8,128)(2,1)S(1)}, bf16[64,1536]{1,0:T(8,128)(2,1)S(1)}, u32[]{:S(2)}, u32[]{:S(2)}) collective-permute-start(bf16[64,1536]{1,0:T(8,128)(2,1)S(1)} %get-tuple-element.64), channel_id=1, source_target_pairs={{0,16},{1,49},{2,82},{3,115},{4,20},{5,53},{6,86},{7,119},{8,24},{... | collective-permute-start | bytes 589832 | tf_op jit(solution)/shard_map/ppermute | solution.py:44
  125.1 15.1 %collective-permute-start.26 = (bf16[64,1536]{1,0:T(8,128)(2,1)S(1)}, bf16[64,1536]{1,0:T(8,128)(2,1)S(1)}, u32[]{:S(2)}, u32[]{:S(2)}) collective-permute-start(bf16[64,1536]{1,0:T(8,128)(2,1)S(1)} %get-tuple-element.65), channel_id=1, source_target_pairs={{0,0},{1,33},{2,66},{3,99},{4,4},{5,37},{6,70},{7,103},{8,8},{9,41... | collective-permute-start | bytes 589832 | tf_op jit(solution)/shard_map/ppermute | solution.py:44
  125.8 18.9 %collective-permute-start.27 = (bf16[64,1536]{1,0:T(8,128)(2,1)S(1)}, bf16[64,1536]{1,0:T(8,128)(2,1)S(1)}, u32[]{:S(2)}, u32[]{:S(2)}) collective-permute-start(bf16[64,1536]{1,0:T(8,128)(2,1)S(1)} %get-tuple-element.66), channel_id=1, source_target_pairs={{0,112},{1,17},{2,50},{3,83},{4,116},{5,21},{6,54},{7,87},{8,120},... | collective-permute-start | bytes 589832 | tf_op jit(solution)/shard_map/ppermute | solution.py:44
  130.4 17.1 %collective-permute-start.28 = (bf16[64,1536]{1,0:T(8,128)(2,1)S(1)}, bf16[64,1536]{1,0:T(8,128)(2,1)S(1)}, u32[]{:S(2)}, u32[]{:S(2)}) collective-permute-start(bf16[64,1536]{1,0:T(8,128)(2,1)S(1)} %get-tuple-element.67), channel_id=1, source_target_pairs={{0,96},{1,1},{2,34},{3,67},{4,100},{5,5},{6,38},{7,71},{8,104},{9,... | collective-permute-start | bytes 589832 | tf_op jit(solution)/shard_map/ppermute | solution.py:44
  132.3 15.2 %collective-permute-start.29 = (bf16[64,1536]{1,0:T(8,128)(2,1)S(1)}, bf16[64,1536]{1,0:T(8,128)(2,1)S(1)}, u32[]{:S(2)}, u32[]{:S(2)}) collective-permute-start(bf16[64,1536]{1,0:T(8,128)(2,1)S(1)} %get-tuple-element.68), channel_id=1, source_target_pairs={{0,48},{1,81},{2,114},{3,19},{4,52},{5,85},{6,118},{7,23},{8,56},{... | collective-permute-start | bytes 589832 | tf_op jit(solution)/shard_map/ppermute | solution.py:44
  138.2 16.3 %collective-permute-start.30 = (bf16[64,1536]{1,0:T(8,128)(2,1)S(1)}, bf16[64,1536]{1,0:T(8,128)(2,1)S(1)}, u32[]{:S(2)}, u32[]{:S(2)}) collective-permute-start(bf16[64,1536]{1,0:T(8,128)(2,1)S(1)} %get-tuple-element.69), channel_id=1, source_target_pairs={{0,32},{1,65},{2,98},{3,3},{4,36},{5,69},{6,102},{7,7},{8,40},{9,7... | collective-permute-start | bytes 589832 | tf_op jit(solution)/shard_map/ppermute | solution.py:44
  (23 other events, 259.6 us)

commit v2 on v1

--- a/solution.py
+++ b/solution.py
@@ -467,13 +467,13 @@
     cols = w_mlp_in.shape[0]
     pos = patch_pos[None]
     mine = jnp.stack([lax.dynamic_slice_in_dim(patches, (x + 4 * i) * cols, cols, 1) for i in range(2)])
-    counts = route(tile_counts, count_to)
-    mine = cross(after(mine, counts))
+    mine = cross(mine)
     stat = measure(patches, pos, pos_table, 8)
     stat = after(stat, wq_c, wm_c)
+    counts = route(after(tile_counts, stat), count_to)
     bias = mlp_bias[None]
     bias_far = send(after(bias, stat), c=1)
-    e, normed = embed(info, mine, cross(stat), pos_table, norm_gain[None])
+    e, normed = embed(info, mine, after(cross(stat), counts), pos_table, norm_gain[None])
     xs = {0: normed}
     for k in (2, 1, 3):
         xs[k] = send(normed, y=k)

time: 169 us -> 169 us (level)
  waiting for transfers between devices: 52 us -> 67.1 us
  starting transfers between devices: 75.8 us -> 61.2 us
    ppermute x38, waiting for transfers between devices: 52 us -> 67.1 us  [route(): return lax.ppermute(value, AXES, pairs(place))]
    ppermute x38, starting transfers between devices: 75.8 us -> 61.2 us  [route(): return lax.ppermute(value, AXES, pairs(place))]
  transfers between devices with their start and end apart: 38 -> 38, of which waited for: 10 -> 18; matrix products, arithmetic and copies ran while one was open for 1% -> 1% of each run, Pallas kernels for 21% -> 21%
where the time goes in v2:
time: 169 us; the launch traced here: 168 us
  waiting for transfers between devices  67.1 us (40%)
  starting transfers between devices  61.2 us (36%)
  Pallas kernels  37.4 us (22%)
    ppermute x38, waiting for transfers between devices, route(): return lax.ppermute(value, AXES, pairs(place))  67.1 us
    ppermute x38, starting transfers between devices, route(): return lax.ppermute(value, AXES, pairs(place))  61.2 us
    pallas_call x1, Pallas kernels, measure(): pl.pallas_call(measure_kernel, grid=(blocks,), in_specs=[pl.BlockSpec((ro...  9.11 us
    pallas_call x2, Pallas kernels, project(): pl.pallas_call(project_kernel, grid=(steps,), in_specs=[pl.BlockSpec(memo...  8.52 us
    pallas_call x2, Pallas kernels, output(): pl.pallas_call(functools.partial(output_kernel, ks), grid=(6,), in_specs=...  8.42 us
  transfers between devices with their start and end apart: 38, of which 18 were waited for; matrix products, arithmetic and copies ran while one was open for 1% of the time, Pallas kernels for 21%

profile of v2, /device:TPU:32, one launch (start us, length us, event | category | flops | bytes accessed | tf_op | source)
XLA Modules:
  0.0 168.2 jit_solution(7586840309053169923)
XLA Ops:
  2.4 5.4 %collective-permute-start = (bf16[2,128,768]{2,1,0:T(8,128)(2,1)}, bf16[2,128,768]{2,1,0:T(8,128)(2,1)S(1)}, u32[]{:S(2)}, u32[]{:S(2)}) collective-permute-start(bf16[2,128,768]{2,1,0:T(8,128)(2,1)} %pad_maximum_fusion), channel_id=1, source_target_pairs={{0,0},{1,1},{2,2},{3,3},{4,16},{5,17},{6,18},{7,19},{8,8},{9,9},{1... | collective-permute-start | bytes 1179656 | tf_op jit(solution)/shard_map/ppermute | solution.py:44
  7.8 9.1 %measure.1 = f32[8,128]{1,0:T(8,128)S(1)} custom-call(bf16[128,6144]{1,0:T(8,128)(2,1)S(1)} %copy-done, s32[1,128]{1,0:T(1,128)S(1)} %bitcast.16, bf16[1024,6144]{1,0:T(8,128)(2,1)} %t3.3, bf16[1024,6144]{1,0:T(8,128)(2,1)} %t3.3, bf16[1024,6144]{1,0:T(8,128)(2,1)} %t3.3, bf16[1024,6144]{1,0:T(8,128)(2,1)} %t3.3), custom_call_target="tpu_custom_call" | custom-call | flops 1000 | bytes 1000 | tf_op jit(solution)/shard_map/measure/pallas_call | solution.py:125
  19.1 6.4 %collective-permute-start.4 = (s32[1]{0:T(128)}, s32[1]{0:T(128)}, u32[]{:S(2)}, u32[]{:S(2)}) collective-permute-start(s32[1]{0:T(128)} %param.13), channel_id=1, source_target_pairs={{0,0},{1,20},{2,1},{3,21},{4,18},{5,6},{6,19},{7,7},{8,8},{9,28},{... | collective-permute-start | bytes 20 | tf_op jit(solution)/shard_map/ppermute | solution.py:44
  26.9 3.3 %embed.1 = (bf16[2,128,768]{2,1,0:T(8,128)(2,1)S(1)}, bf16[2,128,768]{2,1,0:T(8,128)(2,1)S(1)}) custom-call(s32[5]{0:T(128)S(1)} %stack.32.info_ref, bf16[2,128,768]{2,1,0:T(8,128)(2,1)S(1)} %collective-permute-done.patches_ref, f32[8,128]{1,0:T(8,128)S(1)} %collective-permute-done.3.stat_ref, f32[1,6144]{1,0:T(1,128)S(1)} %bitcast.15, ...), custom_call_target="tpu_custom_call" | custom-call | flops 1000 | bytes 1000 | tf_op jit(solution)/shard_map/embed/pallas_call | solution.py:158
  32.0 2.7 %collective-permute-start.6 = (bf16[2,128,768]{2,1,0:T(8,128)(2,1)S(1)}, bf16[2,128,768]{2,1,0:T(8,128)(2,1)S(1)}, u32[]{:S(2)}, u32[]{:S(2)}) collective-permute-start(bf16[2,128,768]{2,1,0:T(8,128)(2,1)S(1)} %get-tuple-element.46.x0), channel_id=1, source_target_pairs={{0,64},{1,65},{2,66},{3,67},{4,68},{5,69},{6,70},{7,71},{8,72},{9,... | collective-permute-start | bytes 1179656 | tf_op jit(solution)/shard_map/ppermute | solution.py:44
  35.0 8.0 %collective-permute-done.5.x1 = bf16[2,128,768]{2,1,0:T(8,128)(2,1)S(1)} collective-permute-done((bf16[2,128,768]{2,1,0:T(8,128)(2,1)S(1)}, bf16[2,128,768]{2,1,0:T(8,128)(2,1)S(1)}, u32[]{:S(2)}, u32[]{:S(2)}) %collective-permute-start.5) | collective-permute-done | bytes 393248 | tf_op jit(solution)/shard_map/ppermute | solution.py:44
  43.1 9.4 %collective-permute-done.6.x2 = bf16[2,128,768]{2,1,0:T(8,128)(2,1)S(1)} collective-permute-done((bf16[2,128,768]{2,1,0:T(8,128)(2,1)S(1)}, bf16[2,128,768]{2,1,0:T(8,128)(2,1)S(1)}, u32[]{:S(2)}, u32[]{:S(2)}) %collective-permute-start.6) | collective-permute-done | bytes 393248 | tf_op jit(solution)/shard_map/ppermute | solution.py:44
  52.5 4.5 %project.2 = (f32[128,1536]{1,0:T(8,128)S(1)}, bf16[128,1536]{1,0:T(8,128)(2,1)S(1)}, bf16[128,1536]{1,0:T(8,128)(2,1)S(1)}, bf16[128,1536]{1,0:T(8,128)(2,1)S(1)}) custom-call(s32[5]{0:T(128)S(1)} %stack.32.info_ref, bf16[2,128,768]{2,1,0:T(8,128)(2,1)S(1)} %get-tuple-element.46.x0, bf16[2,128,768]{2,1,0:T(8,128)(2,1)S(1)} %collective-permute-done.5.x1, ...), custom_call_target="tpu_custom_call" | custom-call | flops 1000 | bytes 1000 | tf_op jit(solution)/shard_map/project/pallas_call | solution.py:210
  63.6 4.1 %project.3 = (f32[128,1536]{1,0:T(8,128)S(1)}, bf16[128,1536]{1,0:T(8,128)(2,1)S(1)}, bf16[128,1536]{1,0:T(8,128)(2,1)S(1)}, bf16[128,1536]{1,0:T(8,128)(2,1)S(1)}) custom-call(s32[5]{0:T(128)S(1)} %stack.32.info_ref, bf16[2,128,768]{2,1,0:T(8,128)(2,1)S(1)} %get-tuple-element.46.x0, bf16[2,128,768]{2,1,0:T(8,128)(2,1)S(1)} %collective-permute-done.5.x1, ...), custom_call_target="tpu_custom_call" | custom-call | flops 1000 | bytes 1000 | tf_op jit(solution)/shard_map/project/pallas_call | solution.py:210
  68.9 11.1 %collective-permute-done.13.p1 = bf16[128,1536]{1,0:T(8,128)(2,1)S(1)} collective-permute-done((bf16[128,1536]{1,0:T(8,128)(2,1)S(1)}, bf16[128,1536]{1,0:T(8,128)(2,1)S(1)}, u32[]{:S(2)}, u32[]{:S(2)}) %collective-permute-start.13) | collective-permute-done | bytes 393248 | tf_op jit(solution)/shard_map/ppermute | solution.py:44
  81.7 2.5 %heads.1 = (bf16[128,512]{1,0:T(8,128)(2,1)S(1)}, bf16[2,128,512]{2,1,0:T(8,128)(2,1)S(1)}) custom-call(f32[128,1536]{1,0:T(8,128)S(1)} %get-tuple-element.53.p0, bf16[128,1536]{1,0:T(8,128)(2,1)S(1)} %collective-permute-done.13.p1, bf16[128,1536]{1,0:T(8,128)(2,1)S(1)} %collective-permute-done.14.p2, bf16[128,1536]{1,0:T(8,128)(2,1)S(1)} %collective-permute-done.15.p3, ...), custom_call_target="tpu_custom_call" | custom-call | flops 1000 | bytes 1000 | tf_op jit(solution)/shard_map/heads/pallas_call | solution.py:244
  85.8 2.8 %attend.1.att_ref = bf16[128,512]{1,0:T(8,128)(2,1)S(1)} custom-call(s32[5]{0:T(128)S(1)} %stack.32.info_ref, s32[1]{0:T(128)} %collective-permute-done.4.count_ref, bf16[128,512]{1,0:T(8,128)(2,1)S(1)} %get-tuple-element.57.q_ref, bf16[2,128,512]{2,1,0:T(8,128)(2,1)S(1)} %get-tuple-element.58.near_ref, bf16[2,128,512]{2,1,0:T(8,128)(2,1)S(1)} %collective-permute-done.16.far_ref), custom_call_target="tpu_custom_call" | custom-call | flops 1000 | bytes 1000 | tf_op jit(solution)/shard_map/attend/pallas_call | solution.py:311
  89.1 8.2 %collective-permute-done.18.p2 = bf16[128,1536]{1,0:T(8,128)(2,1)S(1)} collective-permute-done((bf16[128,1536]{1,0:T(8,128)(2,1)S(1)}, bf16[128,1536]{1,0:T(8,128)(2,1)S(1)}, u32[]{:S(2)}, u32[]{:S(2)}) %collective-permute-start.18) | collective-permute-done | bytes 393248 | tf_op jit(solution)/shard_map/ppermute | solution.py:44
  102.2 11.9 %collective-permute-done.20.refs_1_ = bf16[128,2048]{1,0:T(8,128)(2,1)S(1)} collective-permute-done((bf16[128,2048]{1,0:T(8,128)(2,1)S(1)}, bf16[128,2048]{1,0:T(8,128)(2,1)S(1)}, u32[]{:S(2)}, u32[]{:S(2)}) %collective-permute-start.20) | collective-permute-done | bytes 524320 | tf_op jit(solution)/shard_map/ppermute | solution.py:44
  114.1 2.6 %collective-permute-start.31 = (bf16[128,2048]{1,0:T(8,128)(2,1)S(1)}, bf16[128,2048]{1,0:T(8,128)(2,1)S(1)}, u32[]{:S(2)}, u32[]{:S(2)}) collective-permute-start(bf16[128,2048]{1,0:T(8,128)(2,1)S(1)} %hidden.1.refs_0_), channel_id=1, source_target_pairs={{0,2},{1,3},{2,0},{3,1},{4,6},{5,7},{6,4},{7,5},{8,10},{9,11},{10,... | collective-permute-start | bytes 1572872 | tf_op jit(solution)/shard_map/ppermute | solution.py:44
  116.7 5.2 %output.2 = (bf16[64,1536]{1,0:T(8,128)(2,1)S(1)}, bf16[64,1536]{1,0:T(8,128)(2,1)S(1)}, bf16[64,1536]{1,0:T(8,128)(2,1)S(1)}, bf16[64,1536]{1,0:T(8,128)(2,1)S(...) custom-call(s32[5]{0:T(128)S(1)} %stack.32.info_ref, bf16[2,128,768]{2,1,0:T(8,128)(2,1)S(1)} %get-tuple-element.45.e_ref, ...), custom_call_target="tpu_custom_call" | custom-call | flops 1000 | bytes 1000 | tf_op jit(solution)/shard_map/output/pallas_call | solution.py:374
  121.9 2.7 %collective-permute-start.25 = (bf16[64,1536]{1,0:T(8,128)(2,1)S(1)}, bf16[64,1536]{1,0:T(8,128)(2,1)S(1)}, u32[]{:S(2)}, u32[]{:S(2)}) collective-permute-start(bf16[64,1536]{1,0:T(8,128)(2,1)S(1)} %get-tuple-element.66), channel_id=1, source_target_pairs={{0,16},{1,49},{2,82},{3,115},{4,20},{5,53},{6,86},{7,119},{8,24},{... | collective-permute-start | bytes 589832 | tf_op jit(solution)/shard_map/ppermute | solution.py:44
  125.2 3.3 %collective-permute-start.27 = (bf16[64,1536]{1,0:T(8,128)(2,1)S(1)}, bf16[64,1536]{1,0:T(8,128)(2,1)S(1)}, u32[]{:S(2)}, u32[]{:S(2)}) collective-permute-start(bf16[64,1536]{1,0:T(8,128)(2,1)S(1)} %get-tuple-element.68), channel_id=1, source_target_pairs={{0,112},{1,17},{2,50},{3,83},{4,116},{5,21},{6,54},{7,87},{8,120},... | collective-permute-start | bytes 589832 | tf_op jit(solution)/shard_map/ppermute | solution.py:44
  131.0 4.5 %collective-permute-start.29 = (bf16[64,1536]{1,0:T(8,128)(2,1)S(1)}, bf16[64,1536]{1,0:T(8,128)(2,1)S(1)}, u32[]{:S(2)}, u32[]{:S(2)}) collective-permute-start(bf16[64,1536]{1,0:T(8,128)(2,1)S(1)} %get-tuple-element.70), channel_id=1, source_target_pairs={{0,48},{1,81},{2,114},{3,19},{4,52},{5,85},{6,118},{7,23},{8,56},{... | collective-permute-start | bytes 589832 | tf_op jit(solution)/shard_map/ppermute | solution.py:44
  135.4 3.2 %output.3 = (bf16[64,1536]{1,0:T(8,128)(2,1)S(1)}, bf16[64,1536]{1,0:T(8,128)(2,1)S(1)}) custom-call(s32[5]{0:T(128)S(1)} %stack.32.info_ref, bf16[2,128,768]{2,1,0:T(8,128)(2,1)S(1)} %get-tuple-element.45.e_ref, bf16[128,2048]{1,0:T(8,128)(2,1)S(1)} %collective-permute-done.31.refs_0_, ...), custom_call_target="tpu_custom_call" | custom-call | flops 1000 | bytes 1000 | tf_op jit(solution)/shard_map/output/pallas_call | solution.py:374
  140.6 6.2 %collective-permute-start.32 = (bf16[64,1536]{1,0:T(8,128)(2,1)S(1)}, bf16[64,1536]{1,0:T(8,128)(2,1)S(1)}, u32[]{:S(2)}, u32[]{:S(2)}) collective-permute-start(bf16[64,1536]{1,0:T(8,128)(2,1)S(1)} %get-tuple-element.73), channel_id=1, source_target_pairs={{0,80},{1,113},{2,18},{3,51},{4,84},{5,117},{6,22},{7,55},{8,88},{... | collective-permute-start | bytes 589832 | tf_op jit(solution)/shard_map/ppermute | solution.py:44
  148.7 3.7 %collective-permute-done.30.refs_5_ = bf16[64,1536]{1,0:T(8,128)(2,1)S(1)} collective-permute-done((bf16[64,1536]{1,0:T(8,128)(2,1)S(1)}, bf16[64,1536]{1,0:T(8,128)(2,1)S(1)}, u32[]{:S(2)}, u32[]{:S(2)}) %collective-permute-start.30) | collective-permute-done | bytes 196640 | tf_op jit(solution)/shard_map/ppermute | solution.py:44
  157.4 3.6 %collective-permute-start.36 = (bf16[16,1536]{1,0:T(8,128)(2,1)S(1)}, bf16[16,1536]{1,0:T(8,128)(2,1)S(1)}, u32[]{:S(2)}, u32[]{:S(2)}) collective-permute-start(bf16[16,1536]{1,0:T(8,128)(2,1)S(1)} %get-tuple-element.77), channel_id=1, source_target_pairs={{0,3},{1,0},{2,1},{3,2},{4,19},{5,16},{6,17},{7,18},{8,11},{9,8},{... | collective-permute-start | bytes 147464 | tf_op jit(solution)/shard_map/ppermute | solution.py:44
  163.6 3.4 %collective-permute-done.37.refs_3_ = bf16[16,1536]{1,0:T(8,128)(2,1)S(1)} collective-permute-done((bf16[16,1536]{1,0:T(8,128)(2,1)S(1)}, bf16[16,1536]{1,0:T(8,128)(2,1)S(1)}, u32[]{:S(2)}, u32[]{:S(2)}) %collective-permute-start.37) | collective-permute-done | bytes 49184 | tf_op jit(solution)/shard_map/ppermute | solution.py:44
  (87 shorter events, 40.2 us)
Async XLA Ops:
  0.0 16.9 %collective-permute-start.1 = (bf16[3,768,256]{2,1,0:T(8,128)(2,1)}, bf16[3,768,256]{2,1,0:T(8,128)(2,1)}, u32[]{:S(2)}, u32[]{:S(2)}) collective-permute-start(bf16[3,768,256]{2,1,0:T(8,128)(2,1)} %bitcast.12), channel_id=1, source_target_pairs={{0,8},{1,9},{2,10},{3,11},{4,12},{5,13},{6,14},{7,15},{8,0},{9,1},... | collective-permute-start | bytes 3538952 | tf_op jit(solution)/shard_map/ppermute | solution.py:44
  0.0 16.9 %collective-permute-start.2 = (bf16[768,768]{1,0:T(8,128)(2,1)}, bf16[768,768]{1,0:T(8,128)(2,1)S(1)}, u32[]{:S(2)}, u32[]{:S(2)}) collective-permute-start(bf16[768,768]{1,0:T(8,128)(2,1)} %w00.1), channel_id=1, source_target_pairs={{0,8},{1,9},{2,10},{3,11},{4,12},{5,13},{6,14},{7,15},{8,0},{9,1},... | collective-permute-start | bytes 3538952 | tf_op jit(solution)/shard_map/ppermute | solution.py:44
  0.5 29.7 %collective-permute-start.8 = (bf16[3,768,256]{2,1,0:T(8,128)(2,1)}, bf16[3,768,256]{2,1,0:T(8,128)(2,1)}, u32[]{:S(2)}, u32[]{:S(2)}) collective-permute-start(bf16[3,768,256]{2,1,0:T(8,128)(2,1)} %bitcast.13), channel_id=1, source_target_pairs={{0,4},{1,5},{2,6},{3,7},{4,0},{5,1},{6,2},{7,3},{8,12},{9,13},{10,... | collective-permute-start | bytes 3538952 | tf_op jit(solution)/shard_map/ppermute | solution.py:44
  2.4 24.5 %collective-permute-start = (bf16[2,128,768]{2,1,0:T(8,128)(2,1)}, bf16[2,128,768]{2,1,0:T(8,128)(2,1)S(1)}, u32[]{:S(2)}, u32[]{:S(2)}) collective-permute-start(bf16[2,128,768]{2,1,0:T(8,128)(2,1)} %pad_maximum_fusion), channel_id=1, source_target_pairs={{0,0},{1,1},{2,2},{3,3},{4,16},{5,17},{6,18},{7,19},{8,8},{9,9},{1... | collective-permute-start | bytes 1179656 | tf_op jit(solution)/shard_map/ppermute | solution.py:44
  30.3 22.2 %collective-permute-start.10 = (bf16[3,768,256]{2,1,0:T(8,128)(2,1)}, bf16[3,768,256]{2,1,0:T(8,128)(2,1)S(1)}, u32[]{:S(2)}, u32[]{:S(2)}) collective-permute-start(bf16[3,768,256]{2,1,0:T(8,128)(2,1)} %collective-permute-done.8.w01), channel_id=1, source_target_pairs={{0,8},{1,9},{2,10},{3,11},{4,12},{5,13},{6,14},{7,15},{8,0},{9,1},... | collective-permute-start | bytes 3538952 | tf_op jit(solution)/shard_map/ppermute | solution.py:44
  30.4 28.4 %collective-permute-start.11 = (bf16[768,768]{1,0:T(8,128)(2,1)S(1)}, bf16[768,768]{1,0:T(8,128)(2,1)S(1)}, u32[]{:S(2)}, u32[]{:S(2)}) collective-permute-start(bf16[768,768]{1,0:T(8,128)(2,1)S(1)} %copy-done.2), channel_id=1, source_target_pairs={{0,4},{1,5},{2,6},{3,7},{4,0},{5,1},{6,2},{7,3},{8,12},{9,13},{10,... | collective-permute-start | bytes 3538952 | tf_op jit(solution)/shard_map/ppermute | solution.py:44
  32.0 20.5 %collective-permute-start.6 = (bf16[2,128,768]{2,1,0:T(8,128)(2,1)S(1)}, bf16[2,128,768]{2,1,0:T(8,128)(2,1)S(1)}, u32[]{:S(2)}, u32[]{:S(2)}) collective-permute-start(bf16[2,128,768]{2,1,0:T(8,128)(2,1)S(1)} %get-tuple-element.46.x0), channel_id=1, source_target_pairs={{0,64},{1,65},{2,66},{3,67},{4,68},{5,69},{6,70},{7,71},{8,72},{9,... | collective-permute-start | bytes 1179656 | tf_op jit(solution)/shard_map/ppermute | solution.py:44
  34.7 17.8 %collective-permute-start.7 = (bf16[2,128,768]{2,1,0:T(8,128)(2,1)S(1)}, bf16[2,128,768]{2,1,0:T(8,128)(2,1)S(1)}, u32[]{:S(2)}, u32[]{:S(2)}) collective-permute-start(bf16[2,128,768]{2,1,0:T(8,128)(2,1)S(1)} %get-tuple-element.46.x0), channel_id=1, source_target_pairs={{0,96},{1,97},{2,98},{3,99},{4,100},{5,101},{6,102},{7,103},{8,104... | collective-permute-start | bytes 1179656 | tf_op jit(solution)/shard_map/ppermute | solution.py:44
  58.8 39.6 %collective-permute-start.23 = (bf16[1024,768]{1,0:T(8,128)(2,1)S(1)}, bf16[1024,768]{1,0:T(8,128)(2,1)S(1)}, u32[]{:S(2)}, u32[]{:S(2)}) collective-permute-start(bf16[1024,768]{1,0:T(8,128)(2,1)S(1)} %constant_dynamic-update-slice_fusion.refs_3_.refs_1_), channel_id=1, source_target_pairs={{0,4},{1,5},{2,6},{3,7},{4,0},{5,1},{6,2},{7,3},{8,12},{9,13},{10,... | collective-permute-start | bytes 4718600 | tf_op jit(solution)/shard_map/ppermute | solution.py:44
  59.2 20.8 %collective-permute-start.13 = (bf16[128,1536]{1,0:T(8,128)(2,1)S(1)}, bf16[128,1536]{1,0:T(8,128)(2,1)S(1)}, u32[]{:S(2)}, u32[]{:S(2)}) collective-permute-start(bf16[128,1536]{1,0:T(8,128)(2,1)S(1)} %get-tuple-element.54), channel_id=1, source_target_pairs={{0,1},{1,2},{2,3},{3,0},{4,5},{5,6},{6,7},{7,4},{8,9},{9,10},{10,1... | collective-permute-start | bytes 1179656 | tf_op jit(solution)/shard_map/ppermute | solution.py:44
  60.8 20.3 %collective-permute-start.14 = (bf16[128,1536]{1,0:T(8,128)(2,1)S(1)}, bf16[128,1536]{1,0:T(8,128)(2,1)S(1)}, u32[]{:S(2)}, u32[]{:S(2)}) collective-permute-start(bf16[128,1536]{1,0:T(8,128)(2,1)S(1)} %get-tuple-element.55), channel_id=1, source_target_pairs={{0,2},{1,3},{2,0},{3,1},{4,6},{5,7},{6,4},{7,5},{8,10},{9,11},{10,... | collective-permute-start | bytes 1179656 | tf_op jit(solution)/shard_map/ppermute | solution.py:44
  62.7 18.9 %collective-permute-start.15 = (bf16[128,1536]{1,0:T(8,128)(2,1)S(1)}, bf16[128,1536]{1,0:T(8,128)(2,1)S(1)}, u32[]{:S(2)}, u32[]{:S(2)}) collective-permute-start(bf16[128,1536]{1,0:T(8,128)(2,1)S(1)} %get-tuple-element.56), channel_id=1, source_target_pairs={{0,3},{1,0},{2,1},{3,2},{4,7},{5,4},{6,5},{7,6},{8,11},{9,8},{10,9... | collective-permute-start | bytes 1179656 | tf_op jit(solution)/shard_map/ppermute | solution.py:44
  67.6 21.4 %collective-permute-start.17 = (bf16[128,1536]{1,0:T(8,128)(2,1)S(1)}, bf16[128,1536]{1,0:T(8,128)(2,1)S(1)}, u32[]{:S(2)}, u32[]{:S(2)}) collective-permute-start(bf16[128,1536]{1,0:T(8,128)(2,1)S(1)} %get-tuple-element.59), channel_id=1, source_target_pairs={{0,1},{1,2},{2,3},{3,0},{4,5},{5,6},{6,7},{7,4},{8,9},{9,10},{10,1... | collective-permute-start | bytes 1179656 | tf_op jit(solution)/shard_map/ppermute | solution.py:44
  80.0 17.2 %collective-permute-start.18 = (bf16[128,1536]{1,0:T(8,128)(2,1)S(1)}, bf16[128,1536]{1,0:T(8,128)(2,1)S(1)}, u32[]{:S(2)}, u32[]{:S(2)}) collective-permute-start(bf16[128,1536]{1,0:T(8,128)(2,1)S(1)} %get-tuple-element.60), channel_id=1, source_target_pairs={{0,2},{1,3},{2,0},{3,1},{4,6},{5,7},{6,4},{7,5},{8,10},{9,11},{10,... | collective-permute-start | bytes 1179656 | tf_op jit(solution)/shard_map/ppermute | solution.py:44
  81.1 16.5 %collective-permute-start.19 = (bf16[128,1536]{1,0:T(8,128)(2,1)S(1)}, bf16[128,1536]{1,0:T(8,128)(2,1)S(1)}, u32[]{:S(2)}, u32[]{:S(2)}) collective-permute-start(bf16[128,1536]{1,0:T(8,128)(2,1)S(1)} %get-tuple-element.61), channel_id=1, source_target_pairs={{0,3},{1,0},{2,1},{3,2},{4,7},{5,4},{6,5},{7,6},{8,11},{9,8},{10,9... | collective-permute-start | bytes 1179656 | tf_op jit(solution)/shard_map/ppermute | solution.py:44
  98.4 18.3 %collective-permute-start.22 = (bf16[1024,768]{1,0:T(8,128)(2,1)S(1)}, bf16[1024,768]{1,0:T(8,128)(2,1)S(1)}, u32[]{:S(2)}, u32[]{:S(2)}) collective-permute-start(bf16[1024,768]{1,0:T(8,128)(2,1)S(1)} %constant_dynamic-update-slice_fusion.refs_3_.refs_1_), channel_id=1, source_target_pairs={{0,8},{1,9},{2,10},{3,11},{4,12},{5,13},{6,14},{7,15},{8,0},{9,1},... | collective-permute-start | bytes 4718600 | tf_op jit(solution)/shard_map/ppermute | solution.py:44
  98.5 18.2 %collective-permute-start.24 = (bf16[1024,768]{1,0:T(8,128)(2,1)S(1)}, bf16[1024,768]{1,0:T(8,128)(2,1)S(1)}, u32[]{:S(2)}, u32[]{:S(2)}) collective-permute-start(bf16[1024,768]{1,0:T(8,128)(2,1)S(1)} %collective-permute-done.23.refs_5_.refs_3_), channel_id=1, source_target_pairs={{0,8},{1,9},{2,10},{3,11},{4,12},{5,13},{6,14},{7,15},{8,0},{9,1},... | collective-permute-start | bytes 4718600 | tf_op jit(solution)/shard_map/ppermute | solution.py:44
  99.0 15.1 %collective-permute-start.20 = (bf16[128,2048]{1,0:T(8,128)(2,1)S(1)}, bf16[128,2048]{1,0:T(8,128)(2,1)S(1)}, u32[]{:S(2)}, u32[]{:S(2)}) collective-permute-start(bf16[128,2048]{1,0:T(8,128)(2,1)S(1)} %hidden.1.refs_0_), channel_id=1, source_target_pairs={{0,1},{1,2},{2,3},{3,0},{4,5},{5,6},{6,7},{7,4},{8,9},{9,10},{10,1... | collective-permute-start | bytes 1572872 | tf_op jit(solution)/shard_map/ppermute | solution.py:44
  114.1 16.9 %collective-permute-start.31 = (bf16[128,2048]{1,0:T(8,128)(2,1)S(1)}, bf16[128,2048]{1,0:T(8,128)(2,1)S(1)}, u32[]{:S(2)}, u32[]{:S(2)}) collective-permute-start(bf16[128,2048]{1,0:T(8,128)(2,1)S(1)} %hidden.1.refs_0_), channel_id=1, source_target_pairs={{0,2},{1,3},{2,0},{3,1},{4,6},{5,7},{6,4},{7,5},{8,10},{9,11},{10,... | collective-permute-start | bytes 1572872 | tf_op jit(solution)/shard_map/ppermute | solution.py:44
  121.9 16.8 %collective-permute-start.25 = (bf16[64,1536]{1,0:T(8,128)(2,1)S(1)}, bf16[64,1536]{1,0:T(8,128)(2,1)S(1)}, u32[]{:S(2)}, u32[]{:S(2)}) collective-permute-start(bf16[64,1536]{1,0:T(8,128)(2,1)S(1)} %get-tuple-element.66), channel_id=1, source_target_pairs={{0,16},{1,49},{2,82},{3,115},{4,20},{5,53},{6,86},{7,119},{8,24},{... | collective-permute-start | bytes 589832 | tf_op jit(solution)/shard_map/ppermute | solution.py:44
  124.5 16.1 %collective-permute-start.26 = (bf16[64,1536]{1,0:T(8,128)(2,1)S(1)}, bf16[64,1536]{1,0:T(8,128)(2,1)S(1)}, u32[]{:S(2)}, u32[]{:S(2)}) collective-permute-start(bf16[64,1536]{1,0:T(8,128)(2,1)S(1)} %get-tuple-element.67), channel_id=1, source_target_pairs={{0,0},{1,33},{2,66},{3,99},{4,4},{5,37},{6,70},{7,103},{8,8},{9,41... | collective-permute-start | bytes 589832 | tf_op jit(solution)/shard_map/ppermute | solution.py:44
  125.2 21.6 %collective-permute-start.27 = (bf16[64,1536]{1,0:T(8,128)(2,1)S(1)}, bf16[64,1536]{1,0:T(8,128)(2,1)S(1)}, u32[]{:S(2)}, u32[]{:S(2)}) collective-permute-start(bf16[64,1536]{1,0:T(8,128)(2,1)S(1)} %get-tuple-element.68), channel_id=1, source_target_pairs={{0,112},{1,17},{2,50},{3,83},{4,116},{5,21},{6,54},{7,87},{8,120},... | collective-permute-start | bytes 589832 | tf_op jit(solution)/shard_map/ppermute | solution.py:44
  128.5 20.2 %collective-permute-start.28 = (bf16[64,1536]{1,0:T(8,128)(2,1)S(1)}, bf16[64,1536]{1,0:T(8,128)(2,1)S(1)}, u32[]{:S(2)}, u32[]{:S(2)}) collective-permute-start(bf16[64,1536]{1,0:T(8,128)(2,1)S(1)} %get-tuple-element.69), channel_id=1, source_target_pairs={{0,96},{1,1},{2,34},{3,67},{4,100},{5,5},{6,38},{7,71},{8,104},{9,... | collective-permute-start | bytes 589832 | tf_op jit(solution)/shard_map/ppermute | solution.py:44
  131.0 17.7 %collective-permute-start.29 = (bf16[64,1536]{1,0:T(8,128)(2,1)S(1)}, bf16[64,1536]{1,0:T(8,128)(2,1)S(1)}, u32[]{:S(2)}, u32[]{:S(2)}) collective-permute-start(bf16[64,1536]{1,0:T(8,128)(2,1)S(1)} %get-tuple-element.70), channel_id=1, source_target_pairs={{0,48},{1,81},{2,114},{3,19},{4,52},{5,85},{6,118},{7,23},{8,56},{... | collective-permute-start | bytes 589832 | tf_op jit(solution)/shard_map/ppermute | solution.py:44
  (23 other events, 249.9 us)

commit v3 on v2

--- a/solution.py
+++ b/solution.py
@@ -176,16 +176,18 @@
     )(info, patches, stat, gain, table, table, table, table)
 
 
-def project_kernel(info_ref, x0, x1, x2, x3, w00, w01, w10, w11, o0, o1, o2, o3, held):
+def project_kernel(info_ref, x0, x1, x2a, x2b, x3, w00, w01, w10, w11, o0, o1, o2, o3, held):
     rows = x0.shape[1]
     zl, x = info_ref[1], info_ref[2]
 
     @pl.when(pl.program_id(0) == 0)
     def _():
-        for far, ref in enumerate((x0, x1, x2, x3)):
+        for far, ref in enumerate((x0, x1, None, x3)):
             k = lax.rem(8 - x - far, 4)
             for s in range(2):
-                held[s, pl.ds(pl.multiple_of(k * rows, rows), rows)] = ref[lax.rem(zl + s, 2)]
+                side = lax.rem(zl + s, 2)
+                block = jnp.where(side == 0, x2a[0], x2b[0]) if ref is None else ref[side]
+                held[s, pl.ds(pl.multiple_of(k * rows, rows), rows)] = block
 
     def weight(ref):
         w = ref[...]
@@ -210,7 +212,7 @@
     return pl.pallas_call(
         project_kernel,
         grid=(steps,),
-        in_specs=[pl.BlockSpec(memory_space=pltpu.SMEM)] + [whole((2, rows, depth))] * 4 + [spec] * 4,
+        in_specs=[pl.BlockSpec(memory_space=pltpu.SMEM)] + [whole(v.shape) for v in xs] + [spec] * 4,
         out_specs=[pl.BlockSpec((rows, n), lambda i: (0, i))] * 4,
         out_shape=[shape_of(rows, steps * n, dtype=f32 if k == 0 else bf16) for k in range(4)],
         scratch_shapes=[pltpu.VMEM((2, 4 * rows, depth), bf16)],
@@ -318,18 +320,20 @@
     )(info, count, q, near, far)
 
 
-def output_kernel(ks, info_ref, e_ref, *refs):
-    u_refs, weights, outs = refs[: len(ks)], refs[len(ks) : len(ks) + 4], refs[len(ks) + 4 : -2]
+def output_kernel(ks, count, info_ref, e_ref, *refs):
+    u_refs, weights, outs = refs[:count], refs[count : count + 4], refs[count + 4 : -2]
     held, total = refs[-2:]
     step = pl.program_id(0)
-    rows, a_cols = u_refs[0].shape[0], u_refs[0].shape[1] // 4
+    rows, a_cols = e_ref.shape[1], u_refs[0].shape[1] // 4
     half, n = rows // 2, total.shape[1]
     zh, zl, x = info_ref[0], info_ref[1], info_ref[2]
 
     @pl.when(step == 0)
     def _():
-        for i, ref in enumerate(u_refs):
-            held[i * rows : (i + 1) * rows] = ref[...]
+        at = 0
+        for ref in u_refs:
+            held[at : at + ref.shape[0]] = ref[...]
+            at += ref.shape[0]
 
     def multiply(ws, side):
         depth = a_cols // 2
@@ -366,13 +370,13 @@
 
 
 def output(info, e, ks, units, ws):
-    rows, half = units[0].shape[0], units[0].shape[0] // 2
+    rows, half = e.shape[1], e.shape[1] // 2
     depth, width = ws[0][0].shape
     n = width // 3
     near = pl.BlockSpec((depth, n), lambda j: (0, jnp.minimum(j, 2)))
     far = pl.BlockSpec((depth, n), lambda j: (0, jnp.maximum(j - 3, 0)))
     return pl.pallas_call(
-        functools.partial(output_kernel, ks),
+        functools.partial(output_kernel, ks, len(units)),
         grid=(6,),
         in_specs=[pl.BlockSpec(memory_space=pltpu.SMEM)]
         + [whole(v.shape) for v in [e] + units]
@@ -475,11 +479,11 @@
     bias_far = send(after(bias, stat), c=1)
     e, normed = embed(info, mine, after(cross(stat), counts), pos_table, norm_gain[None])
     xs = {0: normed}
-    for k in (2, 1, 3):
+    for k in (1, 3):
         xs[k] = send(normed, y=k)
-    xs = [xs[k] for k in range(4)]
-
-    wm_z = send(after(w_mlp_in, wq_z, normed, bias_far), zl=1)
+    xs = [xs[0], xs[1], send(xs[1][0:1], y=1), send(xs[3][1:2], y=3), xs[3]]
+
+    wm_z = send(after(w_mlp_in, wq_z, mine, bias_far), zl=1)
     wq_cz = send(after(wq_z, normed, bias_far), c=1)
     wo = jnp.concatenate([after(w_attn_out, normed), w_mlp_out])
 
@@ -507,11 +511,11 @@
 
         return place
 
-    far = {0: units, 1: send(units, x=1), 3: send(units, x=3)}
-    far[2] = send(after(units, far[1], far[3]), x=2)
+    far = {0: [units], 1: [send(units, x=1)], 3: [send(units, x=3)]}
+    far[2] = [send(after(units, far[1][0], far[3][0]), x=2)]
     parts = []
     for ks in GROUPS:
-        got = output(info, e, ks, [far[k] for k in ks], [[wo, wo_c], [wo_z, wo_cz]])
+        got = output(info, e, ks, [v for k in ks for v in far[k]], [[wo, wo_c], [wo_z, wo_cz]])
         parts += [route(got[2 * i + h], to_owner(k, h)) for i, k in enumerate(ks) for h in (1, 0)]
     pieces = finish(info, parts)
     return assemble(info, [cross(pieces[k], k) for k in (2, 1, 3, 0)])

time: 169 us -> 170 us (level)
  starting transfers between devices: 61.2 us -> 75.6 us
  waiting for transfers between devices: 67.1 us -> 53.9 us
    ppermute x38 -> x39, starting transfers between devices: 61.2 us -> 75.6 us  [route(): return lax.ppermute(value, AXES, pairs(place))]
    ppermute x38 -> x39, waiting for transfers between devices: 67.1 us -> 53.9 us  [route(): return lax.ppermute(value, AXES, pairs(place))]
  transfers between devices with their start and end apart: 38 -> 39, of which waited for: 18 -> 12; matrix products, arithmetic and copies ran while one was open for 1% -> 1% of each run, Pallas kernels for 21% -> 19%
where the time goes in v3:
time: 170 us; the launch traced here: 169 us
  starting transfers between devices  75.6 us (44%)
  waiting for transfers between devices  53.9 us (32%)
  Pallas kernels  37.1 us (22%)
    ppermute x39, starting transfers between devices, route(): return lax.ppermute(value, AXES, pairs(place))  75.6 us
    ppermute x39, waiting for transfers between devices, route(): return lax.ppermute(value, AXES, pairs(place))  53.9 us
    pallas_call x1, Pallas kernels, measure(): pl.pallas_call(measure_kernel, grid=(blocks,), in_specs=[pl.BlockSpec((ro...  9.11 us
    pallas_call x2, Pallas kernels, project(): pl.pallas_call(project_kernel, grid=(steps,), in_specs=[pl.BlockSpec(memo...  8.54 us
    pallas_call x2, Pallas kernels, output(): pl.pallas_call(functools.partial(output_kernel, ks, len(units)), grid=(6,...  8.42 us
  transfers between devices with their start and end apart: 39, of which 12 were waited for; matrix products, arithmetic and copies ran while one was open for 1% of the time, Pallas kernels for 19%

profile of v3, /device:TPU:32, one launch (start us, length us, event | category | flops | bytes accessed | tf_op | source)
XLA Modules:
  0.0 169.2 jit_solution(15898725151245287334)
XLA Ops:
  2.4 5.4 %collective-permute-start = (bf16[2,128,768]{2,1,0:T(8,128)(2,1)}, bf16[2,128,768]{2,1,0:T(8,128)(2,1)S(1)}, u32[]{:S(2)}, u32[]{:S(2)}) collective-permute-start(bf16[2,128,768]{2,1,0:T(8,128)(2,1)} %pad_maximum_fusion), channel_id=1, source_target_pairs={{0,0},{1,1},{2,2},{3,3},{4,16},{5,17},{6,18},{7,19},{8,8},{9,9},{1... | collective-permute-start | bytes 1179656 | tf_op jit(solution)/shard_map/ppermute | solution.py:44
  7.8 9.1 %measure.1 = f32[8,128]{1,0:T(8,128)S(1)} custom-call(bf16[128,6144]{1,0:T(8,128)(2,1)S(1)} %copy-done, s32[1,128]{1,0:T(1,128)S(1)} %bitcast.16, bf16[1024,6144]{1,0:T(8,128)(2,1)} %t3.3, bf16[1024,6144]{1,0:T(8,128)(2,1)} %t3.3, bf16[1024,6144]{1,0:T(8,128)(2,1)} %t3.3, bf16[1024,6144]{1,0:T(8,128)(2,1)} %t3.3), custom_call_target="tpu_custom_call" | custom-call | flops 1000 | bytes 1000 | tf_op jit(solution)/shard_map/measure/pallas_call | solution.py:125
  19.1 6.4 %collective-permute-start.4 = (s32[1]{0:T(128)}, s32[1]{0:T(128)}, u32[]{:S(2)}, u32[]{:S(2)}) collective-permute-start(s32[1]{0:T(128)} %param.13), channel_id=1, source_target_pairs={{0,0},{1,20},{2,1},{3,21},{4,18},{5,6},{6,19},{7,7},{8,8},{9,28},{... | collective-permute-start | bytes 20 | tf_op jit(solution)/shard_map/ppermute | solution.py:44
  25.5 3.3 %collective-permute-done.9.w01 = bf16[3,768,256]{2,1,0:T(8,128)(2,1)} collective-permute-done((bf16[3,768,256]{2,1,0:T(8,128)(2,1)}, bf16[3,768,256]{2,1,0:T(8,128)(2,1)}, u32[]{:S(2)}, u32[]{:S(2)}) %collective-permute-start.9) | collective-permute-done | bytes 1179680 | tf_op jit(solution)/shard_map/ppermute | solution.py:44
  28.8 3.1 %embed.1 = (bf16[2,128,768]{2,1,0:T(8,128)(2,1)S(1)}, bf16[2,128,768]{2,1,0:T(8,128)(2,1)S(1)}) custom-call(s32[5]{0:T(128)S(1)} %stack.32.info_ref, bf16[2,128,768]{2,1,0:T(8,128)(2,1)S(1)} %collective-permute-done.patches_ref, f32[8,128]{1,0:T(8,128)S(1)} %collective-permute-done.3.stat_ref, f32[1,6144]{1,0:T(1,128)S(1)} %bitcast.15, ...), custom_call_target="tpu_custom_call" | custom-call | flops 1000 | bytes 1000 | tf_op jit(solution)/shard_map/embed/pallas_call | solution.py:158
  35.6 9.2 %collective-permute-done.5.x1 = bf16[2,128,768]{2,1,0:T(8,128)(2,1)S(1)} collective-permute-done((bf16[2,128,768]{2,1,0:T(8,128)(2,1)S(1)}, bf16[2,128,768]{2,1,0:T(8,128)(2,1)S(1)}, u32[]{:S(2)}, u32[]{:S(2)}) %collective-permute-start.5) | collective-permute-done | bytes 393248 | tf_op jit(solution)/shard_map/ppermute | solution.py:44
  45.3 3.0 %collective-permute-start.8 = (bf16[1,128,768]{2,1,0:T(8,128)(2,1)S(1)}, bf16[1,128,768]{2,1,0:T(8,128)(2,1)S(1)}, u32[]{:S(2)}, u32[]{:S(2)}) collective-permute-start(bf16[1,128,768]{2,1,0:T(8,128)(2,1)S(1)} %slice.9), channel_id=1, source_target_pairs={{0,96},{1,97},{2,98},{3,99},{4,100},{5,101},{6,102},{7,103},{8,104... | collective-permute-start | bytes 589832 | tf_op jit(solution)/shard_map/ppermute | solution.py:44
  48.3 4.0 %collective-permute-done.6.x2a = bf16[1,128,768]{2,1,0:T(8,128)(2,1)S(1)} collective-permute-done((bf16[1,128,768]{2,1,0:T(8,128)(2,1)S(1)}, bf16[1,128,768]{2,1,0:T(8,128)(2,1)S(1)}, u32[]{:S(2)}, u32[]{:S(2)}) %collective-permute-start.6) | collective-permute-done | bytes 196640 | tf_op jit(solution)/shard_map/ppermute | solution.py:44
  52.3 4.5 %project.2 = (f32[128,1536]{1,0:T(8,128)S(1)}, bf16[128,1536]{1,0:T(8,128)(2,1)S(1)}, bf16[128,1536]{1,0:T(8,128)(2,1)S(1)}, bf16[128,1536]{1,0:T(8,128)(2,1)S(1)}) custom-call(s32[5]{0:T(128)S(1)} %stack.32.info_ref, bf16[2,128,768]{2,1,0:T(8,128)(2,1)S(1)} %get-tuple-element.46.x0, bf16[2,128,768]{2,1,0:T(8,128)(2,1)S(1)} %collective-permute-done.5.x1, ...), custom_call_target="tpu_custom_call" | custom-call | flops 1000 | bytes 1000 | tf_op jit(solution)/shard_map/project/pallas_call | solution.py:212
  56.8 3.6 %collective-permute-done.12.w01 = bf16[768,768]{1,0:T(8,128)(2,1)S(1)} collective-permute-done((bf16[768,768]{1,0:T(8,128)(2,1)S(1)}, bf16[768,768]{1,0:T(8,128)(2,1)S(1)}, u32[]{:S(2)}, u32[]{:S(2)}) %collective-permute-start.12) | collective-permute-done | bytes 1179680 | tf_op jit(solution)/shard_map/ppermute | solution.py:44
  62.4 2.7 %collective-permute-start.15 = (bf16[128,1536]{1,0:T(8,128)(2,1)S(1)}, bf16[128,1536]{1,0:T(8,128)(2,1)S(1)}, u32[]{:S(2)}, u32[]{:S(2)}) collective-permute-start(bf16[128,1536]{1,0:T(8,128)(2,1)S(1)} %get-tuple-element.55), channel_id=1, source_target_pairs={{0,2},{1,3},{2,0},{3,1},{4,6},{5,7},{6,4},{7,5},{8,10},{9,11},{10,... | collective-permute-start | bytes 1179656 | tf_op jit(solution)/shard_map/ppermute | solution.py:44
  66.5 4.1 %project.3 = (f32[128,1536]{1,0:T(8,128)S(1)}, bf16[128,1536]{1,0:T(8,128)(2,1)S(1)}, bf16[128,1536]{1,0:T(8,128)(2,1)S(1)}, bf16[128,1536]{1,0:T(8,128)(2,1)S(1)}) custom-call(s32[5]{0:T(128)S(1)} %stack.32.info_ref, bf16[2,128,768]{2,1,0:T(8,128)(2,1)S(1)} %get-tuple-element.46.x0, bf16[2,128,768]{2,1,0:T(8,128)(2,1)S(1)} %collective-permute-done.5.x1, ...), custom_call_target="tpu_custom_call" | custom-call | flops 1000 | bytes 1000 | tf_op jit(solution)/shard_map/project/pallas_call | solution.py:212
  73.4 10.8 %collective-permute-start.19 = (bf16[128,1536]{1,0:T(8,128)(2,1)S(1)}, bf16[128,1536]{1,0:T(8,128)(2,1)S(1)}, u32[]{:S(2)}, u32[]{:S(2)}) collective-permute-start(bf16[128,1536]{1,0:T(8,128)(2,1)S(1)} %get-tuple-element.60), channel_id=1, source_target_pairs={{0,2},{1,3},{2,0},{3,1},{4,6},{5,7},{6,4},{7,5},{8,10},{9,11},{10,... | collective-permute-start | bytes 1179656 | tf_op jit(solution)/shard_map/ppermute | solution.py:44
  88.4 2.7 %attend.1.att_ref = bf16[128,512]{1,0:T(8,128)(2,1)S(1)} custom-call(s32[5]{0:T(128)S(1)} %stack.32.info_ref, s32[1]{0:T(128)} %collective-permute-done.4.count_ref, bf16[128,512]{1,0:T(8,128)(2,1)S(1)} %get-tuple-element.57.q_ref, bf16[2,128,512]{2,1,0:T(8,128)(2,1)S(1)} %get-tuple-element.58.near_ref, bf16[2,128,512]{2,1,0:T(8,128)(2,1)S(1)} %collective-permute-done.17.far_ref), custom_call_target="tpu_custom_call" | custom-call | flops 1000 | bytes 1000 | tf_op jit(solution)/shard_map/attend/pallas_call | solution.py:313
  91.1 8.7 %collective-permute-done.19.p2 = bf16[128,1536]{1,0:T(8,128)(2,1)S(1)} collective-permute-done((bf16[128,1536]{1,0:T(8,128)(2,1)S(1)}, bf16[128,1536]{1,0:T(8,128)(2,1)S(1)}, u32[]{:S(2)}, u32[]{:S(2)}) %collective-permute-start.19) | collective-permute-done | bytes 393248 | tf_op jit(solution)/shard_map/ppermute | solution.py:44
  104.2 11.9 %collective-permute-done.21.refs_1_ = bf16[128,2048]{1,0:T(8,128)(2,1)S(1)} collective-permute-done((bf16[128,2048]{1,0:T(8,128)(2,1)S(1)}, bf16[128,2048]{1,0:T(8,128)(2,1)S(1)}, u32[]{:S(2)}, u32[]{:S(2)}) %collective-permute-start.21) | collective-permute-done | bytes 524320 | tf_op jit(solution)/shard_map/ppermute | solution.py:44
  118.4 5.2 %output.2 = (bf16[64,1536]{1,0:T(8,128)(2,1)S(1)}, bf16[64,1536]{1,0:T(8,128)(2,1)S(1)}, bf16[64,1536]{1,0:T(8,128)(2,1)S(1)}, bf16[64,1536]{1,0:T(8,128)(2,1)S(...) custom-call(s32[5]{0:T(128)S(1)} %stack.32.info_ref, bf16[2,128,768]{2,1,0:T(8,128)(2,1)S(1)} %get-tuple-element.45.e_ref, ...), custom_call_target="tpu_custom_call" | custom-call | flops 1000 | bytes 1000 | tf_op jit(solution)/shard_map/output/pallas_call | solution.py:378
  123.6 3.2 %collective-permute-start.26 = (bf16[64,1536]{1,0:T(8,128)(2,1)S(1)}, bf16[64,1536]{1,0:T(8,128)(2,1)S(1)}, u32[]{:S(2)}, u32[]{:S(2)}) collective-permute-start(bf16[64,1536]{1,0:T(8,128)(2,1)S(1)} %get-tuple-element.66), channel_id=1, source_target_pairs={{0,16},{1,49},{2,82},{3,115},{4,20},{5,53},{6,86},{7,119},{8,24},{... | collective-permute-start | bytes 589832 | tf_op jit(solution)/shard_map/ppermute | solution.py:44
  127.5 2.9 %collective-permute-start.28 = (bf16[64,1536]{1,0:T(8,128)(2,1)S(1)}, bf16[64,1536]{1,0:T(8,128)(2,1)S(1)}, u32[]{:S(2)}, u32[]{:S(2)}) collective-permute-start(bf16[64,1536]{1,0:T(8,128)(2,1)S(1)} %get-tuple-element.68), channel_id=1, source_target_pairs={{0,112},{1,17},{2,50},{3,83},{4,116},{5,21},{6,54},{7,87},{8,120},... | collective-permute-start | bytes 589832 | tf_op jit(solution)/shard_map/ppermute | solution.py:44
  133.1 3.9 %collective-permute-start.30 = (bf16[64,1536]{1,0:T(8,128)(2,1)S(1)}, bf16[64,1536]{1,0:T(8,128)(2,1)S(1)}, u32[]{:S(2)}, u32[]{:S(2)}) collective-permute-start(bf16[64,1536]{1,0:T(8,128)(2,1)S(1)} %get-tuple-element.70), channel_id=1, source_target_pairs={{0,48},{1,81},{2,114},{3,19},{4,52},{5,85},{6,118},{7,23},{8,56},{... | collective-permute-start | bytes 589832 | tf_op jit(solution)/shard_map/ppermute | solution.py:44
  136.9 3.2 %output.3 = (bf16[64,1536]{1,0:T(8,128)(2,1)S(1)}, bf16[64,1536]{1,0:T(8,128)(2,1)S(1)}) custom-call(s32[5]{0:T(128)S(1)} %stack.32.info_ref, bf16[2,128,768]{2,1,0:T(8,128)(2,1)S(1)} %get-tuple-element.45.e_ref, bf16[128,2048]{1,0:T(8,128)(2,1)S(1)} %collective-permute-done.32.refs_0_, ...), custom_call_target="tpu_custom_call" | custom-call | flops 1000 | bytes 1000 | tf_op jit(solution)/shard_map/output/pallas_call | solution.py:378
  142.1 4.7 %collective-permute-start.33 = (bf16[64,1536]{1,0:T(8,128)(2,1)S(1)}, bf16[64,1536]{1,0:T(8,128)(2,1)S(1)}, u32[]{:S(2)}, u32[]{:S(2)}) collective-permute-start(bf16[64,1536]{1,0:T(8,128)(2,1)S(1)} %get-tuple-element.73), channel_id=1, source_target_pairs={{0,80},{1,113},{2,18},{3,51},{4,84},{5,117},{6,22},{7,55},{8,88},{... | collective-permute-start | bytes 589832 | tf_op jit(solution)/shard_map/ppermute | solution.py:44
  151.3 2.8 %collective-permute-done.33.refs_6_ = bf16[64,1536]{1,0:T(8,128)(2,1)S(1)} collective-permute-done((bf16[64,1536]{1,0:T(8,128)(2,1)S(1)}, bf16[64,1536]{1,0:T(8,128)(2,1)S(1)}, u32[]{:S(2)}, u32[]{:S(2)}) %collective-permute-start.33) | collective-permute-done | bytes 196640 | tf_op jit(solution)/shard_map/ppermute | solution.py:44
  161.9 4.0 %collective-permute-start.38 = (bf16[16,1536]{1,0:T(8,128)(2,1)S(1)}, bf16[16,1536]{1,0:T(8,128)(2,1)S(1)}, u32[]{:S(2)}, u32[]{:S(2)}) collective-permute-start(bf16[16,1536]{1,0:T(8,128)(2,1)S(1)} %get-tuple-element.78), channel_id=1, source_target_pairs={{0,0},{1,1},{2,2},{3,3},{4,16},{5,17},{6,18},{7,19},{8,8},{9,9},{1... | collective-permute-start | bytes 147464 | tf_op jit(solution)/shard_map/ppermute | solution.py:44
  (91 shorter events, 46.4 us)
Async XLA Ops:
  0.0 17.0 %collective-permute-start.1 = (bf16[3,768,256]{2,1,0:T(8,128)(2,1)}, bf16[3,768,256]{2,1,0:T(8,128)(2,1)}, u32[]{:S(2)}, u32[]{:S(2)}) collective-permute-start(bf16[3,768,256]{2,1,0:T(8,128)(2,1)} %bitcast.12), channel_id=1, source_target_pairs={{0,8},{1,9},{2,10},{3,11},{4,12},{5,13},{6,14},{7,15},{8,0},{9,1},... | collective-permute-start | bytes 3538952 | tf_op jit(solution)/shard_map/ppermute | solution.py:44
  0.0 16.9 %collective-permute-start.2 = (bf16[768,768]{1,0:T(8,128)(2,1)}, bf16[768,768]{1,0:T(8,128)(2,1)S(1)}, u32[]{:S(2)}, u32[]{:S(2)}) collective-permute-start(bf16[768,768]{1,0:T(8,128)(2,1)} %w00.1), channel_id=1, source_target_pairs={{0,8},{1,9},{2,10},{3,11},{4,12},{5,13},{6,14},{7,15},{8,0},{9,1},... | collective-permute-start | bytes 3538952 | tf_op jit(solution)/shard_map/ppermute | solution.py:44
  0.5 28.3 %collective-permute-start.9 = (bf16[3,768,256]{2,1,0:T(8,128)(2,1)}, bf16[3,768,256]{2,1,0:T(8,128)(2,1)}, u32[]{:S(2)}, u32[]{:S(2)}) collective-permute-start(bf16[3,768,256]{2,1,0:T(8,128)(2,1)} %bitcast.13), channel_id=1, source_target_pairs={{0,4},{1,5},{2,6},{3,7},{4,0},{5,1},{6,2},{7,3},{8,12},{9,13},{10,... | collective-permute-start | bytes 3538952 | tf_op jit(solution)/shard_map/ppermute | solution.py:44
  2.4 23.1 %collective-permute-start = (bf16[2,128,768]{2,1,0:T(8,128)(2,1)}, bf16[2,128,768]{2,1,0:T(8,128)(2,1)S(1)}, u32[]{:S(2)}, u32[]{:S(2)}) collective-permute-start(bf16[2,128,768]{2,1,0:T(8,128)(2,1)} %pad_maximum_fusion), channel_id=1, source_target_pairs={{0,0},{1,1},{2,2},{3,3},{4,16},{5,17},{6,18},{7,19},{8,8},{9,9},{1... | collective-permute-start | bytes 1179656 | tf_op jit(solution)/shard_map/ppermute | solution.py:44
  31.9 20.4 %collective-permute-start.11 = (bf16[3,768,256]{2,1,0:T(8,128)(2,1)}, bf16[3,768,256]{2,1,0:T(8,128)(2,1)S(1)}, u32[]{:S(2)}, u32[]{:S(2)}) collective-permute-start(bf16[3,768,256]{2,1,0:T(8,128)(2,1)} %collective-permute-done.9.w01), channel_id=1, source_target_pairs={{0,8},{1,9},{2,10},{3,11},{4,12},{5,13},{6,14},{7,15},{8,0},{9,1},... | collective-permute-start | bytes 3538952 | tf_op jit(solution)/shard_map/ppermute | solution.py:44
  32.0 28.4 %collective-permute-start.12 = (bf16[768,768]{1,0:T(8,128)(2,1)S(1)}, bf16[768,768]{1,0:T(8,128)(2,1)S(1)}, u32[]{:S(2)}, u32[]{:S(2)}) collective-permute-start(bf16[768,768]{1,0:T(8,128)(2,1)S(1)} %copy-done.2), channel_id=1, source_target_pairs={{0,4},{1,5},{2,6},{3,7},{4,0},{5,1},{6,2},{7,3},{8,12},{9,13},{10,... | collective-permute-start | bytes 3538952 | tf_op jit(solution)/shard_map/ppermute | solution.py:44
  32.4 12.4 %collective-permute-start.5 = (bf16[2,128,768]{2,1,0:T(8,128)(2,1)S(1)}, bf16[2,128,768]{2,1,0:T(8,128)(2,1)S(1)}, u32[]{:S(2)}, u32[]{:S(2)}) collective-permute-start(bf16[2,128,768]{2,1,0:T(8,128)(2,1)S(1)} %get-tuple-element.46.x0), channel_id=1, source_target_pairs={{0,32},{1,33},{2,34},{3,35},{4,36},{5,37},{6,38},{7,39},{8,40},{9,... | collective-permute-start | bytes 1179656 | tf_op jit(solution)/shard_map/ppermute | solution.py:44
  60.5 40.0 %collective-permute-start.24 = (bf16[1024,768]{1,0:T(8,128)(2,1)S(1)}, bf16[1024,768]{1,0:T(8,128)(2,1)S(1)}, u32[]{:S(2)}, u32[]{:S(2)}) collective-permute-start(bf16[1024,768]{1,0:T(8,128)(2,1)S(1)} %constant_dynamic-update-slice_fusion.refs_3_.refs_1_), channel_id=1, source_target_pairs={{0,4},{1,5},{2,6},{3,7},{4,0},{5,1},{6,2},{7,3},{8,12},{9,13},{10,... | collective-permute-start | bytes 4718600 | tf_op jit(solution)/shard_map/ppermute | solution.py:44
  60.9 12.5 %collective-permute-start.14 = (bf16[128,1536]{1,0:T(8,128)(2,1)S(1)}, bf16[128,1536]{1,0:T(8,128)(2,1)S(1)}, u32[]{:S(2)}, u32[]{:S(2)}) collective-permute-start(bf16[128,1536]{1,0:T(8,128)(2,1)S(1)} %get-tuple-element.54), channel_id=1, source_target_pairs={{0,1},{1,2},{2,3},{3,0},{4,5},{5,6},{6,7},{7,4},{8,9},{9,10},{10,1... | collective-permute-start | bytes 1179656 | tf_op jit(solution)/shard_map/ppermute | solution.py:44
  62.4 21.9 %collective-permute-start.15 = (bf16[128,1536]{1,0:T(8,128)(2,1)S(1)}, bf16[128,1536]{1,0:T(8,128)(2,1)S(1)}, u32[]{:S(2)}, u32[]{:S(2)}) collective-permute-start(bf16[128,1536]{1,0:T(8,128)(2,1)S(1)} %get-tuple-element.55), channel_id=1, source_target_pairs={{0,2},{1,3},{2,0},{3,1},{4,6},{5,7},{6,4},{7,5},{8,10},{9,11},{10,... | collective-permute-start | bytes 1179656 | tf_op jit(solution)/shard_map/ppermute | solution.py:44
  65.1 19.1 %collective-permute-start.16 = (bf16[128,1536]{1,0:T(8,128)(2,1)S(1)}, bf16[128,1536]{1,0:T(8,128)(2,1)S(1)}, u32[]{:S(2)}, u32[]{:S(2)}) collective-permute-start(bf16[128,1536]{1,0:T(8,128)(2,1)S(1)} %get-tuple-element.56), channel_id=1, source_target_pairs={{0,3},{1,0},{2,1},{3,2},{4,7},{5,4},{6,5},{7,6},{8,11},{9,8},{10,9... | collective-permute-start | bytes 1179656 | tf_op jit(solution)/shard_map/ppermute | solution.py:44
  70.6 20.4 %collective-permute-start.18 = (bf16[128,1536]{1,0:T(8,128)(2,1)S(1)}, bf16[128,1536]{1,0:T(8,128)(2,1)S(1)}, u32[]{:S(2)}, u32[]{:S(2)}) collective-permute-start(bf16[128,1536]{1,0:T(8,128)(2,1)S(1)} %get-tuple-element.59), channel_id=1, source_target_pairs={{0,1},{1,2},{2,3},{3,0},{4,5},{5,6},{6,7},{7,4},{8,9},{9,10},{10,1... | collective-permute-start | bytes 1179656 | tf_op jit(solution)/shard_map/ppermute | solution.py:44
  73.4 26.3 %collective-permute-start.19 = (bf16[128,1536]{1,0:T(8,128)(2,1)S(1)}, bf16[128,1536]{1,0:T(8,128)(2,1)S(1)}, u32[]{:S(2)}, u32[]{:S(2)}) collective-permute-start(bf16[128,1536]{1,0:T(8,128)(2,1)S(1)} %get-tuple-element.60), channel_id=1, source_target_pairs={{0,2},{1,3},{2,0},{3,1},{4,6},{5,7},{6,4},{7,5},{8,10},{9,11},{10,... | collective-permute-start | bytes 1179656 | tf_op jit(solution)/shard_map/ppermute | solution.py:44
  84.2 15.5 %collective-permute-start.20 = (bf16[128,1536]{1,0:T(8,128)(2,1)S(1)}, bf16[128,1536]{1,0:T(8,128)(2,1)S(1)}, u32[]{:S(2)}, u32[]{:S(2)}) collective-permute-start(bf16[128,1536]{1,0:T(8,128)(2,1)S(1)} %get-tuple-element.61), channel_id=1, source_target_pairs={{0,3},{1,0},{2,1},{3,2},{4,7},{5,4},{6,5},{7,6},{8,11},{9,8},{10,9... | collective-permute-start | bytes 1179656 | tf_op jit(solution)/shard_map/ppermute | solution.py:44
  100.4 18.0 %collective-permute-start.23 = (bf16[1024,768]{1,0:T(8,128)(2,1)S(1)}, bf16[1024,768]{1,0:T(8,128)(2,1)S(1)}, u32[]{:S(2)}, u32[]{:S(2)}) collective-permute-start(bf16[1024,768]{1,0:T(8,128)(2,1)S(1)} %constant_dynamic-update-slice_fusion.refs_3_.refs_1_), channel_id=1, source_target_pairs={{0,8},{1,9},{2,10},{3,11},{4,12},{5,13},{6,14},{7,15},{8,0},{9,1},... | collective-permute-start | bytes 4718600 | tf_op jit(solution)/shard_map/ppermute | solution.py:44
  100.5 17.9 %collective-permute-start.25 = (bf16[1024,768]{1,0:T(8,128)(2,1)S(1)}, bf16[1024,768]{1,0:T(8,128)(2,1)S(1)}, u32[]{:S(2)}, u32[]{:S(2)}) collective-permute-start(bf16[1024,768]{1,0:T(8,128)(2,1)S(1)} %collective-permute-done.24.refs_5_.refs_3_), channel_id=1, source_target_pairs={{0,8},{1,9},{2,10},{3,11},{4,12},{5,13},{6,14},{7,15},{8,0},{9,1},... | collective-permute-start | bytes 4718600 | tf_op jit(solution)/shard_map/ppermute | solution.py:44
  101.0 15.1 %collective-permute-start.21 = (bf16[128,2048]{1,0:T(8,128)(2,1)S(1)}, bf16[128,2048]{1,0:T(8,128)(2,1)S(1)}, u32[]{:S(2)}, u32[]{:S(2)}) collective-permute-start(bf16[128,2048]{1,0:T(8,128)(2,1)S(1)} %hidden.1.refs_0_), channel_id=1, source_target_pairs={{0,1},{1,2},{2,3},{3,0},{4,5},{5,6},{6,7},{7,4},{8,9},{9,10},{10,1... | collective-permute-start | bytes 1572872 | tf_op jit(solution)/shard_map/ppermute | solution.py:44
  102.3 13.8 %collective-permute-start.22 = (bf16[128,2048]{1,0:T(8,128)(2,1)S(1)}, bf16[128,2048]{1,0:T(8,128)(2,1)S(1)}, u32[]{:S(2)}, u32[]{:S(2)}) collective-permute-start(bf16[128,2048]{1,0:T(8,128)(2,1)S(1)} %hidden.1.refs_0_), channel_id=1, source_target_pairs={{0,3},{1,0},{2,1},{3,2},{4,7},{5,4},{6,5},{7,6},{8,11},{9,8},{10,9... | collective-permute-start | bytes 1572872 | tf_op jit(solution)/shard_map/ppermute | solution.py:44
  116.2 16.9 %collective-permute-start.32 = (bf16[128,2048]{1,0:T(8,128)(2,1)S(1)}, bf16[128,2048]{1,0:T(8,128)(2,1)S(1)}, u32[]{:S(2)}, u32[]{:S(2)}) collective-permute-start(bf16[128,2048]{1,0:T(8,128)(2,1)S(1)} %hidden.1.refs_0_), channel_id=1, source_target_pairs={{0,2},{1,3},{2,0},{3,1},{4,6},{5,7},{6,4},{7,5},{8,10},{9,11},{10,... | collective-permute-start | bytes 1572872 | tf_op jit(solution)/shard_map/ppermute | solution.py:44
  123.6 16.5 %collective-permute-start.26 = (bf16[64,1536]{1,0:T(8,128)(2,1)S(1)}, bf16[64,1536]{1,0:T(8,128)(2,1)S(1)}, u32[]{:S(2)}, u32[]{:S(2)}) collective-permute-start(bf16[64,1536]{1,0:T(8,128)(2,1)S(1)} %get-tuple-element.66), channel_id=1, source_target_pairs={{0,16},{1,49},{2,82},{3,115},{4,20},{5,53},{6,86},{7,119},{8,24},{... | collective-permute-start | bytes 589832 | tf_op jit(solution)/shard_map/ppermute | solution.py:44
  126.8 15.3 %collective-permute-start.27 = (bf16[64,1536]{1,0:T(8,128)(2,1)S(1)}, bf16[64,1536]{1,0:T(8,128)(2,1)S(1)}, u32[]{:S(2)}, u32[]{:S(2)}) collective-permute-start(bf16[64,1536]{1,0:T(8,128)(2,1)S(1)} %get-tuple-element.67), channel_id=1, source_target_pairs={{0,0},{1,33},{2,66},{3,99},{4,4},{5,37},{6,70},{7,103},{8,8},{9,41... | collective-permute-start | bytes 589832 | tf_op jit(solution)/shard_map/ppermute | solution.py:44
  127.5 19.4 %collective-permute-start.28 = (bf16[64,1536]{1,0:T(8,128)(2,1)S(1)}, bf16[64,1536]{1,0:T(8,128)(2,1)S(1)}, u32[]{:S(2)}, u32[]{:S(2)}) collective-permute-start(bf16[64,1536]{1,0:T(8,128)(2,1)S(1)} %get-tuple-element.68), channel_id=1, source_target_pairs={{0,112},{1,17},{2,50},{3,83},{4,116},{5,21},{6,54},{7,87},{8,120},... | collective-permute-start | bytes 589832 | tf_op jit(solution)/shard_map/ppermute | solution.py:44
  130.4 18.3 %collective-permute-start.29 = (bf16[64,1536]{1,0:T(8,128)(2,1)S(1)}, bf16[64,1536]{1,0:T(8,128)(2,1)S(1)}, u32[]{:S(2)}, u32[]{:S(2)}) collective-permute-start(bf16[64,1536]{1,0:T(8,128)(2,1)S(1)} %get-tuple-element.69), channel_id=1, source_target_pairs={{0,96},{1,1},{2,34},{3,67},{4,100},{5,5},{6,38},{7,71},{8,104},{9,... | collective-permute-start | bytes 589832 | tf_op jit(solution)/shard_map/ppermute | solution.py:44
  133.1 15.7 %collective-permute-start.30 = (bf16[64,1536]{1,0:T(8,128)(2,1)S(1)}, bf16[64,1536]{1,0:T(8,128)(2,1)S(1)}, u32[]{:S(2)}, u32[]{:S(2)}) collective-permute-start(bf16[64,1536]{1,0:T(8,128)(2,1)S(1)} %get-tuple-element.70), channel_id=1, source_target_pairs={{0,48},{1,81},{2,114},{3,19},{4,52},{5,85},{6,118},{7,23},{8,56},{... | collective-permute-start | bytes 589832 | tf_op jit(solution)/shard_map/ppermute | solution.py:44
  (24 other events, 249.6 us)

commit v4 on v3

--- a/solution.py
+++ b/solution.py
@@ -483,7 +483,7 @@
         xs[k] = send(normed, y=k)
     xs = [xs[0], xs[1], send(xs[1][0:1], y=1), send(xs[3][1:2], y=3), xs[3]]
 
-    wm_z = send(after(w_mlp_in, wq_z, mine, bias_far), zl=1)
+    wm_z = send(after(w_mlp_in, wq_z, normed, bias_far), zl=1)
     wq_cz = send(after(wq_z, normed, bias_far), c=1)
     wo = jnp.concatenate([after(w_attn_out, normed), w_mlp_out])
 

time: 170 us -> 169 us (level)
  starting transfers between devices: 75.6 us -> 62.8 us
  waiting for transfers between devices: 53.9 us -> 65.7 us
    ppermute x39, starting transfers between devices: 75.6 us -> 62.8 us  [route(): return lax.ppermute(value, AXES, pairs(place))]
    ppermute x39, waiting for transfers between devices: 53.9 us -> 65.7 us  [route(): return lax.ppermute(value, AXES, pairs(place))]
  transfers between devices with their start and end apart: 39 -> 39, of which waited for: 12 -> 16; matrix products, arithmetic and copies ran while one was open for 1% -> 1% of each run, Pallas kernels for 19% -> 21%
where the time goes in v4:
time: 169 us; the launch traced here: 168 us
  waiting for transfers between devices  65.7 us (39%)
  starting transfers between devices  62.8 us (37%)
  Pallas kernels  37.1 us (22%)
    ppermute x39, waiting for transfers between devices, route(): return lax.ppermute(value, AXES, pairs(place))  65.7 us
    ppermute x39, starting transfers between devices, route(): return lax.ppermute(value, AXES, pairs(place))  62.8 us
    pallas_call x1, Pallas kernels, measure(): pl.pallas_call(measure_kernel, grid=(blocks,), in_specs=[pl.BlockSpec((ro...  9.11 us
    pallas_call x2, Pallas kernels, project(): pl.pallas_call(project_kernel, grid=(steps,), in_specs=[pl.BlockSpec(memo...  8.54 us
    pallas_call x2, Pallas kernels, output(): pl.pallas_call(functools.partial(output_kernel, ks, len(units)), grid=(6,...  8.42 us
  transfers between devices with their start and end apart: 39, of which 16 were waited for; matrix products, arithmetic and copies ran while one was open for 1% of the time, Pallas kernels for 21%

profile of v4, /device:TPU:32, one launch (start us, length us, event | category | flops | bytes accessed | tf_op | source)
XLA Modules:
  0.0 168.2 jit_solution(18269255053072052678)
XLA Ops:
  2.4 5.4 %collective-permute-start = (bf16[2,128,768]{2,1,0:T(8,128)(2,1)}, bf16[2,128,768]{2,1,0:T(8,128)(2,1)S(1)}, u32[]{:S(2)}, u32[]{:S(2)}) collective-permute-start(bf16[2,128,768]{2,1,0:T(8,128)(2,1)} %pad_maximum_fusion), channel_id=1, source_target_pairs={{0,0},{1,1},{2,2},{3,3},{4,16},{5,17},{6,18},{7,19},{8,8},{9,9},{1... | collective-permute-start | bytes 1179656 | tf_op jit(solution)/shard_map/ppermute | solution.py:44
  7.8 9.1 %measure.1 = f32[8,128]{1,0:T(8,128)S(1)} custom-call(bf16[128,6144]{1,0:T(8,128)(2,1)S(1)} %copy-done, s32[1,128]{1,0:T(1,128)S(1)} %bitcast.16, bf16[1024,6144]{1,0:T(8,128)(2,1)} %t3.3, bf16[1024,6144]{1,0:T(8,128)(2,1)} %t3.3, bf16[1024,6144]{1,0:T(8,128)(2,1)} %t3.3, bf16[1024,6144]{1,0:T(8,128)(2,1)} %t3.3), custom_call_target="tpu_custom_call" | custom-call | flops 1000 | bytes 1000 | tf_op jit(solution)/shard_map/measure/pallas_call | solution.py:125
  19.1 6.4 %collective-permute-start.4 = (s32[1]{0:T(128)}, s32[1]{0:T(128)}, u32[]{:S(2)}, u32[]{:S(2)}) collective-permute-start(s32[1]{0:T(128)} %param.13), channel_id=1, source_target_pairs={{0,0},{1,20},{2,1},{3,21},{4,18},{5,6},{6,19},{7,7},{8,8},{9,28},{... | collective-permute-start | bytes 20 | tf_op jit(solution)/shard_map/ppermute | solution.py:44
  26.9 3.1 %embed.1 = (bf16[2,128,768]{2,1,0:T(8,128)(2,1)S(1)}, bf16[2,128,768]{2,1,0:T(8,128)(2,1)S(1)}) custom-call(s32[5]{0:T(128)S(1)} %stack.32.info_ref, bf16[2,128,768]{2,1,0:T(8,128)(2,1)S(1)} %collective-permute-done.patches_ref, f32[8,128]{1,0:T(8,128)S(1)} %collective-permute-done.3.stat_ref, f32[1,6144]{1,0:T(1,128)S(1)} %bitcast.15, ...), custom_call_target="tpu_custom_call" | custom-call | flops 1000 | bytes 1000 | tf_op jit(solution)/shard_map/embed/pallas_call | solution.py:158
  33.6 9.3 %collective-permute-done.5.x1 = bf16[2,128,768]{2,1,0:T(8,128)(2,1)S(1)} collective-permute-done((bf16[2,128,768]{2,1,0:T(8,128)(2,1)S(1)}, bf16[2,128,768]{2,1,0:T(8,128)(2,1)S(1)}, u32[]{:S(2)}, u32[]{:S(2)}) %collective-permute-start.5) | collective-permute-done | bytes 393248 | tf_op jit(solution)/shard_map/ppermute | solution.py:44
  43.4 2.9 %collective-permute-start.8 = (bf16[1,128,768]{2,1,0:T(8,128)(2,1)S(1)}, bf16[1,128,768]{2,1,0:T(8,128)(2,1)S(1)}, u32[]{:S(2)}, u32[]{:S(2)}) collective-permute-start(bf16[1,128,768]{2,1,0:T(8,128)(2,1)S(1)} %slice.9), channel_id=1, source_target_pairs={{0,96},{1,97},{2,98},{3,99},{4,100},{5,101},{6,102},{7,103},{8,104... | collective-permute-start | bytes 589832 | tf_op jit(solution)/shard_map/ppermute | solution.py:44
  46.3 4.2 %collective-permute-done.6.x2a = bf16[1,128,768]{2,1,0:T(8,128)(2,1)S(1)} collective-permute-done((bf16[1,128,768]{2,1,0:T(8,128)(2,1)S(1)}, bf16[1,128,768]{2,1,0:T(8,128)(2,1)S(1)}, u32[]{:S(2)}, u32[]{:S(2)}) %collective-permute-start.6) | collective-permute-done | bytes 196640 | tf_op jit(solution)/shard_map/ppermute | solution.py:44
  50.5 4.5 %project.2 = (f32[128,1536]{1,0:T(8,128)S(1)}, bf16[128,1536]{1,0:T(8,128)(2,1)S(1)}, bf16[128,1536]{1,0:T(8,128)(2,1)S(1)}, bf16[128,1536]{1,0:T(8,128)(2,1)S(1)}) custom-call(s32[5]{0:T(128)S(1)} %stack.32.info_ref, bf16[2,128,768]{2,1,0:T(8,128)(2,1)S(1)} %get-tuple-element.46.x0, bf16[2,128,768]{2,1,0:T(8,128)(2,1)S(1)} %collective-permute-done.5.x1, ...), custom_call_target="tpu_custom_call" | custom-call | flops 1000 | bytes 1000 | tf_op jit(solution)/shard_map/project/pallas_call | solution.py:212
  55.0 3.5 %collective-permute-done.12.w01 = bf16[768,768]{1,0:T(8,128)(2,1)S(1)} collective-permute-done((bf16[768,768]{1,0:T(8,128)(2,1)S(1)}, bf16[768,768]{1,0:T(8,128)(2,1)S(1)}, u32[]{:S(2)}, u32[]{:S(2)}) %collective-permute-start.12) | collective-permute-done | bytes 1179680 | tf_op jit(solution)/shard_map/ppermute | solution.py:44
  63.4 4.1 %project.3 = (f32[128,1536]{1,0:T(8,128)S(1)}, bf16[128,1536]{1,0:T(8,128)(2,1)S(1)}, bf16[128,1536]{1,0:T(8,128)(2,1)S(1)}, bf16[128,1536]{1,0:T(8,128)(2,1)S(1)}) custom-call(s32[5]{0:T(128)S(1)} %stack.32.info_ref, bf16[2,128,768]{2,1,0:T(8,128)(2,1)S(1)} %get-tuple-element.46.x0, bf16[2,128,768]{2,1,0:T(8,128)(2,1)S(1)} %collective-permute-done.5.x1, ...), custom_call_target="tpu_custom_call" | custom-call | flops 1000 | bytes 1000 | tf_op jit(solution)/shard_map/project/pallas_call | solution.py:212
  68.0 12.5 %collective-permute-done.14.p1 = bf16[128,1536]{1,0:T(8,128)(2,1)S(1)} collective-permute-done((bf16[128,1536]{1,0:T(8,128)(2,1)S(1)}, bf16[128,1536]{1,0:T(8,128)(2,1)S(1)}, u32[]{:S(2)}, u32[]{:S(2)}) %collective-permute-start.14) | collective-permute-done | bytes 393248 | tf_op jit(solution)/shard_map/ppermute | solution.py:44
  85.6 2.6 %attend.1.att_ref = bf16[128,512]{1,0:T(8,128)(2,1)S(1)} custom-call(s32[5]{0:T(128)S(1)} %stack.32.info_ref, s32[1]{0:T(128)} %collective-permute-done.4.count_ref, bf16[128,512]{1,0:T(8,128)(2,1)S(1)} %get-tuple-element.57.q_ref, bf16[2,128,512]{2,1,0:T(8,128)(2,1)S(1)} %get-tuple-element.58.near_ref, bf16[2,128,512]{2,1,0:T(8,128)(2,1)S(1)} %collective-permute-done.17.far_ref), custom_call_target="tpu_custom_call" | custom-call | flops 1000 | bytes 1000 | tf_op jit(solution)/shard_map/attend/pallas_call | solution.py:313
  88.3 8.5 %collective-permute-done.18.p1 = bf16[128,1536]{1,0:T(8,128)(2,1)S(1)} collective-permute-done((bf16[128,1536]{1,0:T(8,128)(2,1)S(1)}, bf16[128,1536]{1,0:T(8,128)(2,1)S(1)}, u32[]{:S(2)}, u32[]{:S(2)}) %collective-permute-start.18) | collective-permute-done | bytes 393248 | tf_op jit(solution)/shard_map/ppermute | solution.py:44
  102.0 11.9 %collective-permute-done.21.refs_1_ = bf16[128,2048]{1,0:T(8,128)(2,1)S(1)} collective-permute-done((bf16[128,2048]{1,0:T(8,128)(2,1)S(1)}, bf16[128,2048]{1,0:T(8,128)(2,1)S(1)}, u32[]{:S(2)}, u32[]{:S(2)}) %collective-permute-start.21) | collective-permute-done | bytes 524320 | tf_op jit(solution)/shard_map/ppermute | solution.py:44
  113.9 2.5 %collective-permute-start.32 = (bf16[128,2048]{1,0:T(8,128)(2,1)S(1)}, bf16[128,2048]{1,0:T(8,128)(2,1)S(1)}, u32[]{:S(2)}, u32[]{:S(2)}) collective-permute-start(bf16[128,2048]{1,0:T(8,128)(2,1)S(1)} %hidden.1.refs_0_), channel_id=1, source_target_pairs={{0,2},{1,3},{2,0},{3,1},{4,6},{5,7},{6,4},{7,5},{8,10},{9,11},{10,... | collective-permute-start | bytes 1572872 | tf_op jit(solution)/shard_map/ppermute | solution.py:44
  116.5 5.2 %output.2 = (bf16[64,1536]{1,0:T(8,128)(2,1)S(1)}, bf16[64,1536]{1,0:T(8,128)(2,1)S(1)}, bf16[64,1536]{1,0:T(8,128)(2,1)S(1)}, bf16[64,1536]{1,0:T(8,128)(2,1)S(...) custom-call(s32[5]{0:T(128)S(1)} %stack.32.info_ref, bf16[2,128,768]{2,1,0:T(8,128)(2,1)S(1)} %get-tuple-element.45.e_ref, ...), custom_call_target="tpu_custom_call" | custom-call | flops 1000 | bytes 1000 | tf_op jit(solution)/shard_map/output/pallas_call | solution.py:378
  121.7 3.0 %collective-permute-start.26 = (bf16[64,1536]{1,0:T(8,128)(2,1)S(1)}, bf16[64,1536]{1,0:T(8,128)(2,1)S(1)}, u32[]{:S(2)}, u32[]{:S(2)}) collective-permute-start(bf16[64,1536]{1,0:T(8,128)(2,1)S(1)} %get-tuple-element.66), channel_id=1, source_target_pairs={{0,16},{1,49},{2,82},{3,115},{4,20},{5,53},{6,86},{7,119},{8,24},{... | collective-permute-start | bytes 589832 | tf_op jit(solution)/shard_map/ppermute | solution.py:44
  125.3 3.1 %collective-permute-start.28 = (bf16[64,1536]{1,0:T(8,128)(2,1)S(1)}, bf16[64,1536]{1,0:T(8,128)(2,1)S(1)}, u32[]{:S(2)}, u32[]{:S(2)}) collective-permute-start(bf16[64,1536]{1,0:T(8,128)(2,1)S(1)} %get-tuple-element.68), channel_id=1, source_target_pairs={{0,112},{1,17},{2,50},{3,83},{4,116},{5,21},{6,54},{7,87},{8,120},... | collective-permute-start | bytes 589832 | tf_op jit(solution)/shard_map/ppermute | solution.py:44
  130.9 4.5 %collective-permute-start.30 = (bf16[64,1536]{1,0:T(8,128)(2,1)S(1)}, bf16[64,1536]{1,0:T(8,128)(2,1)S(1)}, u32[]{:S(2)}, u32[]{:S(2)}) collective-permute-start(bf16[64,1536]{1,0:T(8,128)(2,1)S(1)} %get-tuple-element.70), channel_id=1, source_target_pairs={{0,48},{1,81},{2,114},{3,19},{4,52},{5,85},{6,118},{7,23},{8,56},{... | collective-permute-start | bytes 589832 | tf_op jit(solution)/shard_map/ppermute | solution.py:44
  135.4 3.2 %output.3 = (bf16[64,1536]{1,0:T(8,128)(2,1)S(1)}, bf16[64,1536]{1,0:T(8,128)(2,1)S(1)}) custom-call(s32[5]{0:T(128)S(1)} %stack.32.info_ref, bf16[2,128,768]{2,1,0:T(8,128)(2,1)S(1)} %get-tuple-element.45.e_ref, bf16[128,2048]{1,0:T(8,128)(2,1)S(1)} %collective-permute-done.32.refs_0_, ...), custom_call_target="tpu_custom_call" | custom-call | flops 1000 | bytes 1000 | tf_op jit(solution)/shard_map/output/pallas_call | solution.py:378
  140.6 6.2 %collective-permute-start.33 = (bf16[64,1536]{1,0:T(8,128)(2,1)S(1)}, bf16[64,1536]{1,0:T(8,128)(2,1)S(1)}, u32[]{:S(2)}, u32[]{:S(2)}) collective-permute-start(bf16[64,1536]{1,0:T(8,128)(2,1)S(1)} %get-tuple-element.73), channel_id=1, source_target_pairs={{0,80},{1,113},{2,18},{3,51},{4,84},{5,117},{6,22},{7,55},{8,88},{... | collective-permute-start | bytes 589832 | tf_op jit(solution)/shard_map/ppermute | solution.py:44
  148.7 3.7 %collective-permute-done.31.refs_5_ = bf16[64,1536]{1,0:T(8,128)(2,1)S(1)} collective-permute-done((bf16[64,1536]{1,0:T(8,128)(2,1)S(1)}, bf16[64,1536]{1,0:T(8,128)(2,1)S(1)}, u32[]{:S(2)}, u32[]{:S(2)}) %collective-permute-start.31) | collective-permute-done | bytes 196640 | tf_op jit(solution)/shard_map/ppermute | solution.py:44
  157.4 3.6 %collective-permute-start.37 = (bf16[16,1536]{1,0:T(8,128)(2,1)S(1)}, bf16[16,1536]{1,0:T(8,128)(2,1)S(1)}, u32[]{:S(2)}, u32[]{:S(2)}) collective-permute-start(bf16[16,1536]{1,0:T(8,128)(2,1)S(1)} %get-tuple-element.77), channel_id=1, source_target_pairs={{0,3},{1,0},{2,1},{3,2},{4,19},{5,16},{6,17},{7,18},{8,11},{9,8},{... | collective-permute-start | bytes 147464 | tf_op jit(solution)/shard_map/ppermute | solution.py:44
  163.6 3.4 %collective-permute-done.38.refs_3_ = bf16[16,1536]{1,0:T(8,128)(2,1)S(1)} collective-permute-done((bf16[16,1536]{1,0:T(8,128)(2,1)S(1)}, bf16[16,1536]{1,0:T(8,128)(2,1)S(1)}, u32[]{:S(2)}, u32[]{:S(2)}) %collective-permute-start.38) | collective-permute-done | bytes 49184 | tf_op jit(solution)/shard_map/ppermute | solution.py:44
  (91 shorter events, 41.4 us)
Async XLA Ops:
  0.0 17.0 %collective-permute-start.1 = (bf16[3,768,256]{2,1,0:T(8,128)(2,1)}, bf16[3,768,256]{2,1,0:T(8,128)(2,1)}, u32[]{:S(2)}, u32[]{:S(2)}) collective-permute-start(bf16[3,768,256]{2,1,0:T(8,128)(2,1)} %bitcast.12), channel_id=1, source_target_pairs={{0,8},{1,9},{2,10},{3,11},{4,12},{5,13},{6,14},{7,15},{8,0},{9,1},... | collective-permute-start | bytes 3538952 | tf_op jit(solution)/shard_map/ppermute | solution.py:44
  0.0 16.9 %collective-permute-start.2 = (bf16[768,768]{1,0:T(8,128)(2,1)}, bf16[768,768]{1,0:T(8,128)(2,1)S(1)}, u32[]{:S(2)}, u32[]{:S(2)}) collective-permute-start(bf16[768,768]{1,0:T(8,128)(2,1)} %w00.1), channel_id=1, source_target_pairs={{0,8},{1,9},{2,10},{3,11},{4,12},{5,13},{6,14},{7,15},{8,0},{9,1},... | collective-permute-start | bytes 3538952 | tf_op jit(solution)/shard_map/ppermute | solution.py:44
  0.5 29.5 %collective-permute-start.9 = (bf16[3,768,256]{2,1,0:T(8,128)(2,1)}, bf16[3,768,256]{2,1,0:T(8,128)(2,1)}, u32[]{:S(2)}, u32[]{:S(2)}) collective-permute-start(bf16[3,768,256]{2,1,0:T(8,128)(2,1)} %bitcast.13), channel_id=1, source_target_pairs={{0,4},{1,5},{2,6},{3,7},{4,0},{5,1},{6,2},{7,3},{8,12},{9,13},{10,... | collective-permute-start | bytes 3538952 | tf_op jit(solution)/shard_map/ppermute | solution.py:44
  2.4 24.5 %collective-permute-start = (bf16[2,128,768]{2,1,0:T(8,128)(2,1)}, bf16[2,128,768]{2,1,0:T(8,128)(2,1)S(1)}, u32[]{:S(2)}, u32[]{:S(2)}) collective-permute-start(bf16[2,128,768]{2,1,0:T(8,128)(2,1)} %pad_maximum_fusion), channel_id=1, source_target_pairs={{0,0},{1,1},{2,2},{3,3},{4,16},{5,17},{6,18},{7,19},{8,8},{9,9},{1... | collective-permute-start | bytes 1179656 | tf_op jit(solution)/shard_map/ppermute | solution.py:44
  30.1 20.5 %collective-permute-start.11 = (bf16[3,768,256]{2,1,0:T(8,128)(2,1)}, bf16[3,768,256]{2,1,0:T(8,128)(2,1)S(1)}, u32[]{:S(2)}, u32[]{:S(2)}) collective-permute-start(bf16[3,768,256]{2,1,0:T(8,128)(2,1)} %collective-permute-done.9.w01), channel_id=1, source_target_pairs={{0,8},{1,9},{2,10},{3,11},{4,12},{5,13},{6,14},{7,15},{8,0},{9,1},... | collective-permute-start | bytes 3538952 | tf_op jit(solution)/shard_map/ppermute | solution.py:44
  30.2 28.4 %collective-permute-start.12 = (bf16[768,768]{1,0:T(8,128)(2,1)S(1)}, bf16[768,768]{1,0:T(8,128)(2,1)S(1)}, u32[]{:S(2)}, u32[]{:S(2)}) collective-permute-start(bf16[768,768]{1,0:T(8,128)(2,1)S(1)} %copy-done.2), channel_id=1, source_target_pairs={{0,4},{1,5},{2,6},{3,7},{4,0},{5,1},{6,2},{7,3},{8,12},{9,13},{10,... | collective-permute-start | bytes 3538952 | tf_op jit(solution)/shard_map/ppermute | solution.py:44
  58.6 39.6 %collective-permute-start.24 = (bf16[1024,768]{1,0:T(8,128)(2,1)S(1)}, bf16[1024,768]{1,0:T(8,128)(2,1)S(1)}, u32[]{:S(2)}, u32[]{:S(2)}) collective-permute-start(bf16[1024,768]{1,0:T(8,128)(2,1)S(1)} %constant_dynamic-update-slice_fusion.refs_3_.refs_1_), channel_id=1, source_target_pairs={{0,4},{1,5},{2,6},{3,7},{4,0},{5,1},{6,2},{7,3},{8,12},{9,13},{10,... | collective-permute-start | bytes 4718600 | tf_op jit(solution)/shard_map/ppermute | solution.py:44
  59.0 21.6 %collective-permute-start.14 = (bf16[128,1536]{1,0:T(8,128)(2,1)S(1)}, bf16[128,1536]{1,0:T(8,128)(2,1)S(1)}, u32[]{:S(2)}, u32[]{:S(2)}) collective-permute-start(bf16[128,1536]{1,0:T(8,128)(2,1)S(1)} %get-tuple-element.54), channel_id=1, source_target_pairs={{0,1},{1,2},{2,3},{3,0},{4,5},{5,6},{6,7},{7,4},{8,9},{9,10},{10,1... | collective-permute-start | bytes 1179656 | tf_op jit(solution)/shard_map/ppermute | solution.py:44
  60.7 19.8 %collective-permute-start.15 = (bf16[128,1536]{1,0:T(8,128)(2,1)S(1)}, bf16[128,1536]{1,0:T(8,128)(2,1)S(1)}, u32[]{:S(2)}, u32[]{:S(2)}) collective-permute-start(bf16[128,1536]{1,0:T(8,128)(2,1)S(1)} %get-tuple-element.55), channel_id=1, source_target_pairs={{0,2},{1,3},{2,0},{3,1},{4,6},{5,7},{6,4},{7,5},{8,10},{9,11},{10,... | collective-permute-start | bytes 1179656 | tf_op jit(solution)/shard_map/ppermute | solution.py:44
  61.9 19.6 %collective-permute-start.16 = (bf16[128,1536]{1,0:T(8,128)(2,1)S(1)}, bf16[128,1536]{1,0:T(8,128)(2,1)S(1)}, u32[]{:S(2)}, u32[]{:S(2)}) collective-permute-start(bf16[128,1536]{1,0:T(8,128)(2,1)S(1)} %get-tuple-element.56), channel_id=1, source_target_pairs={{0,3},{1,0},{2,1},{3,2},{4,7},{5,4},{6,5},{7,6},{8,11},{9,8},{10,9... | collective-permute-start | bytes 1179656 | tf_op jit(solution)/shard_map/ppermute | solution.py:44
  67.5 29.3 %collective-permute-start.18 = (bf16[128,1536]{1,0:T(8,128)(2,1)S(1)}, bf16[128,1536]{1,0:T(8,128)(2,1)S(1)}, u32[]{:S(2)}, u32[]{:S(2)}) collective-permute-start(bf16[128,1536]{1,0:T(8,128)(2,1)S(1)} %get-tuple-element.59), channel_id=1, source_target_pairs={{0,1},{1,2},{2,3},{3,0},{4,5},{5,6},{6,7},{7,4},{8,9},{9,10},{10,1... | collective-permute-start | bytes 1179656 | tf_op jit(solution)/shard_map/ppermute | solution.py:44
  80.5 16.3 %collective-permute-start.19 = (bf16[128,1536]{1,0:T(8,128)(2,1)S(1)}, bf16[128,1536]{1,0:T(8,128)(2,1)S(1)}, u32[]{:S(2)}, u32[]{:S(2)}) collective-permute-start(bf16[128,1536]{1,0:T(8,128)(2,1)S(1)} %get-tuple-element.60), channel_id=1, source_target_pairs={{0,2},{1,3},{2,0},{3,1},{4,6},{5,7},{6,4},{7,5},{8,10},{9,11},{10,... | collective-permute-start | bytes 1179656 | tf_op jit(solution)/shard_map/ppermute | solution.py:44
  80.6 16.9 %collective-permute-start.20 = (bf16[128,1536]{1,0:T(8,128)(2,1)S(1)}, bf16[128,1536]{1,0:T(8,128)(2,1)S(1)}, u32[]{:S(2)}, u32[]{:S(2)}) collective-permute-start(bf16[128,1536]{1,0:T(8,128)(2,1)S(1)} %get-tuple-element.61), channel_id=1, source_target_pairs={{0,3},{1,0},{2,1},{3,2},{4,7},{5,4},{6,5},{7,6},{8,11},{9,8},{10,9... | collective-permute-start | bytes 1179656 | tf_op jit(solution)/shard_map/ppermute | solution.py:44
  98.2 18.3 %collective-permute-start.23 = (bf16[1024,768]{1,0:T(8,128)(2,1)S(1)}, bf16[1024,768]{1,0:T(8,128)(2,1)S(1)}, u32[]{:S(2)}, u32[]{:S(2)}) collective-permute-start(bf16[1024,768]{1,0:T(8,128)(2,1)S(1)} %constant_dynamic-update-slice_fusion.refs_3_.refs_1_), channel_id=1, source_target_pairs={{0,8},{1,9},{2,10},{3,11},{4,12},{5,13},{6,14},{7,15},{8,0},{9,1},... | collective-permute-start | bytes 4718600 | tf_op jit(solution)/shard_map/ppermute | solution.py:44
  98.3 18.2 %collective-permute-start.25 = (bf16[1024,768]{1,0:T(8,128)(2,1)S(1)}, bf16[1024,768]{1,0:T(8,128)(2,1)S(1)}, u32[]{:S(2)}, u32[]{:S(2)}) collective-permute-start(bf16[1024,768]{1,0:T(8,128)(2,1)S(1)} %collective-permute-done.24.refs_5_.refs_3_), channel_id=1, source_target_pairs={{0,8},{1,9},{2,10},{3,11},{4,12},{5,13},{6,14},{7,15},{8,0},{9,1},... | collective-permute-start | bytes 4718600 | tf_op jit(solution)/shard_map/ppermute | solution.py:44
  98.8 15.1 %collective-permute-start.21 = (bf16[128,2048]{1,0:T(8,128)(2,1)S(1)}, bf16[128,2048]{1,0:T(8,128)(2,1)S(1)}, u32[]{:S(2)}, u32[]{:S(2)}) collective-permute-start(bf16[128,2048]{1,0:T(8,128)(2,1)S(1)} %hidden.1.refs_0_), channel_id=1, source_target_pairs={{0,1},{1,2},{2,3},{3,0},{4,5},{5,6},{6,7},{7,4},{8,9},{9,10},{10,1... | collective-permute-start | bytes 1572872 | tf_op jit(solution)/shard_map/ppermute | solution.py:44
  113.9 17.0 %collective-permute-start.32 = (bf16[128,2048]{1,0:T(8,128)(2,1)S(1)}, bf16[128,2048]{1,0:T(8,128)(2,1)S(1)}, u32[]{:S(2)}, u32[]{:S(2)}) collective-permute-start(bf16[128,2048]{1,0:T(8,128)(2,1)S(1)} %hidden.1.refs_0_), channel_id=1, source_target_pairs={{0,2},{1,3},{2,0},{3,1},{4,6},{5,7},{6,4},{7,5},{8,10},{9,11},{10,... | collective-permute-start | bytes 1572872 | tf_op jit(solution)/shard_map/ppermute | solution.py:44
  121.7 16.9 %collective-permute-start.26 = (bf16[64,1536]{1,0:T(8,128)(2,1)S(1)}, bf16[64,1536]{1,0:T(8,128)(2,1)S(1)}, u32[]{:S(2)}, u32[]{:S(2)}) collective-permute-start(bf16[64,1536]{1,0:T(8,128)(2,1)S(1)} %get-tuple-element.66), channel_id=1, source_target_pairs={{0,16},{1,49},{2,82},{3,115},{4,20},{5,53},{6,86},{7,119},{8,24},{... | collective-permute-start | bytes 589832 | tf_op jit(solution)/shard_map/ppermute | solution.py:44
  124.6 15.9 %collective-permute-start.27 = (bf16[64,1536]{1,0:T(8,128)(2,1)S(1)}, bf16[64,1536]{1,0:T(8,128)(2,1)S(1)}, u32[]{:S(2)}, u32[]{:S(2)}) collective-permute-start(bf16[64,1536]{1,0:T(8,128)(2,1)S(1)} %get-tuple-element.67), channel_id=1, source_target_pairs={{0,0},{1,33},{2,66},{3,99},{4,4},{5,37},{6,70},{7,103},{8,8},{9,41... | collective-permute-start | bytes 589832 | tf_op jit(solution)/shard_map/ppermute | solution.py:44
  125.3 21.4 %collective-permute-start.28 = (bf16[64,1536]{1,0:T(8,128)(2,1)S(1)}, bf16[64,1536]{1,0:T(8,128)(2,1)S(1)}, u32[]{:S(2)}, u32[]{:S(2)}) collective-permute-start(bf16[64,1536]{1,0:T(8,128)(2,1)S(1)} %get-tuple-element.68), channel_id=1, source_target_pairs={{0,112},{1,17},{2,50},{3,83},{4,116},{5,21},{6,54},{7,87},{8,120},... | collective-permute-start | bytes 589832 | tf_op jit(solution)/shard_map/ppermute | solution.py:44
  128.4 20.2 %collective-permute-start.29 = (bf16[64,1536]{1,0:T(8,128)(2,1)S(1)}, bf16[64,1536]{1,0:T(8,128)(2,1)S(1)}, u32[]{:S(2)}, u32[]{:S(2)}) collective-permute-start(bf16[64,1536]{1,0:T(8,128)(2,1)S(1)} %get-tuple-element.69), channel_id=1, source_target_pairs={{0,96},{1,1},{2,34},{3,67},{4,100},{5,5},{6,38},{7,71},{8,104},{9,... | collective-permute-start | bytes 589832 | tf_op jit(solution)/shard_map/ppermute | solution.py:44
  130.9 17.7 %collective-permute-start.30 = (bf16[64,1536]{1,0:T(8,128)(2,1)S(1)}, bf16[64,1536]{1,0:T(8,128)(2,1)S(1)}, u32[]{:S(2)}, u32[]{:S(2)}) collective-permute-start(bf16[64,1536]{1,0:T(8,128)(2,1)S(1)} %get-tuple-element.70), channel_id=1, source_target_pairs={{0,48},{1,81},{2,114},{3,19},{4,52},{5,85},{6,118},{7,23},{8,56},{... | collective-permute-start | bytes 589832 | tf_op jit(solution)/shard_map/ppermute | solution.py:44
  138.6 13.8 %collective-permute-start.31 = (bf16[64,1536]{1,0:T(8,128)(2,1)S(1)}, bf16[64,1536]{1,0:T(8,128)(2,1)S(1)}, u32[]{:S(2)}, u32[]{:S(2)}) collective-permute-start(bf16[64,1536]{1,0:T(8,128)(2,1)S(1)} %get-tuple-element.71), channel_id=1, source_target_pairs={{0,32},{1,65},{2,98},{3,3},{4,36},{5,69},{6,102},{7,7},{8,40},{9,7... | collective-permute-start | bytes 589832 | tf_op jit(solution)/shard_map/ppermute | solution.py:44
  140.6 13.9 %collective-permute-start.33 = (bf16[64,1536]{1,0:T(8,128)(2,1)S(1)}, bf16[64,1536]{1,0:T(8,128)(2,1)S(1)}, u32[]{:S(2)}, u32[]{:S(2)}) collective-permute-start(bf16[64,1536]{1,0:T(8,128)(2,1)S(1)} %get-tuple-element.73), channel_id=1, source_target_pairs={{0,80},{1,113},{2,18},{3,51},{4,84},{5,117},{6,22},{7,55},{8,88},{... | collective-permute-start | bytes 589832 | tf_op jit(solution)/shard_map/ppermute | solution.py:44
  (24 other events, 243.2 us)
